TPU v7x, 32 devices: a whole 2x2x4 slice. The times are simulated.
32 devices in a mesh: lat: 4 (over y, x), lon: 8 (over z, core).
Axes of the slice: x: 2, y: 2, z: 4, core: 2. Of those that a mesh axis runs over, the one named last changes fastest.
Arguments:
- tide_state: float32 [48, 512, 1024], P(None, 'lat', 'lon'), may hold values from -6 to 6
- potential: float32 [48, 512, 1024], P(None, 'lat', 'lon'), may hold values from -6 to 6
- water_depth: float32 [512, 1024], P('lat', 'lon'), may hold values from 0.1 to 1
- drag_coeff: float32 [512, 1024], P('lat', 'lon'), may hold values from 0.1 to 2
- ocean_mask: int32 [512, 1024], P('lat', 'lon'), may hold values 0 or 1
- residual_rows: float32 [16, 1048576], P(None, ('lat', 'lon')), may hold values from -6 to 6
- dest_tile: int32 [1048576, 1], P(('lat', 'lon')), may hold values from 0 to 7; in each aligned block of 32768 rows (0 to 32767, 32768 to 65535, ...) at most 8192 rows name the same one
- dest_cell: int32 [1048576], P(('lat', 'lon')), may hold values from 0 to 16383
Outputs:
- tide_field: float32 [48, 512, 1024], P(None, 'lat', 'lon')
Inputs may be any that keep to these rules, and one draw needn't show every extreme that they name: `dest_tile`: the rows of one device name each longitude tile at most 8192 times, a bound that some block reaches.
All inputs are finite; a program needn't handle non-finite values. No bound on the sum of `ocean_mask` on one device may be relied on, other than what follows from the above.
Results may differ from a plain program's by a relative error of at most 0.00002.
Values sent between devices are 32-bit elements; how exact they have to be, the bound alone decides.
No kernel may reach another device: no remote copies, remote signals or barrier semaphores. Data moves between devices by JAX's collectives and lax.ppermute only.
A program may use at most 192 MiB of HBM per device.

v0:
```python
import jax
import jax.numpy as jnp
from jax import lax
from jax.sharding import PartitionSpec as P

SWEEPS = 3


OMEGAS = [1.405, 1.454, 1.379, 1.458, 0.729, 0.676, 0.725, 0.649]
RELAX_WEIGHT = 0.8


def with_halo(cells, sides, width, closed):
    for axis, dim in sides:
        count = lax.axis_size(axis)
        ends = count if closed else count - 1
        head = lax.slice_in_dim(cells, 0, width, axis=dim)
        tail = lax.slice_in_dim(cells, cells.shape[dim] - width, cells.shape[dim], axis=dim)
        cells = jnp.concatenate(
            [
                lax.ppermute(tail, axis, [(i, (i + 1) % count) for i in range(ends)]),
                cells,
                lax.ppermute(head, axis, [((i + 1) % count, i) for i in range(ends)]),
            ],
            axis=dim,
        )
    return cells


def divide(real_part, imag_part, diag, omega):
    denom = diag * diag + omega * omega
    return (
        (real_part * diag + imag_part * omega) / denom,
        (imag_part * diag - real_part * omega) / denom,
    )


def update(
    center,
    potential,
    forcing,
    flux_lon,
    flux_lat,
    grad_lon,
    grad_lat,
    drag_coeff,
    coriolis,
    ocean,
    omega,
):
    eta_re, eta_im, east_re, east_im, north_re, north_im = center
    diag_vel = 1.0 + drag_coeff
    res_eta_re = potential[0] - (eta_re - omega * eta_im + (flux_lon[0] + flux_lat[0])) + forcing[0]
    res_eta_im = potential[1] - (eta_im + omega * eta_re + (flux_lon[1] + flux_lat[1])) + forcing[1]
    res_east_re = potential[2] - (
        diag_vel * east_re - omega * east_im - coriolis * north_re + grad_lon[0]
    )
    res_east_im = potential[3] - (
        diag_vel * east_im + omega * east_re - coriolis * north_im + grad_lon[1]
    )
    res_north_re = potential[4] - (
        diag_vel * north_re - omega * north_im + coriolis * east_re + grad_lat[0]
    )
    res_north_im = potential[5] - (
        diag_vel * north_im + omega * north_re + coriolis * east_im + grad_lat[1]
    )
    step_eta = divide(res_eta_re, res_eta_im, 1.0, omega)
    step_east = divide(res_east_re, res_east_im, diag_vel, omega)
    step_north = divide(res_north_re, res_north_im, diag_vel, omega)
    steps_all = (step_eta[0], step_eta[1], step_east[0], step_east[1], step_north[0], step_north[1])
    return tuple((ocean * (center[index] + RELAX_WEIGHT * steps_all[index]) for index in range(6)))


def crop_to(array, have, want):
    cut = have - want
    return array


def diff_lon(field):
    return (field[..., 1:-1, 2:] - field[..., 1:-1, :-2]) * 0.5


def diff_lat(field):
    return (field[..., 2:, 1:-1] - field[..., :-2, 1:-1]) * 0.5


def sweep(fields, margin, depth_full, depth_margin, statics, static_margin, lat_start, grid_rows):
    consts = fields.shape[1]
    depth_pad = crop_to(depth_full, depth_margin, margin)
    inner = crop_to(statics, static_margin, margin - 1)
    drag_coeff = inner[0]
    ocean = inner[1]
    pot = inner[2 : 2 + 6 * consts].reshape((6, consts) + inner.shape[1:])
    force = inner[2 + 6 * consts :].reshape((2, consts) + inner.shape[1:])
    row_ids = lat_start - (margin - 1) + jnp.arange(inner.shape[1], dtype=jnp.int32)
    lat_pos = (row_ids.astype(jnp.float32) + 0.5) / grid_rows - 0.5
    coriolis = (0.5 * jnp.sin(jnp.pi * lat_pos))[:, None]
    omega = jnp.asarray(OMEGAS, jnp.float32)[:, None, None]
    flux_lon = (diff_lon(depth_pad * fields[2]), diff_lon(depth_pad * fields[3]))
    flux_lat = (diff_lat(depth_pad * fields[4]), diff_lat(depth_pad * fields[5]))
    grad_lon = (diff_lon(fields[0]), diff_lon(fields[1]))
    grad_lat = (diff_lat(fields[0]), diff_lat(fields[1]))
    center = tuple((fields[index, :, 1:-1, 1:-1] for index in range(6)))
    result = update(
        center,
        pot,
        force,
        flux_lon,
        flux_lat,
        grad_lon,
        grad_lat,
        drag_coeff,
        coriolis,
        ocean,
        omega,
    )
    return jnp.stack(result)


def local(
    tide_state, potential, water_depth, drag_coeff, ocean_mask, residual_rows, dest_tile, dest_cell
):
    tiles = lax.axis_size("lon")
    row_count = residual_rows.shape[1]
    row_width = residual_rows.shape[0]
    capacity = 2 * row_count // tiles
    tile_rows, tile_cols = water_depth.shape
    cell_count = tile_rows * tile_cols
    target = dest_tile[:, 0]
    tile_ids = jnp.arange(tiles, dtype=jnp.int32)
    onehot_tile = (target[:, None] == tile_ids[None, :]).astype(jnp.int32)
    counts = jnp.sum(onehot_tile, axis=0)
    starts = jnp.cumsum(counts) - counts
    columns = tuple((residual_rows[index] for index in range(row_width)))
    sorted_all = lax.sort((target, dest_cell) + columns, dimension=0, is_stable=True, num_keys=1)
    sorted_tile = sorted_all[0]
    sorted_cell = sorted_all[1]
    sorted_rows = jnp.stack(sorted_all[2:], axis=1)
    start_of = jnp.sum(
        (sorted_tile[:, None] == tile_ids[None, :]).astype(jnp.int32) * starts[None, :], axis=1
    )
    slot = sorted_tile * capacity + (jnp.arange(row_count, dtype=jnp.int32) - start_of)
    out_rows = jnp.zeros((tiles * capacity, row_width), jnp.float32).at[slot].set(sorted_rows)
    out_cells = jnp.full((tiles * capacity,), cell_count, jnp.int32).at[slot].set(sorted_cell)
    outgoing = out_rows.reshape(tiles, capacity * row_width)
    places = out_cells.reshape(tiles, capacity)
    incoming, arrived = (
        lax.all_to_all(outgoing, "lon", split_axis=0, concat_axis=0, tiled=True),
        lax.all_to_all(places, "lon", split_axis=0, concat_axis=0, tiled=True),
    )
    values = incoming.reshape(tiles * capacity, row_width)
    summed = jax.ops.segment_sum(values, arrived.reshape(-1), num_segments=cell_count + 1)
    forcing = summed[:cell_count].T.reshape(row_width, tile_rows, tile_cols)
    fields_total = tide_state.shape[0]
    consts = fields_total // 6
    statics = jnp.concatenate(
        [drag_coeff[None], ocean_mask.astype(jnp.float32)[None], potential, forcing], axis=0
    )
    lat_start = lax.axis_index("lat") * tile_rows
    grid_rows = tile_rows * lax.axis_size("lat")
    current = tide_state.reshape(6, consts, tile_rows, tile_cols)
    depth_full = with_halo(water_depth, (("lat", 0),), 1, False)
    depth_full = with_halo(depth_full, (("lon", 1),), 1, True)
    for sweep_index in range(SWEEPS):
        flat = current.reshape(fields_total, tile_rows, tile_cols)
        padded = with_halo(flat, (("lat", 1),), 1, False)
        padded = with_halo(padded, (("lon", 2),), 1, True)
        padded = padded.reshape((6, consts) + padded.shape[1:])
        current = sweep(padded, 1, depth_full, 1, statics, 0, lat_start, grid_rows)
    return current.reshape(fields_total, tile_rows, tile_cols)


def solution(mesh):
    placed = (
        P(None, "lat", "lon"),
        P(None, "lat", "lon"),
        P("lat", "lon"),
        P("lat", "lon"),
        P("lat", "lon"),
        P(None, ("lat", "lon")),
        P(("lat", "lon"), None),
        P(("lat", "lon")),
    )
    return jax.shard_map(
        local, mesh=mesh, in_specs=placed, out_specs=P(None, "lat", "lon"), check_vma=False
    )
```

profile of v0, /device:TPU:0, one launch (start us, length us, event | category | flops | bytes accessed | tf_op | source)
XLA Modules:
  0.0 1038.7 jit_solution(9264821029055082582)
XLA Ops:
  0.0 8.7 fusion.174
  9.1 86.1 %sort.151 = (s32[32768]{0:T(1024)S(1)}, s32[32768]{0:T(1024)}, f32[32768]{0:T(1024)S(1)}, f32[32768]{0:T(1024)S(1)}, f32[32768]{0:T(1024)S(1)}, /*index=5*/f32[3...) sort(s32[32768]{0:T(1024)S(1)} %bitcast.385, ...), dimensions={0}, to_apply=%region_0.0 | sort | flops 491520 | bytes 4980736 | tf_op jit(solution)/shard_map/sort | solution.py:135
  95.2 5.6 stack.130
  100.8 8.7 copy.198
  110.3 93.6 %scatter_custom_fusion.1 = f32[65536,16]{1,0:T(8,128)} fusion(s32[32768]{0:T(1024)S(1)} %compare_select_fusion, f32[32768,16]{1,0:T(8,128)} %copy.198, f32[]{:T(128)} %constant.15.clone.1), kind=kCustom, calls=%fused_computation.3 | custom fusion | bytes 4194816 | tf_op jit(solution)/shard_map/scatter | solution.py:143
  203.9 18.3 %all_to_all.16 = f32[8,1,131072]{2,1,0:T(1,128)} reshape(f32[65536,16]{1,0:T(8,128)} %scatter_custom_fusion.1) | data formatting | bytes 8388608 | tf_op jit(solution)/shard_map/all_to_all | solution.py:148
  222.2 6.6 all-to-all-start.1
  230.4 4.0 collective-permute-start
  235.7 4.5 collective-permute-start.4
  244.0 120.8 %scatter_custom_fusion = s32[65536]{0:T(1024)} fusion(s32[32768]{0:T(1024)} %copy-done.38, s32[32768]{0:T(1024)} %get-tuple-element.42, s32[]{:T(128)} %constant.16.clone.1), kind=kCustom, calls=%fused_computation.239 | custom fusion | bytes 262656 | tf_op jit(solution)/shard_map/scatter | solution.py:144
  401.0 8.1 pad_maximum_fusion
  409.2 4.0 all-to-all-start
  413.2 8.3 fusion.179
  423.8 13.6 %reduce = f32[8,131072]{1,0:T(8,128)} reduce(f32[8,1,131072]{2,1,0:T(1,128)} %all-to-all-done.1, f32[]{:T(128)} %constant.49), dimensions={1}, to_apply=%all_to_all.15.reduce_sub_computation | reduce | bytes 8388612 | tf_op jit(solution)/shard_map/all_to_all | solution.py:148
  437.3 24.3 %reshape.175 = f32[65536,16]{1,0:T(8,128)} reshape(f32[8,131072]{1,0:T(8,128)} %reduce) | data formatting | bytes 8388608 | tf_op jit(solution)/shard_map/reshape | solution.py:151
  461.6 399.1 %scatter_custom_fusion.2 = f32[16385,16]{1,0:T(8,128)} fusion(s32[65536]{0:T(1024)} %bitcast.23, f32[65536,16]{1,0:T(8,128)} %reshape.175, f32[]{:T(128)} %constant.15.clone.1), kind=kCustom, calls=%fused_computation.9 | custom fusion | flops 1048576 | bytes 1049152 | tf_op jit(solution)/shard_map/scatter-add | solution.py:152
  864.5 7.1 fusion.166
  871.6 5.9 copy.200
  877.5 5.9 copy.202
  883.4 6.0 bitcast_dynamic-update-slice_fusion.5
  891.0 4.0 fusion.8
  896.5 4.0 fusion.18
  907.4 5.1 collective-permute-done.9
  920.0 29.9 %collective-permute-start.10 = (f32[48,130,1]{1,0,2:T(8,128)}, f32[48,130,1]{1,0,2:T(8,128)}, u32[]{:S(2)}, u32[]{:S(2)}) collective-permute-start(f32[48,130,1]{1,0,2:T(8,128)} %copy.218), channel_id=1, source_target_pairs={{0,1},{1,2},{2,3},{3,4},{4,5},{5,6},{6,7},{7,0},{8,9},{9,10},{10,1... | collective-permute-start | bytes 74888 | tf_op jit(solution)/shard_map/ppermute | solution.py:21
  950.0 3.9 copy.219
  957.7 4.2 copy.221
  962.0 5.5 pad_maximum_fusion.1
  972.6 4.2 bitcast_dynamic-update-slice_fusion.3
  982.8 4.9 collective-permute-start.12
  1001.0 3.9 copy.239
  1016.2 5.5 pad_maximum_fusion.2
  1026.8 4.2 bitcast_dynamic-update-slice_fusion.1
  (193 shorter events, 118.9 us)
Async XLA Ops:
  0.0 8.7 copy-start.31
  0.0 9.1 copy-start.37
  110.2 93.6 %copy-start.38 = (s32[32768]{0:T(1024)}, s32[32768]{0:T(1024)S(1)}, u32[]{:S(2)}) copy-start(s32[32768]{0:T(1024)S(1)} %compare_select_fusion) | copy-start | bytes 393220
  222.2 13.5 %copy-start.35 = (f32[128,128]{1,0:T(8,128)S(1)}, f32[128,128]{1,0:T(8,128)}, u32[]{:S(2)}) copy-start(f32[128,128]{1,0:T(8,128)} %param.13) | copy-start | bytes 196612
  222.2 19.4 %copy-start.41 = (f32[128,128]{1,0:T(8,128)S(1)}, f32[128,128]{1,0:T(8,128)}, u32[]{:S(2)}) copy-start(f32[128,128]{1,0:T(8,128)} %param.14) | copy-start | bytes 196612
  222.2 19.4 %copy-start.30 = (f32[48,128,128]{2,1,0:T(8,128)S(1)}, f32[48,128,128]{2,1,0:T(8,128)}, u32[]{:S(2)}) copy-start(f32[48,128,128]{2,1,0:T(8,128)} %param.12) | copy-start | bytes 9437188
  222.2 187.0 %all-to-all-start.1 = ((f32[8,1,131072]{2,1,0:T(1,128)}), f32[8,1,131072]{2,1,0:T(1,128)}, u32[]{:S(2)}, u32[]{:S(2)}) async-start(f32[8,1,131072]{2,1,0:T(1,128)} %all_to_all.16), calls=%async_computation.1 | async-start | bytes 8388608 | tf_op jit(solution)/shard_map/all_to_all | solution.py:148
  230.4 138.7 %collective-permute-start = (f32[48,1,128]{2,0,1:T(8,128)}, f32[48,1,128]{2,0,1:T(8,128)}, u32[]{:S(2)}, u32[]{:S(2)}) collective-permute-start(f32[48,1,128]{2,0,1:T(8,128)} %copy.305), channel_id=1, source_target_pairs={{0,8},{8,16},{16,24},{1,9},{9,17},{17,25},{2,10},{10,18},{18,26},{... | collective-permute-start | bytes 73736 | tf_op jit(solution)/shard_map/ppermute | solution.py:21
  234.4 139.3 %collective-permute-start.1 = (f32[48,1,128]{2,0,1:T(8,128)S(1)}, f32[48,1,128]{2,0,1:T(8,128)}, u32[]{:S(2)}, u32[]{:S(2)}) collective-permute-start(f32[48,1,128]{2,0,1:T(8,128)S(1)} %copy.306), channel_id=1, source_target_pairs={{8,0},{16,8},{24,16},{9,1},{17,9},{25,17},{10,2},{18,10},{26,18},{... | collective-permute-start | bytes 73736 | tf_op jit(solution)/shard_map/ppermute | solution.py:23
  235.7 129.1 %collective-permute-start.4 = (f32[1,128]{1,0:T(1,128)S(1)}, f32[1,128]{1,0:T(1,128)S(1)}, u32[]{:S(2)}, u32[]{:S(2)}) collective-permute-start(f32[1,128]{1,0:T(1,128)S(1)} %get-tuple-element.147), channel_id=1, source_target_pairs={{0,8},{8,16},{16,24},{1,9},{9,17},{17,25},{2,10},{10,18},{18,26},{... | collective-permute-start | bytes 1544 | tf_op jit(solution)/shard_map/ppermute | solution.py:21
  240.3 124.5 %collective-permute-start.5 = (f32[1,128]{1,0:T(1,128)S(1)}, f32[1,128]{1,0:T(1,128)S(1)}, u32[]{:S(2)}, u32[]{:S(2)}) collective-permute-start(f32[1,128]{1,0:T(1,128)S(1)} %get-tuple-element.148), channel_id=1, source_target_pairs={{8,0},{16,8},{24,16},{9,1},{17,9},{25,17},{10,2},{18,10},{26,18},{... | collective-permute-start | bytes 1544 | tf_op jit(solution)/shard_map/ppermute | solution.py:23
  365.5 26.1 %collective-permute-start.6 = (f32[130,1]{1,0:T(8,128)}, f32[130,1]{1,0:T(8,128)S(1)}, u32[]{:S(2)}, u32[]{:S(2)}) collective-permute-start(f32[130,1]{1,0:T(8,128)} %get-tuple-element.143), channel_id=1, source_target_pairs={{0,1},{1,2},{2,3},{3,4},{4,5},{5,6},{6,7},{7,0},{8,9},{9,10},{10,1... | collective-permute-start | bytes 1568 | tf_op jit(solution)/shard_map/ppermute | solution.py:21
  365.5 26.7 %collective-permute-start.7 = (f32[130,1]{1,0:T(8,128)S(1)}, f32[130,1]{1,0:T(8,128)}, u32[]{:S(2)}, u32[]{:S(2)}) collective-permute-start(f32[130,1]{1,0:T(8,128)S(1)} %get-tuple-element.144), channel_id=1, source_target_pairs={{1,0},{2,1},{3,2},{4,3},{5,4},{6,5},{7,6},{0,7},{9,8},{10,9},{11,1... | collective-permute-start | bytes 1568 | tf_op jit(solution)/shard_map/ppermute | solution.py:23
  380.0 12.3 %copy-start.46 = (f32[1,128]{1,0:T(1,128)S(1)}, f32[1,128]{1,0:T(1,128)}, u32[]{:S(2)}) copy-start(f32[1,128]{1,0:T(1,128)} %copy-done.45) | copy-start | bytes 1540
  380.0 12.3 %copy-start.48 = (f32[1,128]{1,0:T(1,128)S(1)}, f32[1,128]{1,0:T(1,128)}, u32[]{:S(2)}) copy-start(f32[1,128]{1,0:T(1,128)} %copy-done.47) | copy-start | bytes 1540
  384.0 9.4 collective-permute-start.2
  387.9 9.3 collective-permute-start.3
  409.2 52.5 %all-to-all-start = ((s32[8,1,8192]{2,1,0:T(1,128)}), s32[8,1,8192]{2,1,0:T(1,128)}, u32[]{:S(2)}, u32[]{:S(2)}) async-start(s32[8,1,8192]{2,1,0:T(1,128)} %bitcast.367), calls=%async_computation | async-start | bytes 524288 | tf_op jit(solution)/shard_map/all_to_all | solution.py:149
  413.2 8.3 copy-start.6
  883.4 7.5 copy-start.1
  883.4 7.5 copy-start.13
  883.4 7.5 copy-start.16
  883.4 7.5 copy-start.39
  902.6 2.8 collective-permute-start.8
  903.9 8.6 collective-permute-start.9
  907.4 8.7 copy-start.32
  920.0 33.9 %collective-permute-start.10 = (f32[48,130,1]{1,0,2:T(8,128)}, f32[48,130,1]{1,0,2:T(8,128)}, u32[]{:S(2)}, u32[]{:S(2)}) collective-permute-start(f32[48,130,1]{1,0,2:T(8,128)} %copy.218), channel_id=1, source_target_pairs={{0,1},{1,2},{2,3},{3,4},{4,5},{5,6},{6,7},{7,0},{8,9},{9,10},{10,1... | collective-permute-start | bytes 74888 | tf_op jit(solution)/shard_map/ppermute | solution.py:21
  953.9 3.8 collective-permute-start.11
  982.8 6.4 collective-permute-start.12
  987.7 5.7 collective-permute-start.13
  1001.0 7.5 collective-permute-start.14
  1005.0 7.4 collective-permute-start.15
  (35 other events, 131.8 us)
where the time goes:
time: 1050 us; the launch traced here: 1040 us
  other arithmetic  577 us (55%)
  local copies, waits for them, and re-layouts  381 us (36%)
  starting transfers between devices  71.5 us (7%)
    scatter-add x1, other arithmetic, local(): jax.ops.segment_sum(values, arrived.reshape(-1), num_segments=cell_count...  399 us
    scatter x1, local copies, waits for them, and re-layouts, local(): jnp.full((tiles * capacity,), cell_count, jnp.int32).at[slot]  121 us
    scatter x1, local copies, waits for them, and re-layouts, local(): jnp.zeros((tiles * capacity, row_width), jnp.float32).at[slot]  93.6 us
    sort x1, other arithmetic, local(): lax.sort((target, dest_cell) + columns, dimension=0, is_stable=True, num_...  86.1 us
    ppermute x8, starting transfers between devices, with_halo(): lax.ppermute(tail, axis, [(i, (i + 1) % count) for i in range(ends)])  44.7 us
    unnamed x15, other arithmetic  35.2 us
    reshape x1, local copies, waits for them, and re-layouts, local(): values = incoming.reshape(tiles * capacity, row_width)  24.3 us
    slice x8, local copies, waits for them, and re-layouts, with_halo(): lax.slice_in_dim(cells, cells.shape[dim] - width, cells.shape[dim], axis=...  23.4 us
  transfers between devices with their start and end apart: 18, of which 3 were waited for; matrix products, arithmetic and copies ran while one was open for 22% of the time, Pallas kernels for 0%

commit v1 on v0

v1 whole, which is shorter than its diff:
```python
import functools

import jax
import jax.numpy as jnp
from jax import lax
from jax.experimental import pallas as pl
from jax.experimental.pallas import tpu as pltpu
from jax.sharding import PartitionSpec as P

OMEGAS = [1.405, 1.454, 1.379, 1.458, 0.729, 0.676, 0.725, 0.649]
RELAX = 0.8
LANES = 128
BLOCK = 256
HEAD = 8
MIB = 1 << 20
NT = (((1,), (1,)), ((), ()))
NN = (((1,), (0,)), ((), ()))
VMEM = pl.BlockSpec(memory_space=pltpu.VMEM)
SMEM = pl.BlockSpec(memory_space=pltpu.SMEM)


def iota(shape, dim):
    return lax.broadcasted_iota(jnp.int32, shape, dim)


def params(mib):
    return pltpu.CompilerParams(vmem_limit_bytes=mib * MIB)


def cost(flops, nbytes):
    return pl.CostEstimate(flops=flops, bytes_accessed=nbytes, transcendentals=0)


def rank_kernel(tiles, dest_ref, slot_ref, count_ref, base_ref, place_ref, total_ref):
    blocks, block = dest_ref.shape
    dest = dest_ref[...]
    upper = (iota((block, block), 0) < iota((block, block), 1)).astype(jnp.bfloat16)
    lane = iota((blocks, LANES), 1)
    slot = jnp.zeros((blocks, block), jnp.float32)
    base = jnp.zeros((blocks, 1), jnp.float32)
    counts = jnp.zeros((blocks, LANES), jnp.float32)
    bases = jnp.zeros((blocks, LANES), jnp.float32)
    for tile in range(tiles):
        mine = dest == tile
        ones = jnp.where(mine, 1.0, 0.0)
        before = lax.dot_general(
            ones.astype(jnp.bfloat16), upper, NN, preferred_element_type=jnp.float32
        )
        slot = slot + jnp.where(mine, before + base, 0.0)
        count = jnp.sum(ones, axis=1, keepdims=True)
        counts = counts + jnp.where(lane == tile, count, 0.0)
        bases = bases + jnp.where(lane == tile, base, 0.0)
        base = base + count
    lower = (iota((blocks, blocks), 1) < iota((blocks, blocks), 0)).astype(jnp.bfloat16)
    places = lax.dot_general(
        lower, counts.astype(jnp.bfloat16), NN, preferred_element_type=jnp.float32
    )
    slot_ref[...] = slot.astype(jnp.int32)
    count_ref[...] = counts.astype(jnp.int32)
    base_ref[...] = bases.astype(jnp.int32)
    place_ref[...] = places.astype(jnp.int32)
    total = jnp.sum(counts, axis=0, keepdims=True).astype(jnp.int32)
    total_ref[...] = jnp.broadcast_to(total, total_ref.shape)


def bucket_kernel(
    tiles, capacity, width, group, me_ref, count_ref, base_ref, place_ref, total_ref, *refs
):
    slot_ref, cell_ref, rows_ref = refs[:3]
    outs = refs[3 : 3 + tiles]
    staged, held = refs[3 + tiles :]
    blocks = slot_ref.shape[0]
    windows = capacity // LANES
    room = capacity + BLOCK
    chunk = max(8, 512 // tiles)
    row_of = iota((BLOCK, BLOCK), 0)
    third = iota((16, BLOCK), 0)
    pad = jnp.zeros((LANES - 2 * width - 16, BLOCK), jnp.bfloat16)

    def permute(at, first):
        block = first + at
        slot = slot_ref[pl.ds(block, 1), :]
        cell = cell_ref[pl.ds(block, 1), :]
        rows = rows_ref[:, pl.ds(pl.multiple_of(block * BLOCK, BLOCK), BLOCK)]
        high = rows.astype(jnp.bfloat16)
        low = (rows - high.astype(jnp.float32)).astype(jnp.bfloat16)
        cells = jnp.where(
            third == 0, cell >> 7, jnp.where(third == 1, cell & 127, 0)
        ).astype(jnp.float32)
        payload = jnp.concatenate([high, low, cells.astype(jnp.bfloat16), pad], axis=0)
        onehot = jnp.where(row_of == slot, 1.0, 0.0).astype(jnp.bfloat16)
        staged[pl.ds(pl.multiple_of(at * BLOCK, BLOCK), BLOCK), :] = lax.dot_general(
            onehot, payload, NT, preferred_element_type=jnp.float32
        )
        return first

    def spread(at, first):
        block = first + at
        for tile in range(tiles):
            count = count_ref[block, tile]
            source = at * BLOCK + base_ref[block, tile]
            place = tile * room + place_ref[block, tile]
            held[pl.ds(place, chunk), :] = staged[pl.ds(source, chunk), :]

            @pl.when(count > chunk)
            def _more():
                def step(part, carry):
                    held[pl.ds(place + part * chunk, chunk), :] = staged[
                        pl.ds(source + part * chunk, chunk), :
                    ]
                    return carry

                lax.fori_loop(1, pl.cdiv(count, chunk), step, 0)

        return first

    for part in range(blocks // group):
        lax.fori_loop(0, group, permute, part * group, unroll=2)
        lax.fori_loop(0, group, spread, part * group)

    row, lane = iota((32, LANES), 0), iota((32, LANES), 1)
    joined = jnp.where((row < width) & ((lane == row) | (lane == row + width)), 1.0, 0.0)
    joined = joined + jnp.where((row == width) & (lane == 2 * width), 128.0, 0.0)
    joined = joined + jnp.where((row == width) & (lane == 2 * width + 1), 1.0, 0.0)
    joined = joined.astype(jnp.bfloat16)
    lanes = iota((1, BLOCK), 1)
    me = me_ref[0]
    for step in range(tiles):
        tile = me ^ step
        count = total_ref[0, tile]
        out = outs[step]

        def turn(part, carry, tile=tile, count=count, out=out):
            block = held[pl.ds(pl.multiple_of(tile * room + part * BLOCK, 8), BLOCK), :]
            both = lax.dot_general(
                joined, block.astype(jnp.bfloat16), NT, preferred_element_type=jnp.float32
            )
            cells = jnp.where(lanes + part * BLOCK < count, both[width : width + 1], -1.0)
            for side in range(BLOCK // LANES):
                at = part * (BLOCK // LANES) + side
                cut = slice(side * LANES, (side + 1) * LANES)
                out[pl.ds(pl.multiple_of(at * width, width), width), :] = both[:width, cut]
                out[pl.ds(windows * width + at, 1), :] = cells[:, cut]
            return carry

        lax.fori_loop(0, pl.cdiv(count, BLOCK), turn, 0)
        out[windows * (width + 1) :, :] = jnp.full((HEAD, LANES), count, jnp.int32).astype(
            jnp.float32
        )


def sum_kernel(width, windows, amount, fresh, *refs):
    buckets = refs[:amount]
    out = refs[-1]
    half, wide = out.shape[1:]
    chunk = 2 * LANES
    if fresh:
        out[...] = jnp.zeros_like(out)
    else:
        out[...] = refs[amount][...]
    row_of = iota((half, chunk), 0)
    col_of = iota((wide, chunk), 0)
    for bucket in buckets:
        count = jnp.max(bucket[windows * (width + 1) :, :]).astype(jnp.int32)

        def step(part, carry, bucket=bucket):
            vals, cells = [], []
            for side in range(chunk // LANES):
                at = part * (chunk // LANES) + side
                vals.append(bucket[pl.ds(pl.multiple_of(at * width, width), width), :])
                cells.append(bucket[pl.ds(windows * width + at, 1), :])
            rows = jnp.concatenate(vals, axis=1)
            cell = jnp.concatenate(cells, axis=1).astype(jnp.int32)
            grid_row = cell >> 7
            low_row = jnp.where(cell < 0, -1, grid_row & (half - 1))
            column = (cell & 127) + jnp.where(grid_row >= half, LANES, 0)
            high = rows.astype(jnp.bfloat16)
            low = (rows - high.astype(jnp.float32)).astype(jnp.bfloat16)
            mine = row_of == low_row
            onehot = jnp.where(col_of == column, 1.0, 0.0).astype(jnp.bfloat16)
            left = []
            for channel in range(width):
                left.append(
                    jnp.concatenate(
                        [
                            jnp.where(mine, high[channel : channel + 1].astype(jnp.float32), 0.0),
                            jnp.where(mine, low[channel : channel + 1].astype(jnp.float32), 0.0),
                        ],
                        axis=1,
                    ).astype(jnp.bfloat16)
                )
            product = lax.dot_general(
                jnp.concatenate(left, axis=0),
                jnp.concatenate([onehot, onehot], axis=1),
                NT,
                preferred_element_type=jnp.float32,
            )
            out[...] += product.reshape(out.shape)
            return carry

        lax.fori_loop(0, pl.cdiv(count, chunk), step, 0)


def put_edges(strips, k, rows, r0, last_row, fields):
    north, south, west, east = strips
    eta_re, eta_im, east_re, east_im, north_re, north_im = fields
    lane = iota((rows, LANES), 1)
    part = pl.ds(r0, rows)
    for group, field in enumerate((eta_re, eta_im, east_re, east_im)):
        at = group * 8 + k
        west[part, :] = jnp.where(lane == at, pltpu.roll(field, at, 1), west[part, :])
        east[part, :] = jnp.where(lane == at, pltpu.roll(field, at + 1, 1), east[part, :])
    for group, field in enumerate((eta_re, eta_im, north_re, north_im)):
        at = group * 8 + k
        if r0 == 0:
            north[pl.ds(at, 1), :] = field[0:1]
        if r0 + rows == last_row:
            south[pl.ds(at, 1), :] = field[rows - 1 : rows]


def edges_kernel(rows, state_ref, depth_ref, *strips):
    k = pl.program_id(0)
    height = depth_ref.shape[0]
    for r0 in range(0, height, rows):
        part = slice(r0, r0 + rows)
        depth = depth_ref[part, :]
        fields = [state_ref[g, 0, part, :] for g in range(6)]
        fields = fields[:2] + [depth * field for field in fields[2:]]
        put_edges(strips, k, rows, r0, height, fields)


def force(force_ref, channel, r0, rows, half):
    side = r0 // half
    at = r0 % half
    return force_ref[channel, at : at + rows, side * LANES : (side + 1) * LANES]


def join_kernel(rows, omega_ref, eta_ref, east_ref, north_ref, depth_ref, ocean_ref, re_ref, im_ref, out_ref, *strips):
    k = pl.program_id(0)
    omega = omega_ref[k]
    weight = RELAX / (1.0 + omega * omega)
    height = depth_ref.shape[0]
    for r0 in range(0, height, rows):
        part = slice(r0, r0 + rows)
        depth = depth_ref[part, :]
        ocean = ocean_ref[part, :].astype(jnp.float32) * weight
        f_re = force(re_ref, 0, r0, rows, height // 2)
        f_im = force(im_ref, 0, r0, rows, height // 2)
        eta_re = eta_ref[0, 0, part, :] + ocean * (f_re + f_im * omega)
        eta_im = eta_ref[1, 0, part, :] + ocean * (f_im - f_re * omega)
        out_ref[0, 0, part, :] = eta_re
        out_ref[1, 0, part, :] = eta_im
        fields = [eta_re, eta_im] + [
            depth * ref[g, 0, part, :] for ref in (east_ref, north_ref) for g in range(2)
        ]
        put_edges(strips, k, rows, r0, height, fields)


def sweep_kernel(rows, forced, edges, *refs):
    refs = list(refs)
    omega_ref, eta_ref, vel_e_ref, vel_n_ref, pot_ref = refs[:5]
    depth_ref, drag_ref, ocean_ref, turn_ref = refs[5:9]
    north_in, south_in, west_in, east_in = refs[9:13]
    refs = refs[13:]
    if forced:
        re_ref, im_ref = refs[:2]
        refs = refs[2:]
    out_ref = refs[0]
    strips = refs[1:]
    k = pl.program_id(0)
    omega = omega_ref[k]
    inv_eta = 1.0 / (1.0 + omega * omega)
    height = depth_ref.shape[0]
    lane = iota((rows, LANES), 1)
    row = iota((rows, LANES), 0)

    def dlon(q, group, r0):
        at = group * 8 + k
        part = slice(r0, r0 + rows)
        left = pltpu.roll(q, 1, 1)
        right = pltpu.roll(q, LANES - 1, 1)
        w = pltpu.roll(west_in[part, :], (LANES - at) % LANES, 1)
        e = pltpu.roll(east_in[part, :], LANES - 1 - at, 1)
        return (jnp.where(lane == LANES - 1, e, right) - jnp.where(lane == 0, w, left)) * 0.5

    def shifted(q, first, last, group, r0):
        at = group * 8 + k
        above = first if r0 > 0 else north_in[pl.ds(at, 1), :]
        below = last if r0 + rows < height else south_in[pl.ds(at, 1), :]
        up = jnp.where(row == 0, above, pltpu.roll(q, 1, 0))
        down = jnp.where(row == rows - 1, below, pltpu.roll(q, rows - 1, 0))
        return (down - up) * 0.5

    for r0 in range(0, height, rows):
        part = slice(r0, r0 + rows)
        before = slice(max(r0 - 1, 0), max(r0 - 1, 0) + 1)
        after = slice(min(r0 + rows, height - 1), min(r0 + rows, height - 1) + 1)
        depth = depth_ref[part, :]
        diag = 1.0 + drag_ref[part, :]
        ocean = ocean_ref[part, :].astype(jnp.float32)
        turn = turn_ref[part, :]
        inv = 1.0 / (diag * diag + omega * omega)
        eta = [eta_ref[g, 0, part, :] for g in range(2)]
        east = [vel_e_ref[g, 0, part, :] for g in range(2)]
        north = [vel_n_ref[g, 0, part, :] for g in range(2)]
        pot = [pot_ref[g, 0, part, :] for g in range(6)]
        flux = []
        grad_lat = []
        for g in range(2):
            hn = depth * north[g]
            hn_first = depth_ref[before, :] * vel_n_ref[g, 0, before, :]
            hn_last = depth_ref[after, :] * vel_n_ref[g, 0, after, :]
            flux.append(
                dlon(depth * east[g], 2 + g, r0) + shifted(hn, hn_first, hn_last, 2 + g, r0)
            )
            grad_lat.append(
                shifted(eta[g], eta_ref[g, 0, before, :], eta_ref[g, 0, after, :], g, r0)
            )
        grad_lon = [dlon(eta[g], g, r0) for g in range(2)]
        res_re = pot[0] - (eta[0] - omega * eta[1] + flux[0])
        res_im = pot[1] - (eta[1] + omega * eta[0] + flux[1])
        if forced:
            res_re = res_re + force(re_ref, 0, r0, rows, height // 2)
            res_im = res_im + force(im_ref, 0, r0, rows, height // 2)
        weight = ocean * RELAX
        new = [
            ocean * eta[0] + weight * ((res_re + res_im * omega) * inv_eta),
            ocean * eta[1] + weight * ((res_im - res_re * omega) * inv_eta),
        ]
        scaled = weight * inv
        for own, other, grad, at, sign in (
            (east, north, grad_lon, 2, -1.0),
            (north, east, grad_lat, 4, 1.0),
        ):
            spun = [sign * (turn * other[g]) for g in range(2)]
            res_re = pot[at] - (diag * own[0] - omega * own[1] + spun[0] + grad[0])
            res_im = pot[at + 1] - (diag * own[1] + omega * own[0] + spun[1] + grad[1])
            new.append(ocean * own[0] + scaled * (res_re * diag + res_im * omega))
            new.append(ocean * own[1] + scaled * (res_im * diag - res_re * omega))
        for g in range(6):
            out_ref[g, 0, part, :] = new[g]
        if edges:
            put_edges(strips, k, rows, r0, height, new[:2] + [depth * q for q in new[2:]])


def local(
    tide_state, potential, water_depth, drag_coeff, ocean_mask, residual_rows, dest_tile, dest_cell
):
    f32 = jnp.float32
    tiles = lax.axis_size("lon")
    lats = lax.axis_size("lat")
    width, row_count = residual_rows.shape
    capacity = 2 * row_count // tiles
    height, across = water_depth.shape
    consts = tide_state.shape[0] // 6
    blocks = row_count // BLOCK
    windows = capacity // LANES
    bucket_rows = windows * (width + 1) + HEAD
    me = lax.axis_index("lon").reshape(1)

    omega = jnp.asarray(OMEGAS, f32)
    row_ids = lax.axis_index("lat") * height + jnp.arange(height, dtype=jnp.int32)
    lat_pos = (row_ids.astype(f32) + 0.5) / (height * lats) - 0.5
    turn = jnp.broadcast_to((0.5 * jnp.sin(jnp.pi * lat_pos))[:, None], (height, across))

    state = tide_state.reshape(6, consts, height, across)
    pot = potential.reshape(6, consts, height, across)
    chunk_rows = 32

    def fields(count, first):
        return pl.BlockSpec((count, 1, height, across), lambda k: (first // count, k, 0, 0))

    plane = pl.BlockSpec((height, across), lambda k: (0, 0))
    flat = pl.BlockSpec((4 * consts, across), lambda k: (0, 0))
    half_re = pl.BlockSpec((1, height // 2, 2 * across), lambda k: (k, 0, 0))
    half_im = pl.BlockSpec((1, height // 2, 2 * across), lambda k: (consts + k, 0, 0))
    strip_specs = [flat, flat, plane, plane]
    strip_shapes = [jax.ShapeDtypeStruct((4 * consts, across), f32)] * 2 + [
        jax.ShapeDtypeStruct((height, across), f32)
    ] * 2
    state_shape = jax.ShapeDtypeStruct(state.shape, f32)

    def exchange(strips):
        north, south, west, east = strips
        return (
            lax.ppermute(south, "lat", [(i, i + 1) for i in range(lats - 1)]),
            lax.ppermute(north, "lat", [(i + 1, i) for i in range(lats - 1)]),
            lax.ppermute(east, "lon", [(i, (i + 1) % tiles) for i in range(tiles)]),
            lax.ppermute(west, "lon", [((i + 1) % tiles, i) for i in range(tiles)]),
        )

    def sweep(eta, vel, strips, forcing, edges):
        forced = forcing is not None
        out = pl.pallas_call(
            functools.partial(sweep_kernel, chunk_rows, forced, edges),
            grid=(consts,),
            in_specs=[SMEM, fields(2, 0), fields(2, 2), fields(2, 4), fields(6, 0)]
            + [plane] * 4
            + strip_specs
            + ([half_re, half_im] if forced else []),
            out_specs=[fields(6, 0)] + (strip_specs if edges else []),
            out_shape=[state_shape] + (strip_shapes if edges else []),
            compiler_params=params(32),
            cost_estimate=cost(16 * 10**6, 9 * 10**6),
        )(
            omega, eta, vel, vel, pot, water_depth, drag_coeff, ocean_mask, turn, *strips,
            *((forcing, forcing) if forced else ()),
        )
        return out[0], out[1:]

    table = jax.ShapeDtypeStruct((blocks, LANES), jnp.int32)
    slot, counts, bases, places, totals = pl.pallas_call(
        functools.partial(rank_kernel, tiles),
        in_specs=[VMEM],
        out_specs=[VMEM] * 5,
        out_shape=[jax.ShapeDtypeStruct((blocks, BLOCK), jnp.int32), table, table, table]
        + [jax.ShapeDtypeStruct((8, LANES), jnp.int32)],
        compiler_params=params(32),
    )(dest_tile.reshape(blocks, BLOCK))

    strips = pl.pallas_call(
        functools.partial(edges_kernel, chunk_rows),
        grid=(consts,),
        in_specs=[fields(6, 0), plane],
        out_specs=strip_specs,
        out_shape=strip_shapes,
        compiler_params=params(32),
        cost_estimate=cost(10**6, 3 * 10**6),
    )(state, water_depth)
    strips = exchange(strips)

    group = min(32, blocks)
    buckets = pl.pallas_call(
        functools.partial(bucket_kernel, tiles, capacity, width, group),
        in_specs=[SMEM] * 5 + [VMEM] * 3,
        out_specs=[VMEM] * tiles,
        out_shape=[jax.ShapeDtypeStruct((bucket_rows, LANES), f32)] * tiles,
        scratch_shapes=[
            pltpu.VMEM(((group + 1) * BLOCK, LANES), f32),
            pltpu.VMEM((tiles * (capacity + BLOCK), LANES), f32),
        ],
        compiler_params=params(58),
        cost_estimate=cost(10**10, 7 * 10**6),
    )(me, counts, bases, places, totals, slot, dest_cell.reshape(blocks, BLOCK), residual_rows)

    grid_shape = jax.ShapeDtypeStruct((width, height // 2, 2 * across), f32)

    def add(parts, total):
        return pl.pallas_call(
            functools.partial(sum_kernel, width, windows, len(parts), total is None),
            in_specs=[VMEM] * (len(parts) + (total is not None)),
            out_specs=VMEM,
            out_shape=grid_shape,
            compiler_params=params(40),
            cost_estimate=cost(10**10, 3 * 10**6),
        )(*parts, *(() if total is None else (total,)))

    order = list(range(tiles // 2, tiles)) + list(range(1, tiles // 2))
    arrived = [
        lax.ppermute(buckets[s], "lon", [(i, i ^ s) for i in range(tiles)]) for s in order
    ]
    state, _ = sweep(state, state, strips, None, False)
    forcing = add([buckets[0]], None)
    each = tiles // 8
    for first in range(0, len(arrived), each):
        forcing = add(arrived[first : first + each], forcing)

    eta, *strips = pl.pallas_call(
        functools.partial(join_kernel, chunk_rows),
        grid=(consts,),
        in_specs=[
            SMEM,
            fields(2, 0),
            fields(2, 2),
            fields(2, 4),
            plane,
            plane,
            half_re,
            half_im,
        ],
        out_specs=[fields(2, 0)] + strip_specs,
        out_shape=[jax.ShapeDtypeStruct((2,) + state.shape[1:], f32)] + strip_shapes,
        compiler_params=params(32),
        cost_estimate=cost(10**6, 6 * 10**6),
    )(omega, state, state, state, water_depth, ocean_mask, forcing, forcing)
    state, strips = sweep(eta, state, exchange(strips), forcing, True)
    state, _ = sweep(state, state, exchange(strips), forcing, False)
    return state.reshape(tide_state.shape)


def solution(mesh):
    placed = (
        P(None, "lat", "lon"),
        P(None, "lat", "lon"),
        P("lat", "lon"),
        P("lat", "lon"),
        P("lat", "lon"),
        P(None, ("lat", "lon")),
        P(("lat", "lon"), None),
        P(("lat", "lon")),
    )
    return jax.shard_map(
        local, mesh=mesh, in_specs=placed, out_specs=P(None, "lat", "lon"), check_vma=False
    )
```

time: 1050 us -> 281 us (0.27)
  other arithmetic: 577 us -> 1.91 us
  local copies, waits for them, and re-layouts: 381 us -> 8.18 us
  Pallas kernels: 0 us -> 109 us
  waiting for transfers between devices: 7.49 us -> 69.3 us
  starting transfers between devices: 71.5 us -> 90.8 us
    scatter-add x1 -> x0, other arithmetic: 399 us -> none  [local(): jax.ops.segment_sum(values, arrived.reshape(-1), num_segments=cell_count...]
    scatter x2 -> x0, local copies, waits for them, and re-layouts: 214 us -> none  [the longest x1 121 us: local(): jnp.full((tiles * capacity,), cell_count, jnp.int32).at[slot]]
    pallas_call x0 -> x15, Pallas kernels: none -> 109 us  [the longest x1 50.7 us: local(): pl.pallas_call(functools.partial(bucket_kernel, tiles, capacity, width, g...]
    sort x1 -> x0, other arithmetic: 86.1 us -> none  [local(): lax.sort((target, dest_cell) + columns, dimension=0, is_stable=True, num_...]
    ppermute x16 -> x19, waiting for transfers between devices: 7.49 us -> 69.3 us  [the longest x3 33.2 us: exchange(): lax.ppermute(west, 'lon', [((i + 1) % tiles, i) for i in range(tiles)])]
    slice x17 -> x0, local copies, waits for them, and re-layouts: 53.8 us -> none  [the longest x8 23.4 us: with_halo(): lax.slice_in_dim(cells, cells.shape[dim] - width, cells.shape[dim], axis=...]
    unnamed x15 -> x1, other arithmetic: 35.2 us -> 1.86 us
    ppermute x16 -> x19, starting transfers between devices: 60.8 us -> 90.8 us  [the longest x7 27.1 us: local(): lax.ppermute(buckets[s], 'lon', [(i, i ^ s) for i in range(tiles)])]
  transfers between devices with their start and end apart: 18 -> 19, of which waited for: 3 -> 7; matrix products, arithmetic and copies ran while one was open for 22% -> 0% of each run, Pallas kernels for 0% -> 12%
where the time goes in v1:
time: 281 us; the launch traced here: 279 us
  Pallas kernels  109 us (39%)
  starting transfers between devices  90.8 us (32%)
  waiting for transfers between devices  69.3 us (25%)
  local copies, waits for them, and re-layouts  8.18 us (3%)
    pallas_call x1, Pallas kernels, local(): pl.pallas_call(functools.partial(bucket_kernel, tiles, capacity, width, g...  50.7 us
    pallas_call x8, Pallas kernels, add(): pl.pallas_call(functools.partial(sum_kernel, width, windows, len(parts),...  34.5 us
    ppermute x3, waiting for transfers between devices, exchange(): lax.ppermute(west, 'lon', [((i + 1) % tiles, i) for i in range(tiles)])  33.2 us
    ppermute x7, waiting for transfers between devices, local(): lax.ppermute(buckets[s], 'lon', [(i, i ^ s) for i in range(tiles)])  27.5 us
    ppermute x7, starting transfers between devices, local(): lax.ppermute(buckets[s], 'lon', [(i, i ^ s) for i in range(tiles)])  27.1 us
    ppermute x3, starting transfers between devices, exchange(): lax.ppermute(west, 'lon', [((i + 1) % tiles, i) for i in range(tiles)])  23.7 us
    ppermute x3, starting transfers between devices, exchange(): lax.ppermute(east, 'lon', [(i, (i + 1) % tiles) for i in range(tiles)])  23 us
    pallas_call x3, Pallas kernels, sweep(): pl.pallas_call(functools.partial(sweep_kernel, chunk_rows, forced, edges)...  17.6 us
  transfers between devices with their start and end apart: 19, of which 7 were waited for; matrix products, arithmetic and copies ran while one was open for 0% of the time, Pallas kernels for 12%

profile of v1, /device:TPU:0, one launch (start us, length us, event | category | flops | bytes accessed | tf_op | source)
XLA Modules:
  0.0 279.3 jit_solution(17026831704666711560)
XLA Ops:
  0.5 1.9 reduce.3
  6.0 1.6 reshape.33.refs_1_
  7.6 50.7 %shard_map.94 = (f32[1096,128]{1,0:T(8,128)}, f32[1096,128]{1,0:T(8,128)}, f32[1096,128]{1,0:T(8,128)}, f32[1096,128]{1,0:T(8,128)}, f32[1096,128]{1,0:T(8,128)}...) custom-call(s32[1]{0:T(128)} %bitcast.2.me_ref, s32[128,128]{1,0:T(8,128)} %copy-done.8, ...), custom_call_target="tpu_custom_call" | custom-call | flops 10000000000 | bytes 7000000 | tf_op jit(solution)/shard_map/pallas_call | solution.py:433
  58.3 4.4 %collective-permute-start.10 = (f32[1096,128]{1,0:T(8,128)}, f32[1096,128]{1,0:T(8,128)}, u32[]{:S(2)}, u32[]{:S(2)}) collective-permute-start(f32[1096,128]{1,0:T(8,128)} %get-tuple-element.47), channel_id=1, source_target_pairs={{0,4},{1,5},{2,6},{3,7},{4,0},{5,1},{6,2},{7,3},{8,12},{9,13},{10,... | collective-permute-start | bytes 1683464 | tf_op jit(solution)/shard_map/ppermute | solution.py:460
  62.7 2.6 shard_map.91
  65.3 3.5 %collective-permute-start.3 = (f32[128,128]{1,0:T(8,128)}, f32[128,128]{1,0:T(8,128)S(1)}, u32[]{:S(2)}, u32[]{:S(2)}) collective-permute-start(f32[128,128]{1,0:T(8,128)} %get-tuple-element.35), channel_id=1, source_target_pairs={{1,0},{2,1},{3,2},{4,3},{5,4},{6,5},{7,6},{0,7},{9,8},{10,9},{11,1... | collective-permute-start | bytes 196616 | tf_op jit(solution)/shard_map/ppermute | solution.py:389
  68.9 3.0 %collective-permute-start = (f32[32,128]{1,0:T(8,128)S(1)}, f32[32,128]{1,0:T(8,128)S(1)}, u32[]{:S(2)}, u32[]{:S(2)}) collective-permute-start(f32[32,128]{1,0:T(8,128)S(1)} %get-tuple-element.32), channel_id=1, source_target_pairs={{0,8},{8,16},{16,24},{1,9},{9,17},{17,25},{2,10},{10,18},{18,26},{... | collective-permute-start | bytes 49160 | tf_op jit(solution)/shard_map/ppermute | solution.py:386
  73.2 5.9 %shard_map.95.refs_1_ = f32[16,64,256]{2,1,0:T(8,128)S(1)} custom-call(f32[1096,128]{1,0:T(8,128)S(1)} %copy-done.14), custom_call_target="tpu_custom_call" | custom-call | flops 10000000000 | bytes 3000000 | tf_op jit(solution)/shard_map/pallas_call | solution.py:449
  80.1 6.5 %collective-permute-start.9 = (f32[1096,128]{1,0:T(8,128)}, f32[1096,128]{1,0:T(8,128)S(1)}, u32[]{:S(2)}, u32[]{:S(2)}) collective-permute-start(f32[1096,128]{1,0:T(8,128)} %get-tuple-element.46), channel_id=1, source_target_pairs={{0,5},{1,4},{2,7},{3,6},{4,1},{5,0},{6,3},{7,2},{8,13},{9,12},{10,... | collective-permute-start | bytes 1683464 | tf_op jit(solution)/shard_map/ppermute | solution.py:460
  86.6 5.2 %collective-permute-start.7 = (f32[1096,128]{1,0:T(8,128)}, f32[1096,128]{1,0:T(8,128)S(1)}, u32[]{:S(2)}, u32[]{:S(2)}) collective-permute-start(f32[1096,128]{1,0:T(8,128)} %get-tuple-element.44), channel_id=1, source_target_pairs={{0,7},{1,6},{2,5},{3,4},{4,3},{5,2},{6,1},{7,0},{8,15},{9,14},{10,... | collective-permute-start | bytes 1683464 | tf_op jit(solution)/shard_map/ppermute | solution.py:460
  92.0 1.9 copy-done.1
  93.9 4.5 %shard_map.92.eta_ref.east_ref.north_ref.refs_2_.refs_3_ = f32[6,8,128,128]{3,2,1,0:T(8,128)S(1)} custom-call(f32[8]{0:T(128)S(1)} %copy-done.6, f32[6,8,128,128]{3,2,1,0:T(8,128)S(1)} %bitcast.6, f32[6,8,128,128]{3,2,1,0:T(8,128)S(1)} %bitcast.7, f32[6,8,128,128]{3,2,1,0:T(8,128)S(1)} %bitcast.8, f32[6,8,128,128]{3,2,1,0:T(8,128)S(1)} %bitcast.9, ...), custom_call_target="tpu_custom_call" | custom-call | flops 16000000 | bytes 9000000 | tf_op jit(solution)/shard_map/pallas_call | solution.py:394
  98.5 26.9 %collective-permute-done.10.refs_0_ = f32[1096,128]{1,0:T(8,128)} collective-permute-done((f32[1096,128]{1,0:T(8,128)}, f32[1096,128]{1,0:T(8,128)}, u32[]{:S(2)}, u32[]{:S(2)}) %collective-permute-start.10) | collective-permute-done | bytes 561184 | tf_op jit(solution)/shard_map/ppermute | solution.py:460
  125.4 9.7 %collective-permute-start.5 = (f32[1096,128]{1,0:T(8,128)S(1)}, f32[1096,128]{1,0:T(8,128)S(1)}, u32[]{:S(2)}, u32[]{:S(2)}) collective-permute-start(f32[1096,128]{1,0:T(8,128)S(1)} %copy-done.16), channel_id=1, source_target_pairs={{0,2},{1,3},{2,0},{3,1},{4,6},{5,7},{6,4},{7,5},{8,10},{9,11},{10,... | collective-permute-start | bytes 1683464 | tf_op jit(solution)/shard_map/ppermute | solution.py:460
  135.1 3.6 %shard_map.96.refs_1_ = f32[16,64,256]{2,1,0:T(8,128)S(1)} custom-call(f32[1096,128]{1,0:T(8,128)} %collective-permute-done.10.refs_0_, f32[16,64,256]{2,1,0:T(8,128)S(1)} %copy-done.13), custom_call_target="tpu_custom_call" | custom-call | flops 10000000000 | bytes 3000000 | tf_op jit(solution)/shard_map/pallas_call | solution.py:449
  139.9 2.6 shard_map.97.refs_1_
  142.5 3.5 %shard_map.98.refs_1_ = f32[16,64,256]{2,1,0:T(8,128)S(1)} custom-call(f32[1096,128]{1,0:T(8,128)S(1)} %collective-permute-done.8.refs_0_, f32[16,64,256]{2,1,0:T(8,128)S(1)} %shard_map.97.refs_1_), custom_call_target="tpu_custom_call" | custom-call | flops 10000000000 | bytes 3000000 | tf_op jit(solution)/shard_map/pallas_call | solution.py:449
  146.1 4.5 %shard_map.99.refs_1_ = f32[16,64,256]{2,1,0:T(8,128)S(1)} custom-call(f32[1096,128]{1,0:T(8,128)S(1)} %collective-permute-done.7.refs_0_, f32[16,64,256]{2,1,0:T(8,128)S(1)} %shard_map.98.refs_1_), custom_call_target="tpu_custom_call" | custom-call | flops 10000000000 | bytes 3000000 | tf_op jit(solution)/shard_map/pallas_call | solution.py:449
  150.6 2.6 shard_map.100.refs_1_
  153.2 3.5 %shard_map.101.refs_1_ = f32[16,64,256]{2,1,0:T(8,128)S(1)} custom-call(f32[1096,128]{1,0:T(8,128)S(1)} %collective-permute-done.5.refs_0_, f32[16,64,256]{2,1,0:T(8,128)S(1)} %shard_map.100.refs_1_), custom_call_target="tpu_custom_call" | custom-call | flops 10000000000 | bytes 3000000 | tf_op jit(solution)/shard_map/pallas_call | solution.py:449
  157.3 8.3 %shard_map.102.re_ref.im_ref.refs_13_.refs_14_ = f32[16,64,256]{2,1,0:T(8,128)S(1)} custom-call(f32[1096,128]{1,0:T(8,128)S(1)} %collective-permute-done.4.refs_0_, f32[16,64,256]{2,1,0:T(8,128)S(1)} %shard_map.101.refs_1_), custom_call_target="tpu_custom_call" | custom-call | flops 10000000000 | bytes 3000000 | tf_op jit(solution)/shard_map/pallas_call | solution.py:449
  165.6 2.9 %shard_map.103 = (f32[2,8,128,128]{3,2,1,0:T(8,128)S(1)}, f32[32,128]{1,0:T(8,128)S(1)}, f32[32,128]{1,0:T(8,128)S(1)}, f32[128,128]{1,0:T(8,128)S(1)}, f32[128,128]{1,0:T(8,128)S(1)}) custom-call(f32[8]{0:T(128)S(1)} %copy-done.6, f32[6,8,128,128]{3,2,1,0:T(8,128)S(1)} %shard_map.92.eta_ref.east_ref.north_ref.refs_2_.refs_3_, ...), custom_call_target="tpu_custom_call" | custom-call | flops 1000000 | bytes 6000000 | tf_op jit(solution)/shard_map/pallas_call | solution.py:468
  168.6 15.8 %collective-permute-start.13 = (f32[128,128]{1,0:T(8,128)S(1)}, f32[128,128]{1,0:T(8,128)S(1)}, u32[]{:S(2)}, u32[]{:S(2)}) collective-permute-start(f32[128,128]{1,0:T(8,128)S(1)} %get-tuple-element.52), channel_id=1, source_target_pairs={{0,1},{1,2},{2,3},{3,4},{4,5},{5,6},{6,7},{7,0},{8,9},{9,10},{10,1... | collective-permute-start | bytes 196616 | tf_op jit(solution)/shard_map/ppermute | solution.py:388
  184.4 20.2 %collective-permute-start.14 = (f32[128,128]{1,0:T(8,128)S(1)}, f32[128,128]{1,0:T(8,128)S(1)}, u32[]{:S(2)}, u32[]{:S(2)}) collective-permute-start(f32[128,128]{1,0:T(8,128)S(1)} %get-tuple-element.53), channel_id=1, source_target_pairs={{1,0},{2,1},{3,2},{4,3},{5,4},{6,5},{7,6},{0,7},{9,8},{10,9},{11,1... | collective-permute-start | bytes 196616 | tf_op jit(solution)/shard_map/ppermute | solution.py:389
  204.5 5.6 %collective-permute-start.11 = (f32[32,128]{1,0:T(8,128)S(1)}, f32[32,128]{1,0:T(8,128)S(1)}, u32[]{:S(2)}, u32[]{:S(2)}) collective-permute-start(f32[32,128]{1,0:T(8,128)S(1)} %get-tuple-element.50), channel_id=1, source_target_pairs={{0,8},{8,16},{16,24},{1,9},{9,17},{17,25},{2,10},{10,18},{18,26},{... | collective-permute-start | bytes 49160 | tf_op jit(solution)/shard_map/ppermute | solution.py:386
  211.6 4.2 %collective-permute-done.12.refs_10_ = f32[32,128]{1,0:T(8,128)S(1)} collective-permute-done((f32[32,128]{1,0:T(8,128)S(1)}, f32[32,128]{1,0:T(8,128)S(1)}, u32[]{:S(2)}, u32[]{:S(2)}) %collective-permute-start.12) | collective-permute-done | bytes 16416 | tf_op jit(solution)/shard_map/ppermute | solution.py:387
  215.8 33.1 %collective-permute-done.14.refs_12_ = f32[128,128]{1,0:T(8,128)S(1)} collective-permute-done((f32[128,128]{1,0:T(8,128)S(1)}, f32[128,128]{1,0:T(8,128)S(1)}, u32[]{:S(2)}, u32[]{:S(2)}) %collective-permute-start.14) | collective-permute-done | bytes 65568 | tf_op jit(solution)/shard_map/ppermute | solution.py:389
  248.9 7.1 %shard_map.104 = (f32[6,8,128,128]{3,2,1,0:T(8,128)S(1)}, f32[32,128]{1,0:T(8,128)S(1)}, f32[32,128]{1,0:T(8,128)S(1)}, f32[128,128]{1,0:T(8,128)S(1)}, f32[128,128]{1,0:T(8,128)S(1)}) custom-call(f32[8]{0:T(128)S(1)} %copy-done.6, f32[2,8,128,128]{3,2,1,0:T(8,128)S(1)} %get-tuple-element.49.refs_1_, ...), custom_call_target="tpu_custom_call" | custom-call | flops 16000000 | bytes 9000000 | tf_op jit(solution)/shard_map/pallas_call | solution.py:394
  256.1 7.3 %collective-permute-start.17 = (f32[128,128]{1,0:T(8,128)S(1)}, f32[128,128]{1,0:T(8,128)S(1)}, u32[]{:S(2)}, u32[]{:S(2)}) collective-permute-start(f32[128,128]{1,0:T(8,128)S(1)} %get-tuple-element.57), channel_id=1, source_target_pairs={{0,1},{1,2},{2,3},{3,4},{4,5},{5,6},{6,7},{7,0},{8,9},{9,10},{10,1... | collective-permute-start | bytes 196616 | tf_op jit(solution)/shard_map/ppermute | solution.py:388
  263.4 4.4 %collective-permute-start.15 = (f32[32,128]{1,0:T(8,128)S(1)}, f32[32,128]{1,0:T(8,128)S(1)}, u32[]{:S(2)}, u32[]{:S(2)}) collective-permute-start(f32[32,128]{1,0:T(8,128)S(1)} %get-tuple-element.55), channel_id=1, source_target_pairs={{0,8},{8,16},{16,24},{1,9},{9,17},{17,25},{2,10},{10,18},{18,26},{... | collective-permute-start | bytes 49160 | tf_op jit(solution)/shard_map/ppermute | solution.py:386
  269.2 4.2 %collective-permute-done.16.refs_10_ = f32[32,128]{1,0:T(8,128)S(1)} collective-permute-done((f32[32,128]{1,0:T(8,128)S(1)}, f32[32,128]{1,0:T(8,128)S(1)}, u32[]{:S(2)}, u32[]{:S(2)}) %collective-permute-start.16) | collective-permute-done | bytes 16416 | tf_op jit(solution)/shard_map/ppermute | solution.py:387
  273.4 5.9 %shard_map.105 = f32[6,8,128,128]{3,2,1,0:T(8,128)} custom-call(f32[8]{0:T(128)S(1)} %copy-done.6, f32[6,8,128,128]{3,2,1,0:T(8,128)S(1)} %get-tuple-element.54.refs_1_.refs_2_.refs_3_, f32[6,8,128,128]{3,2,1,0:T(8,128)S(1)} %get-tuple-element.54.refs_1_.refs_2_.refs_3_, f32[6,8,128,128]{3,2,1,0:T(8,128)S(1)} %get-tuple-element.54.refs_1_.refs_2_.refs_3_, ...), custom_call_target="tpu_custom_call" | custom-call | flops 16000000 | bytes 9000000 | tf_op jit(solution)/shard_map/pallas_call | solution.py:394
  (61 shorter events, 11.3 us)
Async XLA Ops:
  2.9 0.7 copy-start.7
  7.5 55.2 %copy-start = (f32[48,128,128]{2,1,0:T(8,128)S(1)}, f32[48,128,128]{2,1,0:T(8,128)}, u32[]{:S(2)}) copy-start(f32[48,128,128]{2,1,0:T(8,128)} %param.9) | copy-start | bytes 9437188
  7.6 55.2 %copy-start.3 = (f32[128,128]{1,0:T(8,128)S(1)}, f32[128,128]{1,0:T(8,128)}, u32[]{:S(2)}) copy-start(f32[128,128]{1,0:T(8,128)} %refs_5_.5) | copy-start | bytes 196612
  58.3 14.9 %copy-start.14 = (f32[1096,128]{1,0:T(8,128)S(1)}, f32[1096,128]{1,0:T(8,128)}, u32[]{:S(2)}) copy-start(f32[1096,128]{1,0:T(8,128)} %get-tuple-element.48.refs_0_) | copy-start | bytes 1683460
  58.3 67.1 %collective-permute-start.10 = (f32[1096,128]{1,0:T(8,128)}, f32[1096,128]{1,0:T(8,128)}, u32[]{:S(2)}, u32[]{:S(2)}) collective-permute-start(f32[1096,128]{1,0:T(8,128)} %get-tuple-element.47), channel_id=1, source_target_pairs={{0,4},{1,5},{2,6},{3,7},{4,0},{5,1},{6,2},{7,3},{8,12},{9,13},{10,... | collective-permute-start | bytes 1683464 | tf_op jit(solution)/shard_map/ppermute | solution.py:460
  65.3 21.3 %collective-permute-start.2 = (f32[128,128]{1,0:T(8,128)}, f32[128,128]{1,0:T(8,128)S(1)}, u32[]{:S(2)}, u32[]{:S(2)}) collective-permute-start(f32[128,128]{1,0:T(8,128)} %get-tuple-element.34), channel_id=1, source_target_pairs={{0,1},{1,2},{2,3},{3,4},{4,5},{5,6},{6,7},{7,0},{8,9},{9,10},{10,1... | collective-permute-start | bytes 196616 | tf_op jit(solution)/shard_map/ppermute | solution.py:388
  65.3 26.5 %collective-permute-start.3 = (f32[128,128]{1,0:T(8,128)}, f32[128,128]{1,0:T(8,128)S(1)}, u32[]{:S(2)}, u32[]{:S(2)}) collective-permute-start(f32[128,128]{1,0:T(8,128)} %get-tuple-element.35), channel_id=1, source_target_pairs={{1,0},{2,1},{3,2},{4,3},{5,4},{6,5},{7,6},{0,7},{9,8},{10,9},{11,1... | collective-permute-start | bytes 196616 | tf_op jit(solution)/shard_map/ppermute | solution.py:389
  68.9 11.3 %collective-permute-start = (f32[32,128]{1,0:T(8,128)S(1)}, f32[32,128]{1,0:T(8,128)S(1)}, u32[]{:S(2)}, u32[]{:S(2)}) collective-permute-start(f32[32,128]{1,0:T(8,128)S(1)} %get-tuple-element.32), channel_id=1, source_target_pairs={{0,8},{8,16},{16,24},{1,9},{9,17},{17,25},{2,10},{10,18},{18,26},{... | collective-permute-start | bytes 49160 | tf_op jit(solution)/shard_map/ppermute | solution.py:386
  71.9 14.7 %collective-permute-start.1 = (f32[32,128]{1,0:T(8,128)S(1)}, f32[32,128]{1,0:T(8,128)S(1)}, u32[]{:S(2)}, u32[]{:S(2)}) collective-permute-start(f32[32,128]{1,0:T(8,128)S(1)} %get-tuple-element.33), channel_id=1, source_target_pairs={{8,0},{16,8},{24,16},{9,1},{17,9},{25,17},{10,2},{18,10},{26,18},{... | collective-permute-start | bytes 49160 | tf_op jit(solution)/shard_map/ppermute | solution.py:387
  73.2 18.8 %copy-start.4 = (s32[128,128]{1,0:T(8,128)S(1)}, s32[128,128]{1,0:T(8,128)}, u32[]{:S(2)}) copy-start(s32[128,128]{1,0:T(8,128)} %refs_7_.5) | copy-start | bytes 196612
  73.2 18.8 %copy-start.5 = (f32[128,128]{1,0:T(8,128)S(1)}, f32[128,128]{1,0:T(8,128)}, u32[]{:S(2)}) copy-start(f32[128,128]{1,0:T(8,128)} %refs_6_.5) | copy-start | bytes 196612
  73.2 18.8 %copy-start.6 = (f32[8]{0:T(128)S(1)}, f32[8]{0:T(128)}, u32[]{:S(2)}) copy-start(f32[8]{0:T(128)} %constant.21.clone.refs_0_.omega_ref) | copy-start | bytes 100
  79.1 1.0 copy-start.12
  80.1 58.6 %collective-permute-start.9 = (f32[1096,128]{1,0:T(8,128)}, f32[1096,128]{1,0:T(8,128)S(1)}, u32[]{:S(2)}, u32[]{:S(2)}) collective-permute-start(f32[1096,128]{1,0:T(8,128)} %get-tuple-element.46), channel_id=1, source_target_pairs={{0,5},{1,4},{2,7},{3,6},{4,1},{5,0},{6,3},{7,2},{8,13},{9,12},{10,... | collective-permute-start | bytes 1683464 | tf_op jit(solution)/shard_map/ppermute | solution.py:460
  86.6 55.9 %collective-permute-start.8 = (f32[1096,128]{1,0:T(8,128)}, f32[1096,128]{1,0:T(8,128)S(1)}, u32[]{:S(2)}, u32[]{:S(2)}) collective-permute-start(f32[1096,128]{1,0:T(8,128)} %get-tuple-element.45), channel_id=1, source_target_pairs={{0,6},{1,7},{2,4},{3,5},{4,2},{5,3},{6,0},{7,1},{8,14},{9,15},{10,... | collective-permute-start | bytes 1683464 | tf_op jit(solution)/shard_map/ppermute | solution.py:460
  86.6 59.5 %collective-permute-start.7 = (f32[1096,128]{1,0:T(8,128)}, f32[1096,128]{1,0:T(8,128)S(1)}, u32[]{:S(2)}, u32[]{:S(2)}) collective-permute-start(f32[1096,128]{1,0:T(8,128)} %get-tuple-element.44), channel_id=1, source_target_pairs={{0,7},{1,6},{2,5},{3,4},{4,3},{5,2},{6,1},{7,0},{8,15},{9,14},{10,... | collective-permute-start | bytes 1683464 | tf_op jit(solution)/shard_map/ppermute | solution.py:460
  91.8 58.8 %collective-permute-start.6 = (f32[1096,128]{1,0:T(8,128)}, f32[1096,128]{1,0:T(8,128)S(1)}, u32[]{:S(2)}, u32[]{:S(2)}) collective-permute-start(f32[1096,128]{1,0:T(8,128)} %get-tuple-element.43), channel_id=1, source_target_pairs={{0,1},{1,0},{2,3},{3,2},{4,5},{5,4},{6,7},{7,6},{8,9},{9,8},{10,11... | collective-permute-start | bytes 1683464 | tf_op jit(solution)/shard_map/ppermute | solution.py:460
  92.0 1.9 copy-start.1
  93.9 31.5 %copy-start.16 = (f32[1096,128]{1,0:T(8,128)S(1)}, f32[1096,128]{1,0:T(8,128)}, u32[]{:S(2)}) copy-start(f32[1096,128]{1,0:T(8,128)} %get-tuple-element.42) | copy-start | bytes 1683460
  93.9 41.2 %copy-start.13 = (f32[16,64,256]{2,1,0:T(8,128)S(1)}, f32[16,64,256]{2,1,0:T(8,128)}, u32[]{:S(2)}) copy-start(f32[16,64,256]{2,1,0:T(8,128)} %copy-done.12) | copy-start | bytes 3145732
  125.4 13.3 %copy-start.15 = (f32[1096,128]{1,0:T(8,128)S(1)}, f32[1096,128]{1,0:T(8,128)}, u32[]{:S(2)}) copy-start(f32[1096,128]{1,0:T(8,128)} %get-tuple-element.41) | copy-start | bytes 1683460
  125.4 27.8 %collective-permute-start.5 = (f32[1096,128]{1,0:T(8,128)S(1)}, f32[1096,128]{1,0:T(8,128)S(1)}, u32[]{:S(2)}, u32[]{:S(2)}) collective-permute-start(f32[1096,128]{1,0:T(8,128)S(1)} %copy-done.16), channel_id=1, source_target_pairs={{0,2},{1,3},{2,0},{3,1},{4,6},{5,7},{6,4},{7,5},{8,10},{9,11},{10,... | collective-permute-start | bytes 1683464 | tf_op jit(solution)/shard_map/ppermute | solution.py:460
  138.7 18.6 %collective-permute-start.4 = (f32[1096,128]{1,0:T(8,128)S(1)}, f32[1096,128]{1,0:T(8,128)S(1)}, u32[]{:S(2)}, u32[]{:S(2)}) collective-permute-start(f32[1096,128]{1,0:T(8,128)S(1)} %copy-done.15), channel_id=1, source_target_pairs={{0,3},{1,2},{2,1},{3,0},{4,7},{5,6},{6,5},{7,4},{8,11},{9,10},{10,... | collective-permute-start | bytes 1683464 | tf_op jit(solution)/shard_map/ppermute | solution.py:460
  165.6 83.3 %copy-start.2 = (f32[48,128,128]{2,1,0:T(8,128)S(1)}, f32[48,128,128]{2,1,0:T(8,128)}, u32[]{:S(2)}) copy-start(f32[48,128,128]{2,1,0:T(8,128)} %param.10) | copy-start | bytes 9437188
  168.6 47.2 %collective-permute-start.13 = (f32[128,128]{1,0:T(8,128)S(1)}, f32[128,128]{1,0:T(8,128)S(1)}, u32[]{:S(2)}, u32[]{:S(2)}) collective-permute-start(f32[128,128]{1,0:T(8,128)S(1)} %get-tuple-element.52), channel_id=1, source_target_pairs={{0,1},{1,2},{2,3},{3,4},{4,5},{5,6},{6,7},{7,0},{8,9},{9,10},{10,1... | collective-permute-start | bytes 196616 | tf_op jit(solution)/shard_map/ppermute | solution.py:388
  184.4 64.6 %collective-permute-start.14 = (f32[128,128]{1,0:T(8,128)S(1)}, f32[128,128]{1,0:T(8,128)S(1)}, u32[]{:S(2)}, u32[]{:S(2)}) collective-permute-start(f32[128,128]{1,0:T(8,128)S(1)} %get-tuple-element.53), channel_id=1, source_target_pairs={{1,0},{2,1},{3,2},{4,3},{5,4},{6,5},{7,6},{0,7},{9,8},{10,9},{11,1... | collective-permute-start | bytes 196616 | tf_op jit(solution)/shard_map/ppermute | solution.py:389
  204.5 7.0 %collective-permute-start.11 = (f32[32,128]{1,0:T(8,128)S(1)}, f32[32,128]{1,0:T(8,128)S(1)}, u32[]{:S(2)}, u32[]{:S(2)}) collective-permute-start(f32[32,128]{1,0:T(8,128)S(1)} %get-tuple-element.50), channel_id=1, source_target_pairs={{0,8},{8,16},{16,24},{1,9},{9,17},{17,25},{2,10},{10,18},{18,26},{... | collective-permute-start | bytes 49160 | tf_op jit(solution)/shard_map/ppermute | solution.py:386
  210.2 5.6 %collective-permute-start.12 = (f32[32,128]{1,0:T(8,128)S(1)}, f32[32,128]{1,0:T(8,128)S(1)}, u32[]{:S(2)}, u32[]{:S(2)}) collective-permute-start(f32[32,128]{1,0:T(8,128)S(1)} %get-tuple-element.51), channel_id=1, source_target_pairs={{8,0},{16,8},{24,16},{9,1},{17,9},{25,17},{10,2},{18,10},{26,18},{... | collective-permute-start | bytes 49160 | tf_op jit(solution)/shard_map/ppermute | solution.py:387
  256.1 17.3 %collective-permute-start.17 = (f32[128,128]{1,0:T(8,128)S(1)}, f32[128,128]{1,0:T(8,128)S(1)}, u32[]{:S(2)}, u32[]{:S(2)}) collective-permute-start(f32[128,128]{1,0:T(8,128)S(1)} %get-tuple-element.57), channel_id=1, source_target_pairs={{0,1},{1,2},{2,3},{3,4},{4,5},{5,6},{6,7},{7,0},{8,9},{9,10},{10,1... | collective-permute-start | bytes 196616 | tf_op jit(solution)/shard_map/ppermute | solution.py:388
  263.4 10.1 %collective-permute-start.18 = (f32[128,128]{1,0:T(8,128)S(1)}, f32[128,128]{1,0:T(8,128)S(1)}, u32[]{:S(2)}, u32[]{:S(2)}) collective-permute-start(f32[128,128]{1,0:T(8,128)S(1)} %get-tuple-element.58), channel_id=1, source_target_pairs={{1,0},{2,1},{3,2},{4,3},{5,4},{6,5},{7,6},{0,7},{9,8},{10,9},{11,1... | collective-permute-start | bytes 196616 | tf_op jit(solution)/shard_map/ppermute | solution.py:389
  263.4 5.9 %collective-permute-start.15 = (f32[32,128]{1,0:T(8,128)S(1)}, f32[32,128]{1,0:T(8,128)S(1)}, u32[]{:S(2)}, u32[]{:S(2)}) collective-permute-start(f32[32,128]{1,0:T(8,128)S(1)} %get-tuple-element.55), channel_id=1, source_target_pairs={{0,8},{8,16},{16,24},{1,9},{9,17},{17,25},{2,10},{10,18},{18,26},{... | collective-permute-start | bytes 49160 | tf_op jit(solution)/shard_map/ppermute | solution.py:386
  267.8 5.6 %collective-permute-start.16 = (f32[32,128]{1,0:T(8,128)S(1)}, f32[32,128]{1,0:T(8,128)S(1)}, u32[]{:S(2)}, u32[]{:S(2)}) collective-permute-start(f32[32,128]{1,0:T(8,128)S(1)} %get-tuple-element.56), channel_id=1, source_target_pairs={{8,0},{16,8},{24,16},{9,1},{17,9},{25,17},{10,2},{18,10},{26,18},{... | collective-permute-start | bytes 49160 | tf_op jit(solution)/shard_map/ppermute | solution.py:387
  (4 other events, 2.4 us)

commit v2 on v1

--- a/solution.py
+++ b/solution.py
@@ -11,6 +11,9 @@
 RELAX = 0.8
 LANES = 128
 BLOCK = 256
+SPAN = 1024
+SUM_SPAN = 1024
+CUT_BITS = 11
 HEAD = 8
 MIB = 1 << 20
 NT = (((1,), (1,)), ((), ()))
@@ -31,40 +34,46 @@
     return pl.CostEstimate(flops=flops, bytes_accessed=nbytes, transcendentals=0)
 
 
-def rank_kernel(tiles, dest_ref, slot_ref, count_ref, base_ref, place_ref, total_ref):
+def rank_kernel(tiles, cuts, dest_ref, cell_ref, *outs):
+    slot_ref, count_ref, base_ref, place_ref, total_ref = outs
     blocks, block = dest_ref.shape
-    dest = dest_ref[...]
+    keys = dest_ref[...] * cuts + ((cell_ref[...] >> CUT_BITS) & (cuts - 1))
     upper = (iota((block, block), 0) < iota((block, block), 1)).astype(jnp.bfloat16)
     lane = iota((blocks, LANES), 1)
     slot = jnp.zeros((blocks, block), jnp.float32)
     base = jnp.zeros((blocks, 1), jnp.float32)
     counts = jnp.zeros((blocks, LANES), jnp.float32)
     bases = jnp.zeros((blocks, LANES), jnp.float32)
-    for tile in range(tiles):
-        mine = dest == tile
+    for key in range(tiles * cuts):
+        mine = keys == key
         ones = jnp.where(mine, 1.0, 0.0)
         before = lax.dot_general(
             ones.astype(jnp.bfloat16), upper, NN, preferred_element_type=jnp.float32
         )
         slot = slot + jnp.where(mine, before + base, 0.0)
         count = jnp.sum(ones, axis=1, keepdims=True)
-        counts = counts + jnp.where(lane == tile, count, 0.0)
-        bases = bases + jnp.where(lane == tile, base, 0.0)
+        counts = jnp.where(lane == key, count, counts)
+        bases = jnp.where(lane == key, base, bases)
         base = base + count
     lower = (iota((blocks, blocks), 1) < iota((blocks, blocks), 0)).astype(jnp.bfloat16)
     places = lax.dot_general(
         lower, counts.astype(jnp.bfloat16), NN, preferred_element_type=jnp.float32
     )
+    total = jnp.broadcast_to(jnp.sum(counts, axis=0, keepdims=True), (8, LANES))
+    first = jnp.zeros((8, LANES), jnp.float32)
+    for back in range(1, cuts):
+        inside = (iota((8, LANES), 1) & (cuts - 1)) >= back
+        first = first + jnp.where(inside, pltpu.roll(total, back, 1), 0.0)
+    most = jnp.max(counts, axis=1, keepdims=True)
     slot_ref[...] = slot.astype(jnp.int32)
-    count_ref[...] = counts.astype(jnp.int32)
+    count_ref[...] = jnp.where(lane == LANES - 1, most, counts).astype(jnp.int32)
     base_ref[...] = bases.astype(jnp.int32)
-    place_ref[...] = places.astype(jnp.int32)
-    total = jnp.sum(counts, axis=0, keepdims=True).astype(jnp.int32)
-    total_ref[...] = jnp.broadcast_to(total, total_ref.shape)
+    place_ref[...] = (places + first[0:1]).astype(jnp.int32)
+    total_ref[...] = total.astype(jnp.int32)
 
 
 def bucket_kernel(
-    tiles, capacity, width, group, me_ref, count_ref, base_ref, place_ref, total_ref, *refs
+    tiles, cuts, capacity, width, group, me_ref, count_ref, base_ref, place_ref, total_ref, *refs
 ):
     slot_ref, cell_ref, rows_ref = refs[:3]
     outs = refs[3 : 3 + tiles]
@@ -72,7 +81,8 @@
     blocks = slot_ref.shape[0]
     windows = capacity // LANES
     room = capacity + BLOCK
-    chunk = max(8, 512 // tiles)
+    chunk = 32
+    inside = iota((chunk, LANES), 0)
     row_of = iota((BLOCK, BLOCK), 0)
     third = iota((16, BLOCK), 0)
     pad = jnp.zeros((LANES - 2 * width - 16, BLOCK), jnp.bfloat16)
@@ -96,26 +106,34 @@
 
     def spread(at, first):
         block = first + at
-        for tile in range(tiles):
-            count = count_ref[block, tile]
-            source = at * BLOCK + base_ref[block, tile]
-            place = tile * room + place_ref[block, tile]
-            held[pl.ds(place, chunk), :] = staged[pl.ds(source, chunk), :]
-
-            @pl.when(count > chunk)
-            def _more():
-                def step(part, carry):
-                    held[pl.ds(place + part * chunk, chunk), :] = staged[
-                        pl.ds(source + part * chunk, chunk), :
-                    ]
+
+        def move(key, part):
+            count = count_ref[block, key]
+            source = at * BLOCK + base_ref[block, key] + part * chunk
+            place = (key // cuts) * room + place_ref[block, key] + part * chunk
+            pltpu.store(
+                held.at[pl.ds(place, chunk), :],
+                staged[pl.ds(source, chunk), :],
+                mask=inside < count - part * chunk,
+            )
+
+        for key in range(tiles * cuts):
+            move(key, 0)
+
+        @pl.when(count_ref[block, LANES - 1] > chunk)
+        def _more():
+            for key in range(tiles * cuts):
+
+                def step(part, carry, key=key):
+                    move(key, part)
                     return carry
 
-                lax.fori_loop(1, pl.cdiv(count, chunk), step, 0)
+                lax.fori_loop(1, pl.cdiv(count_ref[block, key], chunk), step, 0)
 
         return first
 
     for part in range(blocks // group):
-        lax.fori_loop(0, group, permute, part * group, unroll=2)
+        lax.fori_loop(0, group, permute, part * group, unroll=16)
         lax.fori_loop(0, group, spread, part * group)
 
     row, lane = iota((32, LANES), 0), iota((32, LANES), 1)
@@ -127,78 +145,97 @@
     me = me_ref[0]
     for step in range(tiles):
         tile = me ^ step
-        count = total_ref[0, tile]
+        sizes = [total_ref[0, tile * cuts + cut] for cut in range(cuts)]
+        count = functools.reduce(lambda a, b: a + b, sizes)
         out = outs[step]
 
         def turn(part, carry, tile=tile, count=count, out=out):
-            block = held[pl.ds(pl.multiple_of(tile * room + part * BLOCK, 8), BLOCK), :]
-            both = lax.dot_general(
-                joined, block.astype(jnp.bfloat16), NT, preferred_element_type=jnp.float32
-            )
-            cells = jnp.where(lanes + part * BLOCK < count, both[width : width + 1], -1.0)
-            for side in range(BLOCK // LANES):
-                at = part * (BLOCK // LANES) + side
-                cut = slice(side * LANES, (side + 1) * LANES)
-                out[pl.ds(pl.multiple_of(at * width, width), width), :] = both[:width, cut]
-                out[pl.ds(windows * width + at, 1), :] = cells[:, cut]
+            for piece in range(SPAN // BLOCK):
+                first = part * SPAN + piece * BLOCK
+                block = held[pl.ds(pl.multiple_of(tile * room + first, 8), BLOCK), :]
+                both = lax.dot_general(
+                    joined, block.astype(jnp.bfloat16), NT, preferred_element_type=jnp.float32
+                )
+                cells = jnp.where(lanes + first < count, both[width : width + 1], -1.0)
+                for side in range(BLOCK // LANES):
+                    at = part * (SPAN // LANES) + piece * (BLOCK // LANES) + side
+                    cut = slice(side * LANES, (side + 1) * LANES)
+                    out[pl.ds(pl.multiple_of(at * width, width), width), :] = both[:width, cut]
+                    out[pl.ds(windows * width + at, 1), :] = cells[:, cut]
             return carry
 
-        lax.fori_loop(0, pl.cdiv(count, BLOCK), turn, 0)
-        out[windows * (width + 1) :, :] = jnp.full((HEAD, LANES), count, jnp.int32).astype(
-            jnp.float32
-        )
-
-
-def sum_kernel(width, windows, amount, fresh, *refs):
+        lax.fori_loop(0, pl.cdiv(count, SPAN), turn, 0)
+        line = iota((HEAD, LANES), 0)
+        head = jnp.zeros((HEAD, LANES), jnp.int32)
+        for cut in range(cuts):
+            head = jnp.where(line == cut, sizes[cut], head)
+        out[windows * (width + 1) :, :] = head.astype(jnp.float32)
+
+
+def sum_kernel(width, windows, amount, cuts, fresh, *refs):
     buckets = refs[:amount]
     out = refs[-1]
     half, wide = out.shape[1:]
-    chunk = 2 * LANES
+    high_of = half // cuts
+    chunk = SUM_SPAN
     if fresh:
         out[...] = jnp.zeros_like(out)
     else:
         out[...] = refs[amount][...]
-    row_of = iota((half, chunk), 0)
+    row_of = iota((high_of, chunk), 0)
     col_of = iota((wide, chunk), 0)
+    lanes = iota((1, LANES), 1)
     for bucket in buckets:
-        count = jnp.max(bucket[windows * (width + 1) :, :]).astype(jnp.int32)
-
-        def step(part, carry, bucket=bucket):
-            vals, cells = [], []
-            for side in range(chunk // LANES):
-                at = part * (chunk // LANES) + side
-                vals.append(bucket[pl.ds(pl.multiple_of(at * width, width), width), :])
-                cells.append(bucket[pl.ds(windows * width + at, 1), :])
-            rows = jnp.concatenate(vals, axis=1)
-            cell = jnp.concatenate(cells, axis=1).astype(jnp.int32)
-            grid_row = cell >> 7
-            low_row = jnp.where(cell < 0, -1, grid_row & (half - 1))
-            column = (cell & 127) + jnp.where(grid_row >= half, LANES, 0)
-            high = rows.astype(jnp.bfloat16)
-            low = (rows - high.astype(jnp.float32)).astype(jnp.bfloat16)
-            mine = row_of == low_row
-            onehot = jnp.where(col_of == column, 1.0, 0.0).astype(jnp.bfloat16)
-            left = []
-            for channel in range(width):
-                left.append(
-                    jnp.concatenate(
-                        [
-                            jnp.where(mine, high[channel : channel + 1].astype(jnp.float32), 0.0),
-                            jnp.where(mine, low[channel : channel + 1].astype(jnp.float32), 0.0),
-                        ],
-                        axis=1,
-                    ).astype(jnp.bfloat16)
+        top = windows * (width + 1)
+        sizes = [
+            jnp.max(bucket[top + cut : top + cut + 1, :]).astype(jnp.int32) for cut in range(cuts)
+        ]
+        total = functools.reduce(lambda a, b: a + b, sizes)
+        start = jnp.int32(0)
+        for cut in range(cuts):
+            first = start // LANES
+            start = start + sizes[cut]
+
+            def step(part, carry, bucket=bucket, cut=cut, first=first):
+                vals, cells = [], []
+                for side in range(chunk // LANES):
+                    at = first + part * (chunk // LANES) + side
+                    read = jnp.minimum(at, windows - 1)
+                    vals.append(bucket[pl.ds(pl.multiple_of(read * width, width), width), :])
+                    cell = bucket[pl.ds(windows * width + read, 1), :]
+                    cells.append(jnp.where(at * LANES + lanes < total, cell, -1.0))
+                rows = jnp.concatenate(vals, axis=1)
+                cell = jnp.concatenate(cells, axis=1).astype(jnp.int32)
+                grid_row = cell >> 7
+                low_row = jnp.where(cell < 0, -1, (grid_row & (half - 1)) - cut * high_of)
+                column = (cell & 127) + jnp.where(grid_row >= half, LANES, 0)
+                high = rows.astype(jnp.bfloat16)
+                low = (rows - high.astype(jnp.float32)).astype(jnp.bfloat16)
+                mine = row_of == low_row
+                onehot = jnp.where(col_of == column, 1.0, 0.0).astype(jnp.bfloat16)
+                left = []
+                for channel in range(width):
+                    one = slice(channel, channel + 1)
+                    left.append(
+                        jnp.concatenate(
+                            [
+                                jnp.where(mine, high[one].astype(jnp.float32), 0.0),
+                                jnp.where(mine, low[one].astype(jnp.float32), 0.0),
+                            ],
+                            axis=1,
+                        ).astype(jnp.bfloat16)
+                    )
+                product = lax.dot_general(
+                    jnp.concatenate(left, axis=0),
+                    jnp.concatenate([onehot, onehot], axis=1),
+                    NT,
+                    preferred_element_type=jnp.float32,
                 )
-            product = lax.dot_general(
-                jnp.concatenate(left, axis=0),
-                jnp.concatenate([onehot, onehot], axis=1),
-                NT,
-                preferred_element_type=jnp.float32,
-            )
-            out[...] += product.reshape(out.shape)
-            return carry
-
-        lax.fori_loop(0, pl.cdiv(count, chunk), step, 0)
+                part_of = slice(cut * high_of, (cut + 1) * high_of)
+                out[:, part_of, :] += product.reshape(width, high_of, wide)
+                return carry
+
+            lax.fori_loop(0, pl.cdiv(start - first * LANES, chunk), step, 0)
 
 
 def put_edges(strips, k, rows, r0, last_row, fields):
@@ -355,6 +392,8 @@
     consts = tide_state.shape[0] // 6
     blocks = row_count // BLOCK
     windows = capacity // LANES
+    cuts = max(1, min(4, 32 // tiles))
+    cells = dest_cell.reshape(blocks, BLOCK)
     bucket_rows = windows * (width + 1) + HEAD
     me = lax.axis_index("lon").reshape(1)
 
@@ -410,13 +449,13 @@
 
     table = jax.ShapeDtypeStruct((blocks, LANES), jnp.int32)
     slot, counts, bases, places, totals = pl.pallas_call(
-        functools.partial(rank_kernel, tiles),
-        in_specs=[VMEM],
+        functools.partial(rank_kernel, tiles, cuts),
+        in_specs=[VMEM, VMEM],
         out_specs=[VMEM] * 5,
         out_shape=[jax.ShapeDtypeStruct((blocks, BLOCK), jnp.int32), table, table, table]
         + [jax.ShapeDtypeStruct((8, LANES), jnp.int32)],
         compiler_params=params(32),
-    )(dest_tile.reshape(blocks, BLOCK))
+    )(dest_tile.reshape(blocks, BLOCK), cells)
 
     strips = pl.pallas_call(
         functools.partial(edges_kernel, chunk_rows),
@@ -431,7 +470,7 @@
 
     group = min(32, blocks)
     buckets = pl.pallas_call(
-        functools.partial(bucket_kernel, tiles, capacity, width, group),
+        functools.partial(bucket_kernel, tiles, cuts, capacity, width, group),
         in_specs=[SMEM] * 5 + [VMEM] * 3,
         out_specs=[VMEM] * tiles,
         out_shape=[jax.ShapeDtypeStruct((bucket_rows, LANES), f32)] * tiles,
@@ -441,13 +480,13 @@
         ],
         compiler_params=params(58),
         cost_estimate=cost(10**10, 7 * 10**6),
-    )(me, counts, bases, places, totals, slot, dest_cell.reshape(blocks, BLOCK), residual_rows)
+    )(me, counts, bases, places, totals, slot, cells, residual_rows)
 
     grid_shape = jax.ShapeDtypeStruct((width, height // 2, 2 * across), f32)
 
     def add(parts, total):
         return pl.pallas_call(
-            functools.partial(sum_kernel, width, windows, len(parts), total is None),
+            functools.partial(sum_kernel, width, windows, len(parts), cuts, total is None),
             in_specs=[VMEM] * (len(parts) + (total is not None)),
             out_specs=VMEM,
             out_shape=grid_shape,

time: 281 us -> 197 us (0.70)
  the two profiles are of different devices: /device:TPU:0 before, /device:TPU:11 now
where the time goes in v2:
time: 197 us; the launch traced here: 196 us
  Pallas kernels  72.5 us (37%)
  waiting for transfers between devices  67.6 us (34%)
  starting transfers between devices  45.7 us (23%)
  local copies, waits for them, and re-layouts  7.61 us (4%)
    ppermute x3, waiting for transfers between devices, exchange(): lax.ppermute(east, 'lon', [(i, (i + 1) % tiles) for i in range(tiles)])  45 us
    pallas_call x1, Pallas kernels, local(): pl.pallas_call(functools.partial(bucket_kernel, tiles, cuts, capacity, wi...  29.7 us
    pallas_call x8, Pallas kernels, add(): pl.pallas_call(functools.partial(sum_kernel, width, windows, len(parts),...  18.2 us
    pallas_call x3, Pallas kernels, sweep(): pl.pallas_call(functools.partial(sweep_kernel, chunk_rows, forced, edges)...  17.6 us
    ppermute x3, starting transfers between devices, exchange(): lax.ppermute(east, 'lon', [(i, (i + 1) % tiles) for i in range(tiles)])  16.7 us
    ppermute x7, waiting for transfers between devices, local(): lax.ppermute(buckets[s], 'lon', [(i, i ^ s) for i in range(tiles)])  16.6 us
    ppermute x7, starting transfers between devices, local(): lax.ppermute(buckets[s], 'lon', [(i, i ^ s) for i in range(tiles)])  12.3 us
    ppermute x3, starting transfers between devices, exchange(): lax.ppermute(south, 'lat', [(i, i + 1) for i in range(lats - 1)])  8.83 us
  transfers between devices with their start and end apart: 19, of which 5 were waited for; matrix products, arithmetic and copies ran while one was open for 0% of the time, Pallas kernels for 12%

profile of v2, /device:TPU:11, one launch (start us, length us, event | category | flops | bytes accessed | tf_op | source)
XLA Modules:
  0.0 195.7 jit_solution(9315261656532576390)
XLA Ops:
  8.0 29.7 %shard_map.94 = (f32[1096,128]{1,0:T(8,128)}, f32[1096,128]{1,0:T(8,128)}, f32[1096,128]{1,0:T(8,128)}, f32[1096,128]{1,0:T(8,128)}, f32[1096,128]{1,0:T(8,128)}...) custom-call(s32[1]{0:T(128)} %bitcast.2.me_ref, s32[128,128]{1,0:T(8,128)} %copy-done.9, ...), custom_call_target="tpu_custom_call" | custom-call | flops 10000000000 | bytes 7000000 | tf_op jit(solution)/shard_map/pallas_call | solution.py:472
  37.8 2.3 %collective-permute-start.10 = (f32[1096,128]{1,0:T(8,128)}, f32[1096,128]{1,0:T(8,128)}, u32[]{:S(2)}, u32[]{:S(2)}) collective-permute-start(f32[1096,128]{1,0:T(8,128)} %get-tuple-element.47), channel_id=1, source_target_pairs={{0,4},{1,5},{2,6},{3,7},{4,0},{5,1},{6,2},{7,3},{8,12},{9,13},{10,... | collective-permute-start | bytes 1683464 | tf_op jit(solution)/shard_map/ppermute | solution.py:499
  40.1 2.5 %shard_map.91 = (f32[32,128]{1,0:T(8,128)S(1)}, f32[32,128]{1,0:T(8,128)S(1)}, f32[128,128]{1,0:T(8,128)}, f32[128,128]{1,0:T(8,128)}) custom-call(f32[6,8,128,128]{3,2,1,0:T(8,128)S(1)} %bitcast.5, f32[128,128]{1,0:T(8,128)S(1)} %copy-done.3), custom_call_target="tpu_custom_call" | custom-call | flops 1000000 | bytes 3000000 | tf_op jit(solution)/shard_map/pallas_call | solution.py:460
  43.6 3.1 %collective-permute-start = (f32[32,128]{1,0:T(8,128)S(1)}, f32[32,128]{1,0:T(8,128)S(1)}, u32[]{:S(2)}, u32[]{:S(2)}) collective-permute-start(f32[32,128]{1,0:T(8,128)S(1)} %get-tuple-element.32), channel_id=1, source_target_pairs={{0,8},{8,16},{16,24},{1,9},{9,17},{17,25},{2,10},{10,18},{18,26},{... | collective-permute-start | bytes 49160 | tf_op jit(solution)/shard_map/ppermute | solution.py:425
  46.7 2.2 %collective-permute-start.1 = (f32[32,128]{1,0:T(8,128)S(1)}, f32[32,128]{1,0:T(8,128)S(1)}, u32[]{:S(2)}, u32[]{:S(2)}) collective-permute-start(f32[32,128]{1,0:T(8,128)S(1)} %get-tuple-element.33), channel_id=1, source_target_pairs={{8,0},{16,8},{24,16},{9,1},{17,9},{25,17},{10,2},{18,10},{26,18},{... | collective-permute-start | bytes 49160 | tf_op jit(solution)/shard_map/ppermute | solution.py:426
  48.9 2.1 %shard_map.95.refs_1_ = f32[16,64,256]{2,1,0:T(8,128)S(1)} custom-call(f32[1096,128]{1,0:T(8,128)S(1)} %copy-done.15), custom_call_target="tpu_custom_call" | custom-call | flops 10000000000 | bytes 3000000 | tf_op jit(solution)/shard_map/pallas_call | solution.py:488
  52.1 2.9 %collective-permute-start.9 = (f32[1096,128]{1,0:T(8,128)}, f32[1096,128]{1,0:T(8,128)S(1)}, u32[]{:S(2)}, u32[]{:S(2)}) collective-permute-start(f32[1096,128]{1,0:T(8,128)} %get-tuple-element.46), channel_id=1, source_target_pairs={{0,5},{1,4},{2,7},{3,6},{4,1},{5,0},{6,3},{7,2},{8,13},{9,12},{10,... | collective-permute-start | bytes 1683464 | tf_op jit(solution)/shard_map/ppermute | solution.py:499
  55.0 2.5 %collective-permute-start.8 = (f32[1096,128]{1,0:T(8,128)}, f32[1096,128]{1,0:T(8,128)S(1)}, u32[]{:S(2)}, u32[]{:S(2)}) collective-permute-start(f32[1096,128]{1,0:T(8,128)} %get-tuple-element.45), channel_id=1, source_target_pairs={{0,6},{1,7},{2,4},{3,5},{4,2},{5,3},{6,0},{7,1},{8,14},{9,15},{10,... | collective-permute-start | bytes 1683464 | tf_op jit(solution)/shard_map/ppermute | solution.py:499
  57.5 45.0 %collective-permute-done.2.refs_11_ = f32[128,128]{1,0:T(8,128)S(1)} collective-permute-done((f32[128,128]{1,0:T(8,128)}, f32[128,128]{1,0:T(8,128)S(1)}, u32[]{:S(2)}, u32[]{:S(2)}) %collective-permute-start.2) | collective-permute-done | bytes 65568 | tf_op jit(solution)/shard_map/ppermute | solution.py:427
  102.5 2.4 %collective-permute-start.7 = (f32[1096,128]{1,0:T(8,128)}, f32[1096,128]{1,0:T(8,128)S(1)}, u32[]{:S(2)}, u32[]{:S(2)}) collective-permute-start(f32[1096,128]{1,0:T(8,128)} %get-tuple-element.44), channel_id=1, source_target_pairs={{0,7},{1,6},{2,5},{3,4},{4,3},{5,2},{6,1},{7,0},{8,15},{9,14},{10,... | collective-permute-start | bytes 1683464 | tf_op jit(solution)/shard_map/ppermute | solution.py:499
  106.9 4.5 %shard_map.92.eta_ref.east_ref.north_ref.refs_2_.refs_3_ = f32[6,8,128,128]{3,2,1,0:T(8,128)S(1)} custom-call(f32[8]{0:T(128)S(1)} %copy-done.7, f32[6,8,128,128]{3,2,1,0:T(8,128)S(1)} %bitcast.6, f32[6,8,128,128]{3,2,1,0:T(8,128)S(1)} %bitcast.7, f32[6,8,128,128]{3,2,1,0:T(8,128)S(1)} %bitcast.8, f32[6,8,128,128]{3,2,1,0:T(8,128)S(1)} %bitcast.9, ...), custom_call_target="tpu_custom_call" | custom-call | flops 16000000 | bytes 9000000 | tf_op jit(solution)/shard_map/pallas_call | solution.py:433
  111.6 3.5 %shard_map.96.refs_1_ = f32[16,64,256]{2,1,0:T(8,128)S(1)} custom-call(f32[1096,128]{1,0:T(8,128)} %collective-permute-done.10.refs_0_, f32[16,64,256]{2,1,0:T(8,128)S(1)} %copy-done.14), custom_call_target="tpu_custom_call" | custom-call | flops 10000000000 | bytes 3000000 | tf_op jit(solution)/shard_map/pallas_call | solution.py:488
  115.1 2.1 %collective-permute-start.4 = (f32[1096,128]{1,0:T(8,128)S(1)}, f32[1096,128]{1,0:T(8,128)S(1)}, u32[]{:S(2)}, u32[]{:S(2)}) collective-permute-start(f32[1096,128]{1,0:T(8,128)S(1)} %copy-done.16), channel_id=1, source_target_pairs={{0,3},{1,2},{2,1},{3,0},{4,7},{5,6},{6,5},{7,4},{8,11},{9,10},{10,... | collective-permute-start | bytes 1683464 | tf_op jit(solution)/shard_map/ppermute | solution.py:499
  117.2 2.1 %shard_map.97.refs_1_ = f32[16,64,256]{2,1,0:T(8,128)S(1)} custom-call(f32[1096,128]{1,0:T(8,128)S(1)} %collective-permute-done.9.refs_0_, f32[16,64,256]{2,1,0:T(8,128)S(1)} %shard_map.96.refs_1_), custom_call_target="tpu_custom_call" | custom-call | flops 10000000000 | bytes 3000000 | tf_op jit(solution)/shard_map/pallas_call | solution.py:488
  119.3 7.3 %collective-permute-done.8.refs_0_ = f32[1096,128]{1,0:T(8,128)S(1)} collective-permute-done((f32[1096,128]{1,0:T(8,128)}, f32[1096,128]{1,0:T(8,128)S(1)}, u32[]{:S(2)}, u32[]{:S(2)}) %collective-permute-start.8) | collective-permute-done | bytes 561184 | tf_op jit(solution)/shard_map/ppermute | solution.py:499
  126.6 2.1 %shard_map.98.refs_1_ = f32[16,64,256]{2,1,0:T(8,128)S(1)} custom-call(f32[1096,128]{1,0:T(8,128)S(1)} %collective-permute-done.8.refs_0_, f32[16,64,256]{2,1,0:T(8,128)S(1)} %shard_map.97.refs_1_), custom_call_target="tpu_custom_call" | custom-call | flops 10000000000 | bytes 3000000 | tf_op jit(solution)/shard_map/pallas_call | solution.py:488
  128.8 9.3 %collective-permute-done.7.refs_0_ = f32[1096,128]{1,0:T(8,128)S(1)} collective-permute-done((f32[1096,128]{1,0:T(8,128)}, f32[1096,128]{1,0:T(8,128)S(1)}, u32[]{:S(2)}, u32[]{:S(2)}) %collective-permute-start.7) | collective-permute-done | bytes 561184 | tf_op jit(solution)/shard_map/ppermute | solution.py:499
  138.1 2.1 %shard_map.99.refs_1_ = f32[16,64,256]{2,1,0:T(8,128)S(1)} custom-call(f32[1096,128]{1,0:T(8,128)S(1)} %collective-permute-done.7.refs_0_, f32[16,64,256]{2,1,0:T(8,128)S(1)} %shard_map.98.refs_1_), custom_call_target="tpu_custom_call" | custom-call | flops 10000000000 | bytes 3000000 | tf_op jit(solution)/shard_map/pallas_call | solution.py:488
  140.2 2.1 %shard_map.100.refs_1_ = f32[16,64,256]{2,1,0:T(8,128)S(1)} custom-call(f32[1096,128]{1,0:T(8,128)S(1)} %collective-permute-done.6.refs_0_, f32[16,64,256]{2,1,0:T(8,128)S(1)} %shard_map.99.refs_1_), custom_call_target="tpu_custom_call" | custom-call | flops 10000000000 | bytes 3000000 | tf_op jit(solution)/shard_map/pallas_call | solution.py:488
  142.3 2.1 %shard_map.101.refs_1_ = f32[16,64,256]{2,1,0:T(8,128)S(1)} custom-call(f32[1096,128]{1,0:T(8,128)S(1)} %collective-permute-done.5.refs_0_, f32[16,64,256]{2,1,0:T(8,128)S(1)} %shard_map.100.refs_1_), custom_call_target="tpu_custom_call" | custom-call | flops 10000000000 | bytes 3000000 | tf_op jit(solution)/shard_map/pallas_call | solution.py:488
  144.4 2.1 %shard_map.102.re_ref.im_ref.refs_13_.refs_14_ = f32[16,64,256]{2,1,0:T(8,128)S(1)} custom-call(f32[1096,128]{1,0:T(8,128)S(1)} %collective-permute-done.4.refs_0_, f32[16,64,256]{2,1,0:T(8,128)S(1)} %shard_map.101.refs_1_), custom_call_target="tpu_custom_call" | custom-call | flops 10000000000 | bytes 3000000 | tf_op jit(solution)/shard_map/pallas_call | solution.py:488
  146.5 2.9 %shard_map.103 = (f32[2,8,128,128]{3,2,1,0:T(8,128)S(1)}, f32[32,128]{1,0:T(8,128)S(1)}, f32[32,128]{1,0:T(8,128)S(1)}, f32[128,128]{1,0:T(8,128)S(1)}, f32[128,128]{1,0:T(8,128)S(1)}) custom-call(f32[8]{0:T(128)S(1)} %copy-done.7, f32[6,8,128,128]{3,2,1,0:T(8,128)S(1)} %shard_map.92.eta_ref.east_ref.north_ref.refs_2_.refs_3_, ...), custom_call_target="tpu_custom_call" | custom-call | flops 1000000 | bytes 6000000 | tf_op jit(solution)/shard_map/pallas_call | solution.py:507
  149.5 10.3 %collective-permute-start.13 = (f32[128,128]{1,0:T(8,128)S(1)}, f32[128,128]{1,0:T(8,128)S(1)}, u32[]{:S(2)}, u32[]{:S(2)}) collective-permute-start(f32[128,128]{1,0:T(8,128)S(1)} %get-tuple-element.52), channel_id=1, source_target_pairs={{0,1},{1,2},{2,3},{3,4},{4,5},{5,6},{6,7},{7,0},{8,9},{9,10},{10,1... | collective-permute-start | bytes 196616 | tf_op jit(solution)/shard_map/ppermute | solution.py:427
  159.8 3.1 %collective-permute-start.11 = (f32[32,128]{1,0:T(8,128)S(1)}, f32[32,128]{1,0:T(8,128)S(1)}, u32[]{:S(2)}, u32[]{:S(2)}) collective-permute-start(f32[32,128]{1,0:T(8,128)S(1)} %get-tuple-element.50), channel_id=1, source_target_pairs={{0,8},{8,16},{16,24},{1,9},{9,17},{17,25},{2,10},{10,18},{18,26},{... | collective-permute-start | bytes 49160 | tf_op jit(solution)/shard_map/ppermute | solution.py:425
  163.0 2.1 %collective-permute-start.12 = (f32[32,128]{1,0:T(8,128)S(1)}, f32[32,128]{1,0:T(8,128)S(1)}, u32[]{:S(2)}, u32[]{:S(2)}) collective-permute-start(f32[32,128]{1,0:T(8,128)S(1)} %get-tuple-element.51), channel_id=1, source_target_pairs={{8,0},{16,8},{24,16},{9,1},{17,9},{25,17},{10,2},{18,10},{26,18},{... | collective-permute-start | bytes 49160 | tf_op jit(solution)/shard_map/ppermute | solution.py:426
  165.1 3.2 %collective-permute-done.12.refs_10_ = f32[32,128]{1,0:T(8,128)S(1)} collective-permute-done((f32[32,128]{1,0:T(8,128)S(1)}, f32[32,128]{1,0:T(8,128)S(1)}, u32[]{:S(2)}, u32[]{:S(2)}) %collective-permute-start.12) | collective-permute-done | bytes 16416 | tf_op jit(solution)/shard_map/ppermute | solution.py:426
  168.3 7.2 %shard_map.104 = (f32[6,8,128,128]{3,2,1,0:T(8,128)S(1)}, f32[32,128]{1,0:T(8,128)S(1)}, f32[32,128]{1,0:T(8,128)S(1)}, f32[128,128]{1,0:T(8,128)S(1)}, f32[128,128]{1,0:T(8,128)S(1)}) custom-call(f32[8]{0:T(128)S(1)} %copy-done.7, f32[2,8,128,128]{3,2,1,0:T(8,128)S(1)} %get-tuple-element.49.refs_1_, ...), custom_call_target="tpu_custom_call" | custom-call | flops 16000000 | bytes 9000000 | tf_op jit(solution)/shard_map/pallas_call | solution.py:433
  175.5 6.3 %collective-permute-start.17 = (f32[128,128]{1,0:T(8,128)S(1)}, f32[128,128]{1,0:T(8,128)S(1)}, u32[]{:S(2)}, u32[]{:S(2)}) collective-permute-start(f32[128,128]{1,0:T(8,128)S(1)} %get-tuple-element.57), channel_id=1, source_target_pairs={{0,1},{1,2},{2,3},{3,4},{4,5},{5,6},{6,7},{7,0},{8,9},{9,10},{10,1... | collective-permute-start | bytes 196616 | tf_op jit(solution)/shard_map/ppermute | solution.py:427
  181.9 2.6 %collective-permute-start.15 = (f32[32,128]{1,0:T(8,128)S(1)}, f32[32,128]{1,0:T(8,128)S(1)}, u32[]{:S(2)}, u32[]{:S(2)}) collective-permute-start(f32[32,128]{1,0:T(8,128)S(1)} %get-tuple-element.55), channel_id=1, source_target_pairs={{0,8},{8,16},{16,24},{1,9},{9,17},{17,25},{2,10},{10,18},{18,26},{... | collective-permute-start | bytes 49160 | tf_op jit(solution)/shard_map/ppermute | solution.py:425
  184.5 2.7 %collective-permute-start.16 = (f32[32,128]{1,0:T(8,128)S(1)}, f32[32,128]{1,0:T(8,128)S(1)}, u32[]{:S(2)}, u32[]{:S(2)}) collective-permute-start(f32[32,128]{1,0:T(8,128)S(1)} %get-tuple-element.56), channel_id=1, source_target_pairs={{8,0},{16,8},{24,16},{9,1},{17,9},{25,17},{10,2},{18,10},{26,18},{... | collective-permute-start | bytes 49160 | tf_op jit(solution)/shard_map/ppermute | solution.py:426
  187.2 2.7 %collective-permute-done.16.refs_10_ = f32[32,128]{1,0:T(8,128)S(1)} collective-permute-done((f32[32,128]{1,0:T(8,128)S(1)}, f32[32,128]{1,0:T(8,128)S(1)}, u32[]{:S(2)}, u32[]{:S(2)}) %collective-permute-start.16) | collective-permute-done | bytes 16416 | tf_op jit(solution)/shard_map/ppermute | solution.py:426
  189.9 5.9 %shard_map.105 = f32[6,8,128,128]{3,2,1,0:T(8,128)} custom-call(f32[8]{0:T(128)S(1)} %copy-done.7, f32[6,8,128,128]{3,2,1,0:T(8,128)S(1)} %get-tuple-element.54.refs_1_.refs_2_.refs_3_, f32[6,8,128,128]{3,2,1,0:T(8,128)S(1)} %get-tuple-element.54.refs_1_.refs_2_.refs_3_, f32[6,8,128,128]{3,2,1,0:T(8,128)S(1)} %get-tuple-element.54.refs_1_.refs_2_.refs_3_, ...), custom_call_target="tpu_custom_call" | custom-call | flops 16000000 | bytes 9000000 | tf_op jit(solution)/shard_map/pallas_call | solution.py:433
  (63 shorter events, 12.1 us)
Async XLA Ops:
  0.9 7.1 %copy-start.6 = (s32[128,256]{1,0:T(8,128)}, s32[128,256]{1,0:T(8,128)S(1)}, u32[]{:S(2)}) copy-start(s32[128,256]{1,0:T(8,128)S(1)} %reshape.33.cell_ref.refs_1_) | copy-start | bytes 393220
  8.0 32.1 %copy-start = (f32[48,128,128]{2,1,0:T(8,128)S(1)}, f32[48,128,128]{2,1,0:T(8,128)}, u32[]{:S(2)}) copy-start(f32[48,128,128]{2,1,0:T(8,128)} %param.9) | copy-start | bytes 9437188
  8.0 32.1 %copy-start.3 = (f32[128,128]{1,0:T(8,128)S(1)}, f32[128,128]{1,0:T(8,128)}, u32[]{:S(2)}) copy-start(f32[128,128]{1,0:T(8,128)} %refs_5_.5) | copy-start | bytes 196612
  37.8 11.1 %copy-start.15 = (f32[1096,128]{1,0:T(8,128)S(1)}, f32[1096,128]{1,0:T(8,128)}, u32[]{:S(2)}) copy-start(f32[1096,128]{1,0:T(8,128)} %get-tuple-element.48.refs_0_) | copy-start | bytes 1683460
  37.8 73.7 %collective-permute-start.10 = (f32[1096,128]{1,0:T(8,128)}, f32[1096,128]{1,0:T(8,128)}, u32[]{:S(2)}, u32[]{:S(2)}) collective-permute-start(f32[1096,128]{1,0:T(8,128)} %get-tuple-element.47), channel_id=1, source_target_pairs={{0,4},{1,5},{2,6},{3,7},{4,0},{5,1},{6,2},{7,3},{8,12},{9,13},{10,... | collective-permute-start | bytes 1683464 | tf_op jit(solution)/shard_map/ppermute | solution.py:499
  42.6 59.9 %collective-permute-start.2 = (f32[128,128]{1,0:T(8,128)}, f32[128,128]{1,0:T(8,128)S(1)}, u32[]{:S(2)}, u32[]{:S(2)}) collective-permute-start(f32[128,128]{1,0:T(8,128)} %get-tuple-element.34), channel_id=1, source_target_pairs={{0,1},{1,2},{2,3},{3,4},{4,5},{5,6},{6,7},{7,0},{8,9},{9,10},{10,1... | collective-permute-start | bytes 196616 | tf_op jit(solution)/shard_map/ppermute | solution.py:427
  42.7 62.3 %collective-permute-start.3 = (f32[128,128]{1,0:T(8,128)}, f32[128,128]{1,0:T(8,128)S(1)}, u32[]{:S(2)}, u32[]{:S(2)}) collective-permute-start(f32[128,128]{1,0:T(8,128)} %get-tuple-element.35), channel_id=1, source_target_pairs={{1,0},{2,1},{3,2},{4,3},{5,4},{6,5},{7,6},{0,7},{9,8},{10,9},{11,1... | collective-permute-start | bytes 196616 | tf_op jit(solution)/shard_map/ppermute | solution.py:428
  43.6 8.5 %collective-permute-start = (f32[32,128]{1,0:T(8,128)S(1)}, f32[32,128]{1,0:T(8,128)S(1)}, u32[]{:S(2)}, u32[]{:S(2)}) collective-permute-start(f32[32,128]{1,0:T(8,128)S(1)} %get-tuple-element.32), channel_id=1, source_target_pairs={{0,8},{8,16},{16,24},{1,9},{9,17},{17,25},{2,10},{10,18},{18,26},{... | collective-permute-start | bytes 49160 | tf_op jit(solution)/shard_map/ppermute | solution.py:425
  46.7 8.3 %collective-permute-start.1 = (f32[32,128]{1,0:T(8,128)S(1)}, f32[32,128]{1,0:T(8,128)S(1)}, u32[]{:S(2)}, u32[]{:S(2)}) collective-permute-start(f32[32,128]{1,0:T(8,128)S(1)} %get-tuple-element.33), channel_id=1, source_target_pairs={{8,0},{16,8},{24,16},{9,1},{17,9},{25,17},{10,2},{18,10},{26,18},{... | collective-permute-start | bytes 49160 | tf_op jit(solution)/shard_map/ppermute | solution.py:426
  48.9 56.1 %copy-start.4 = (s32[128,128]{1,0:T(8,128)S(1)}, s32[128,128]{1,0:T(8,128)}, u32[]{:S(2)}) copy-start(s32[128,128]{1,0:T(8,128)} %refs_7_.5) | copy-start | bytes 196612
  48.9 56.1 %copy-start.5 = (f32[128,128]{1,0:T(8,128)S(1)}, f32[128,128]{1,0:T(8,128)}, u32[]{:S(2)}) copy-start(f32[128,128]{1,0:T(8,128)} %refs_6_.5) | copy-start | bytes 196612
  48.9 56.1 %copy-start.7 = (f32[8]{0:T(128)S(1)}, f32[8]{0:T(128)}, u32[]{:S(2)}) copy-start(f32[8]{0:T(128)} %constant.21.clone.refs_0_.omega_ref) | copy-start | bytes 100
  51.1 1.0 copy-start.13
  52.1 63.0 %collective-permute-start.9 = (f32[1096,128]{1,0:T(8,128)}, f32[1096,128]{1,0:T(8,128)S(1)}, u32[]{:S(2)}, u32[]{:S(2)}) collective-permute-start(f32[1096,128]{1,0:T(8,128)} %get-tuple-element.46), channel_id=1, source_target_pairs={{0,5},{1,4},{2,7},{3,6},{4,1},{5,0},{6,3},{7,2},{8,13},{9,12},{10,... | collective-permute-start | bytes 1683464 | tf_op jit(solution)/shard_map/ppermute | solution.py:499
  55.0 71.6 %collective-permute-start.8 = (f32[1096,128]{1,0:T(8,128)}, f32[1096,128]{1,0:T(8,128)S(1)}, u32[]{:S(2)}, u32[]{:S(2)}) collective-permute-start(f32[1096,128]{1,0:T(8,128)} %get-tuple-element.45), channel_id=1, source_target_pairs={{0,6},{1,7},{2,4},{3,5},{4,2},{5,3},{6,0},{7,1},{8,14},{9,15},{10,... | collective-permute-start | bytes 1683464 | tf_op jit(solution)/shard_map/ppermute | solution.py:499
  102.5 35.5 %collective-permute-start.7 = (f32[1096,128]{1,0:T(8,128)}, f32[1096,128]{1,0:T(8,128)S(1)}, u32[]{:S(2)}, u32[]{:S(2)}) collective-permute-start(f32[1096,128]{1,0:T(8,128)} %get-tuple-element.44), channel_id=1, source_target_pairs={{0,7},{1,6},{2,5},{3,4},{4,3},{5,2},{6,1},{7,0},{8,15},{9,14},{10,... | collective-permute-start | bytes 1683464 | tf_op jit(solution)/shard_map/ppermute | solution.py:499
  104.9 35.3 %collective-permute-start.6 = (f32[1096,128]{1,0:T(8,128)}, f32[1096,128]{1,0:T(8,128)S(1)}, u32[]{:S(2)}, u32[]{:S(2)}) collective-permute-start(f32[1096,128]{1,0:T(8,128)} %get-tuple-element.43), channel_id=1, source_target_pairs={{0,1},{1,0},{2,3},{3,2},{4,5},{5,4},{6,7},{7,6},{8,9},{9,8},{10,11... | collective-permute-start | bytes 1683464 | tf_op jit(solution)/shard_map/ppermute | solution.py:499
  105.0 1.9 copy-start.1
  106.9 4.6 %copy-start.17 = (f32[1096,128]{1,0:T(8,128)S(1)}, f32[1096,128]{1,0:T(8,128)}, u32[]{:S(2)}) copy-start(f32[1096,128]{1,0:T(8,128)} %get-tuple-element.42) | copy-start | bytes 1683460
  106.9 4.7 %copy-start.14 = (f32[16,64,256]{2,1,0:T(8,128)S(1)}, f32[16,64,256]{2,1,0:T(8,128)}, u32[]{:S(2)}) copy-start(f32[16,64,256]{2,1,0:T(8,128)} %copy-done.13) | copy-start | bytes 3145732
  111.5 3.6 %copy-start.16 = (f32[1096,128]{1,0:T(8,128)S(1)}, f32[1096,128]{1,0:T(8,128)}, u32[]{:S(2)}) copy-start(f32[1096,128]{1,0:T(8,128)} %get-tuple-element.41) | copy-start | bytes 1683460
  111.5 30.8 %collective-permute-start.5 = (f32[1096,128]{1,0:T(8,128)S(1)}, f32[1096,128]{1,0:T(8,128)S(1)}, u32[]{:S(2)}, u32[]{:S(2)}) collective-permute-start(f32[1096,128]{1,0:T(8,128)S(1)} %copy-done.17), channel_id=1, source_target_pairs={{0,2},{1,3},{2,0},{3,1},{4,6},{5,7},{6,4},{7,5},{8,10},{9,11},{10,... | collective-permute-start | bytes 1683464 | tf_op jit(solution)/shard_map/ppermute | solution.py:499
  115.1 29.3 %collective-permute-start.4 = (f32[1096,128]{1,0:T(8,128)S(1)}, f32[1096,128]{1,0:T(8,128)S(1)}, u32[]{:S(2)}, u32[]{:S(2)}) collective-permute-start(f32[1096,128]{1,0:T(8,128)S(1)} %copy-done.16), channel_id=1, source_target_pairs={{0,3},{1,2},{2,1},{3,0},{4,7},{5,6},{6,5},{7,4},{8,11},{9,10},{10,... | collective-permute-start | bytes 1683464 | tf_op jit(solution)/shard_map/ppermute | solution.py:499
  146.5 21.8 %copy-start.2 = (f32[48,128,128]{2,1,0:T(8,128)S(1)}, f32[48,128,128]{2,1,0:T(8,128)}, u32[]{:S(2)}) copy-start(f32[48,128,128]{2,1,0:T(8,128)} %param.10) | copy-start | bytes 9437188
  149.5 18.8 %collective-permute-start.13 = (f32[128,128]{1,0:T(8,128)S(1)}, f32[128,128]{1,0:T(8,128)S(1)}, u32[]{:S(2)}, u32[]{:S(2)}) collective-permute-start(f32[128,128]{1,0:T(8,128)S(1)} %get-tuple-element.52), channel_id=1, source_target_pairs={{0,1},{1,2},{2,3},{3,4},{4,5},{5,6},{6,7},{7,0},{8,9},{9,10},{10,1... | collective-permute-start | bytes 196616 | tf_op jit(solution)/shard_map/ppermute | solution.py:427
  159.8 8.5 %collective-permute-start.14 = (f32[128,128]{1,0:T(8,128)S(1)}, f32[128,128]{1,0:T(8,128)S(1)}, u32[]{:S(2)}, u32[]{:S(2)}) collective-permute-start(f32[128,128]{1,0:T(8,128)S(1)} %get-tuple-element.53), channel_id=1, source_target_pairs={{1,0},{2,1},{3,2},{4,3},{5,4},{6,5},{7,6},{0,7},{9,8},{10,9},{11,1... | collective-permute-start | bytes 196616 | tf_op jit(solution)/shard_map/ppermute | solution.py:428
  159.8 5.3 %collective-permute-start.11 = (f32[32,128]{1,0:T(8,128)S(1)}, f32[32,128]{1,0:T(8,128)S(1)}, u32[]{:S(2)}, u32[]{:S(2)}) collective-permute-start(f32[32,128]{1,0:T(8,128)S(1)} %get-tuple-element.50), channel_id=1, source_target_pairs={{0,8},{8,16},{16,24},{1,9},{9,17},{17,25},{2,10},{10,18},{18,26},{... | collective-permute-start | bytes 49160 | tf_op jit(solution)/shard_map/ppermute | solution.py:425
  163.0 5.4 %collective-permute-start.12 = (f32[32,128]{1,0:T(8,128)S(1)}, f32[32,128]{1,0:T(8,128)S(1)}, u32[]{:S(2)}, u32[]{:S(2)}) collective-permute-start(f32[32,128]{1,0:T(8,128)S(1)} %get-tuple-element.51), channel_id=1, source_target_pairs={{8,0},{16,8},{24,16},{9,1},{17,9},{25,17},{10,2},{18,10},{26,18},{... | collective-permute-start | bytes 49160 | tf_op jit(solution)/shard_map/ppermute | solution.py:426
  175.5 14.3 %collective-permute-start.17 = (f32[128,128]{1,0:T(8,128)S(1)}, f32[128,128]{1,0:T(8,128)S(1)}, u32[]{:S(2)}, u32[]{:S(2)}) collective-permute-start(f32[128,128]{1,0:T(8,128)S(1)} %get-tuple-element.57), channel_id=1, source_target_pairs={{0,1},{1,2},{2,3},{3,4},{4,5},{5,6},{6,7},{7,0},{8,9},{9,10},{10,1... | collective-permute-start | bytes 196616 | tf_op jit(solution)/shard_map/ppermute | solution.py:427
  181.9 8.0 %collective-permute-start.18 = (f32[128,128]{1,0:T(8,128)S(1)}, f32[128,128]{1,0:T(8,128)S(1)}, u32[]{:S(2)}, u32[]{:S(2)}) collective-permute-start(f32[128,128]{1,0:T(8,128)S(1)} %get-tuple-element.58), channel_id=1, source_target_pairs={{1,0},{2,1},{3,2},{4,3},{5,4},{6,5},{7,6},{0,7},{9,8},{10,9},{11,1... | collective-permute-start | bytes 196616 | tf_op jit(solution)/shard_map/ppermute | solution.py:428
  181.9 5.3 %collective-permute-start.15 = (f32[32,128]{1,0:T(8,128)S(1)}, f32[32,128]{1,0:T(8,128)S(1)}, u32[]{:S(2)}, u32[]{:S(2)}) collective-permute-start(f32[32,128]{1,0:T(8,128)S(1)} %get-tuple-element.55), channel_id=1, source_target_pairs={{0,8},{8,16},{16,24},{1,9},{9,17},{17,25},{2,10},{10,18},{18,26},{... | collective-permute-start | bytes 49160 | tf_op jit(solution)/shard_map/ppermute | solution.py:425
  184.5 5.4 %collective-permute-start.16 = (f32[32,128]{1,0:T(8,128)S(1)}, f32[32,128]{1,0:T(8,128)S(1)}, u32[]{:S(2)}, u32[]{:S(2)}) collective-permute-start(f32[32,128]{1,0:T(8,128)S(1)} %get-tuple-element.56), channel_id=1, source_target_pairs={{8,0},{16,8},{24,16},{9,1},{17,9},{25,17},{10,2},{18,10},{26,18},{... | collective-permute-start | bytes 49160 | tf_op jit(solution)/shard_map/ppermute | solution.py:426
  (5 other events, 3.1 us)

commit v3 on v2

--- a/solution.py
+++ b/solution.py
@@ -11,7 +11,7 @@
 RELAX = 0.8
 LANES = 128
 BLOCK = 256
-SPAN = 1024
+SPAN = 2048
 SUM_SPAN = 1024
 CUT_BITS = 11
 HEAD = 8
@@ -20,6 +20,7 @@
 NN = (((1,), (0,)), ((), ()))
 VMEM = pl.BlockSpec(memory_space=pltpu.VMEM)
 SMEM = pl.BlockSpec(memory_space=pltpu.SMEM)
+ANY = pl.BlockSpec(memory_space=pl.ANY)
 
 
 def iota(shape, dim):
@@ -35,9 +36,16 @@
 
 
 def rank_kernel(tiles, cuts, dest_ref, cell_ref, *outs):
-    slot_ref, count_ref, base_ref, place_ref, total_ref = outs
-    blocks, block = dest_ref.shape
-    keys = dest_ref[...] * cuts + ((cell_ref[...] >> CUT_BITS) & (cuts - 1))
+    slot_ref, table_ref = outs
+    blocks, block = dest_ref.shape[0] // 2, BLOCK
+
+    def lines(ref):
+        return jnp.concatenate(
+            [ref[pl.ds(side, blocks, stride=2), :] for side in range(2)], axis=1
+        )
+
+    tile = lines(dest_ref) ^ lax.axis_index("lon")
+    keys = tile * cuts + ((lines(cell_ref) >> CUT_BITS) & (cuts - 1))
     upper = (iota((block, block), 0) < iota((block, block), 1)).astype(jnp.bfloat16)
     lane = iota((blocks, LANES), 1)
     slot = jnp.zeros((blocks, block), jnp.float32)
@@ -66,18 +74,17 @@
         first = first + jnp.where(inside, pltpu.roll(total, back, 1), 0.0)
     most = jnp.max(counts, axis=1, keepdims=True)
     slot_ref[...] = slot.astype(jnp.int32)
-    count_ref[...] = jnp.where(lane == LANES - 1, most, counts).astype(jnp.int32)
-    base_ref[...] = bases.astype(jnp.int32)
-    place_ref[...] = (places + first[0:1]).astype(jnp.int32)
-    total_ref[...] = total.astype(jnp.int32)
-
-
-def bucket_kernel(
-    tiles, cuts, capacity, width, group, me_ref, count_ref, base_ref, place_ref, total_ref, *refs
-):
-    slot_ref, cell_ref, rows_ref = refs[:3]
+    table_ref[:blocks, :] = jnp.where(lane == LANES - 1, most, counts).astype(jnp.int32)
+    table_ref[blocks : 2 * blocks, :] = bases.astype(jnp.int32)
+    table_ref[2 * blocks : 3 * blocks, :] = (places + first[0:1]).astype(jnp.int32)
+    table_ref[3 * blocks :, :] = total.astype(jnp.int32)
+
+
+def bucket_kernel(tiles, cuts, capacity, width, group, table_ref, *refs):
+    slot_ref, cell_ref, rows_any = refs[:3]
     outs = refs[3 : 3 + tiles]
-    staged, held = refs[3 + tiles :]
+    staged, held, turned, rows_ref, read_sem, write_sem = refs[3 + tiles :]
+    keys = tiles * cuts
     blocks = slot_ref.shape[0]
     windows = capacity // LANES
     room = capacity + BLOCK
@@ -90,7 +97,9 @@
     def permute(at, first):
         block = first + at
         slot = slot_ref[pl.ds(block, 1), :]
-        cell = cell_ref[pl.ds(block, 1), :]
+        cell = jnp.concatenate(
+            [cell_ref[pl.ds(2 * block + side, 1), :] for side in range(2)], axis=1
+        )
         rows = rows_ref[:, pl.ds(pl.multiple_of(block * BLOCK, BLOCK), BLOCK)]
         high = rows.astype(jnp.bfloat16)
         low = (rows - high.astype(jnp.float32)).astype(jnp.bfloat16)
@@ -104,37 +113,52 @@
         )
         return first
 
+    def move(at, block, key, part):
+        count = table_ref[block, key]
+        source = at * BLOCK + table_ref[blocks + block, key] + part * chunk
+        place = (key // cuts) * room + table_ref[2 * blocks + block, key] + part * chunk
+        pltpu.store(
+            held.at[pl.ds(place, chunk), :],
+            staged[pl.ds(source, chunk), :],
+            mask=inside < count - part * chunk,
+        )
+
     def spread(at, first):
+        for key in range(keys):
+            move(at, first + at, key, 0)
+        return first
+
+    def spread_rest(at, first):
         block = first + at
 
-        def move(key, part):
-            count = count_ref[block, key]
-            source = at * BLOCK + base_ref[block, key] + part * chunk
-            place = (key // cuts) * room + place_ref[block, key] + part * chunk
-            pltpu.store(
-                held.at[pl.ds(place, chunk), :],
-                staged[pl.ds(source, chunk), :],
-                mask=inside < count - part * chunk,
-            )
-
-        for key in range(tiles * cuts):
-            move(key, 0)
-
-        @pl.when(count_ref[block, LANES - 1] > chunk)
+        @pl.when(table_ref[block, LANES - 1] > chunk)
         def _more():
-            for key in range(tiles * cuts):
+            for key in range(keys):
 
                 def step(part, carry, key=key):
-                    move(key, part)
+                    move(at, block, key, part)
                     return carry
 
-                lax.fori_loop(1, pl.cdiv(count_ref[block, key], chunk), step, 0)
+                lax.fori_loop(1, pl.cdiv(table_ref[block, key], chunk), step, 0)
 
         return first
 
+    span = group * BLOCK
+    reads = [
+        pltpu.make_async_copy(
+            rows_any.at[:, part * span : (part + 1) * span],
+            rows_ref.at[:, part * span : (part + 1) * span],
+            read_sem.at[part],
+        )
+        for part in range(blocks // group)
+    ]
+    for read in reads:
+        read.start()
     for part in range(blocks // group):
+        reads[part].wait()
         lax.fori_loop(0, group, permute, part * group, unroll=16)
-        lax.fori_loop(0, group, spread, part * group)
+        lax.fori_loop(0, group, spread, part * group, unroll=4)
+        lax.fori_loop(0, group, spread_rest, part * group)
 
     row, lane = iota((32, LANES), 0), iota((32, LANES), 1)
     joined = jnp.where((row < width) & ((lane == row) | (lane == row + width)), 1.0, 0.0)
@@ -142,12 +166,11 @@
     joined = joined + jnp.where((row == width) & (lane == 2 * width + 1), 1.0, 0.0)
     joined = joined.astype(jnp.bfloat16)
     lanes = iota((1, BLOCK), 1)
-    me = me_ref[0]
-    for step in range(tiles):
-        tile = me ^ step
-        sizes = [total_ref[0, tile * cuts + cut] for cut in range(cuts)]
+    writes = []
+    for tile in range(tiles):
+        out = turned.at[tile]
+        sizes = [table_ref[3 * blocks, tile * cuts + cut] for cut in range(cuts)]
         count = functools.reduce(lambda a, b: a + b, sizes)
-        out = outs[step]
 
         def turn(part, carry, tile=tile, count=count, out=out):
             for piece in range(SPAN // BLOCK):
@@ -170,6 +193,10 @@
         for cut in range(cuts):
             head = jnp.where(line == cut, sizes[cut], head)
         out[windows * (width + 1) :, :] = head.astype(jnp.float32)
+        writes.append(pltpu.make_async_copy(out, outs[tile], write_sem.at[tile]))
+        writes[-1].start()
+    for write in writes:
+        write.wait()
 
 
 def sum_kernel(width, windows, amount, cuts, fresh, *refs):
@@ -393,9 +420,8 @@
     blocks = row_count // BLOCK
     windows = capacity // LANES
     cuts = max(1, min(4, 32 // tiles))
-    cells = dest_cell.reshape(blocks, BLOCK)
+    cells = dest_cell.reshape(2 * blocks, LANES)
     bucket_rows = windows * (width + 1) + HEAD
-    me = lax.axis_index("lon").reshape(1)
 
     omega = jnp.asarray(OMEGAS, f32)
     row_ids = lax.axis_index("lat") * height + jnp.arange(height, dtype=jnp.int32)
@@ -447,15 +473,16 @@
         )
         return out[0], out[1:]
 
-    table = jax.ShapeDtypeStruct((blocks, LANES), jnp.int32)
-    slot, counts, bases, places, totals = pl.pallas_call(
+    slot, table = pl.pallas_call(
         functools.partial(rank_kernel, tiles, cuts),
         in_specs=[VMEM, VMEM],
-        out_specs=[VMEM] * 5,
-        out_shape=[jax.ShapeDtypeStruct((blocks, BLOCK), jnp.int32), table, table, table]
-        + [jax.ShapeDtypeStruct((8, LANES), jnp.int32)],
+        out_specs=[VMEM] * 2,
+        out_shape=[
+            jax.ShapeDtypeStruct((blocks, BLOCK), jnp.int32),
+            jax.ShapeDtypeStruct((3 * blocks + 8, LANES), jnp.int32),
+        ],
         compiler_params=params(32),
-    )(dest_tile.reshape(blocks, BLOCK), cells)
+    )(dest_tile.reshape(2 * blocks, LANES), cells)
 
     strips = pl.pallas_call(
         functools.partial(edges_kernel, chunk_rows),
@@ -469,18 +496,23 @@
     strips = exchange(strips)
 
     group = min(32, blocks)
+
     buckets = pl.pallas_call(
         functools.partial(bucket_kernel, tiles, cuts, capacity, width, group),
-        in_specs=[SMEM] * 5 + [VMEM] * 3,
-        out_specs=[VMEM] * tiles,
+        in_specs=[SMEM, VMEM, VMEM, ANY],
+        out_specs=[ANY] * tiles,
         out_shape=[jax.ShapeDtypeStruct((bucket_rows, LANES), f32)] * tiles,
         scratch_shapes=[
             pltpu.VMEM(((group + 1) * BLOCK, LANES), f32),
             pltpu.VMEM((tiles * (capacity + BLOCK), LANES), f32),
+            pltpu.VMEM((tiles, bucket_rows, LANES), f32),
+            pltpu.VMEM((width, row_count), f32),
+            pltpu.SemaphoreType.DMA((blocks // group,)),
+            pltpu.SemaphoreType.DMA((tiles,)),
         ],
-        compiler_params=params(58),
+        compiler_params=params(60),
         cost_estimate=cost(10**10, 7 * 10**6),
-    )(me, counts, bases, places, totals, slot, cells, residual_rows)
+    )(table, slot, cells, residual_rows)
 
     grid_shape = jax.ShapeDtypeStruct((width, height // 2, 2 * across), f32)
 

time: 197 us -> 196 us (level)
  the two profiles are of different devices: /device:TPU:11 before, /device:TPU:10 now
where the time goes in v3:
time: 196 us; the launch traced here: 195 us
  Pallas kernels  95.9 us (49%)
  starting transfers between devices  74.6 us (38%)
  waiting for transfers between devices  17.8 us (9%)
  local copies, waits for them, and re-layouts  6.13 us (3%)
    ppermute x7, starting transfers between devices, local(): lax.ppermute(buckets[s], 'lon', [(i, i ^ s) for i in range(tiles)])  51.8 us
    pallas_call x8, Pallas kernels, add(): pl.pallas_call(functools.partial(sum_kernel, width, windows, len(parts),...  42.7 us
    pallas_call x1, Pallas kernels, local(): pl.pallas_call(functools.partial(bucket_kernel, tiles, cuts, capacity, wi...  28.8 us
    pallas_call x3, Pallas kernels, sweep(): pl.pallas_call(functools.partial(sweep_kernel, chunk_rows, forced, edges)...  17.5 us
    ppermute x3, starting transfers between devices, exchange(): lax.ppermute(south, 'lat', [(i, i + 1) for i in range(lats - 1)])  10.5 us
    ppermute x7, waiting for transfers between devices, local(): lax.ppermute(buckets[s], 'lon', [(i, i ^ s) for i in range(tiles)])  9.27 us
    ppermute x3, waiting for transfers between devices, exchange(): lax.ppermute(north, 'lat', [(i + 1, i) for i in range(lats - 1)])  8.49 us
    ppermute x3, starting transfers between devices, exchange(): lax.ppermute(north, 'lat', [(i + 1, i) for i in range(lats - 1)])  6.98 us
  transfers between devices with their start and end apart: 19, of which 4 were waited for; matrix products, arithmetic and copies ran while one was open for 0% of the time, Pallas kernels for 23%

profile of v3, /device:TPU:10, one launch (start us, length us, event | category | flops | bytes accessed | tf_op | source)
XLA Modules:
  0.0 195.0 jit_solution(6257707558818802588)
XLA Ops:
  1.8 1.5 shard_map.93
  4.7 28.8 %shard_map.94 = (f32[1096,128]{1,0:T(8,128)}, f32[1096,128]{1,0:T(8,128)}, f32[1096,128]{1,0:T(8,128)}, f32[1096,128]{1,0:T(8,128)}, f32[1096,128]{1,0:T(8,128)}...) custom-call(s32[392,128]{1,0:T(8,128)} %copy-done.9, s32[128,256]{1,0:T(8,128)} %copy-done.10, ...), custom_call_target="tpu_custom_call" | custom-call | flops 10000000000 | bytes 7000000 | tf_op jit(solution)/shard_map/pallas_call | solution.py:500
  33.5 2.9 %collective-permute-start.10 = (f32[1096,128]{1,0:T(8,128)}, f32[1096,128]{1,0:T(8,128)}, u32[]{:S(2)}, u32[]{:S(2)}) collective-permute-start(f32[1096,128]{1,0:T(8,128)} %get-tuple-element.41), channel_id=1, source_target_pairs={{0,4},{1,5},{2,6},{3,7},{4,0},{5,1},{6,2},{7,3},{8,12},{9,13},{10,... | collective-permute-start | bytes 1683464 | tf_op jit(solution)/shard_map/ppermute | solution.py:531
  36.4 2.5 %shard_map.91 = (f32[32,128]{1,0:T(8,128)S(1)}, f32[32,128]{1,0:T(8,128)S(1)}, f32[128,128]{1,0:T(8,128)}, f32[128,128]{1,0:T(8,128)}) custom-call(f32[6,8,128,128]{3,2,1,0:T(8,128)S(1)} %bitcast.5, f32[128,128]{1,0:T(8,128)S(1)} %copy-done.3), custom_call_target="tpu_custom_call" | custom-call | flops 1000000 | bytes 3000000 | tf_op jit(solution)/shard_map/pallas_call | solution.py:487
  39.0 1.7 collective-permute-start.3
  40.7 3.4 %collective-permute-start = (f32[32,128]{1,0:T(8,128)S(1)}, f32[32,128]{1,0:T(8,128)S(1)}, u32[]{:S(2)}, u32[]{:S(2)}) collective-permute-start(f32[32,128]{1,0:T(8,128)S(1)} %get-tuple-element.29), channel_id=1, source_target_pairs={{0,8},{8,16},{16,24},{1,9},{9,17},{17,25},{2,10},{10,18},{18,26},{... | collective-permute-start | bytes 49160 | tf_op jit(solution)/shard_map/ppermute | solution.py:451
  44.1 2.4 %collective-permute-start.1 = (f32[32,128]{1,0:T(8,128)S(1)}, f32[32,128]{1,0:T(8,128)S(1)}, u32[]{:S(2)}, u32[]{:S(2)}) collective-permute-start(f32[32,128]{1,0:T(8,128)S(1)} %get-tuple-element.30), channel_id=1, source_target_pairs={{8,0},{16,8},{24,16},{9,1},{17,9},{25,17},{10,2},{18,10},{26,18},{... | collective-permute-start | bytes 49160 | tf_op jit(solution)/shard_map/ppermute | solution.py:452
  46.6 4.7 %shard_map.95.refs_1_ = f32[16,64,256]{2,1,0:T(8,128)S(1)} custom-call(f32[1096,128]{1,0:T(8,128)S(1)} %copy-done.13), custom_call_target="tpu_custom_call" | custom-call | flops 10000000000 | bytes 3000000 | tf_op jit(solution)/shard_map/pallas_call | solution.py:520
  52.6 1.3 collective-permute-start.7
  53.8 47.3 %collective-permute-start.6 = (f32[1096,128]{1,0:T(8,128)}, f32[1096,128]{1,0:T(8,128)S(1)}, u32[]{:S(2)}, u32[]{:S(2)}) collective-permute-start(f32[1096,128]{1,0:T(8,128)} %get-tuple-element.37), channel_id=1, source_target_pairs={{0,1},{1,0},{2,3},{3,2},{4,5},{5,4},{6,7},{7,6},{8,9},{9,8},{10,11... | collective-permute-start | bytes 1683464 | tf_op jit(solution)/shard_map/ppermute | solution.py:531
  101.3 1.9 copy-done.1
  103.2 4.5 %shard_map.92.eta_ref.east_ref.north_ref.refs_2_.refs_3_ = f32[6,8,128,128]{3,2,1,0:T(8,128)S(1)} custom-call(f32[8]{0:T(128)S(1)} %copy-done.8, f32[6,8,128,128]{3,2,1,0:T(8,128)S(1)} %bitcast.6, f32[6,8,128,128]{3,2,1,0:T(8,128)S(1)} %bitcast.7, f32[6,8,128,128]{3,2,1,0:T(8,128)S(1)} %bitcast.8, f32[6,8,128,128]{3,2,1,0:T(8,128)S(1)} %bitcast.9, ...), custom_call_target="tpu_custom_call" | custom-call | flops 16000000 | bytes 9000000 | tf_op jit(solution)/shard_map/pallas_call | solution.py:459
  107.8 6.7 %shard_map.96.refs_1_ = f32[16,64,256]{2,1,0:T(8,128)S(1)} custom-call(f32[1096,128]{1,0:T(8,128)} %collective-permute-done.10.refs_0_, f32[16,64,256]{2,1,0:T(8,128)S(1)} %copy-done.12), custom_call_target="tpu_custom_call" | custom-call | flops 10000000000 | bytes 3000000 | tf_op jit(solution)/shard_map/pallas_call | solution.py:520
  114.6 5.0 %shard_map.97.refs_1_ = f32[16,64,256]{2,1,0:T(8,128)S(1)} custom-call(f32[1096,128]{1,0:T(8,128)S(1)} %collective-permute-done.9.refs_0_, f32[16,64,256]{2,1,0:T(8,128)S(1)} %shard_map.96.refs_1_), custom_call_target="tpu_custom_call" | custom-call | flops 10000000000 | bytes 3000000 | tf_op jit(solution)/shard_map/pallas_call | solution.py:520
  119.6 4.2 %collective-permute-done.8.refs_0_ = f32[1096,128]{1,0:T(8,128)S(1)} collective-permute-done((f32[1096,128]{1,0:T(8,128)}, f32[1096,128]{1,0:T(8,128)S(1)}, u32[]{:S(2)}, u32[]{:S(2)}) %collective-permute-start.8) | collective-permute-done | bytes 561184 | tf_op jit(solution)/shard_map/ppermute | solution.py:531
  123.8 5.0 %shard_map.98.refs_1_ = f32[16,64,256]{2,1,0:T(8,128)S(1)} custom-call(f32[1096,128]{1,0:T(8,128)S(1)} %collective-permute-done.8.refs_0_, f32[16,64,256]{2,1,0:T(8,128)S(1)} %shard_map.97.refs_1_), custom_call_target="tpu_custom_call" | custom-call | flops 10000000000 | bytes 3000000 | tf_op jit(solution)/shard_map/pallas_call | solution.py:520
  128.8 5.1 %collective-permute-done.7.refs_0_ = f32[1096,128]{1,0:T(8,128)S(1)} collective-permute-done((f32[1096,128]{1,0:T(8,128)}, f32[1096,128]{1,0:T(8,128)S(1)}, u32[]{:S(2)}, u32[]{:S(2)}) %collective-permute-start.7) | collective-permute-done | bytes 561184 | tf_op jit(solution)/shard_map/ppermute | solution.py:531
  133.9 5.5 %shard_map.99.refs_1_ = f32[16,64,256]{2,1,0:T(8,128)S(1)} custom-call(f32[1096,128]{1,0:T(8,128)S(1)} %collective-permute-done.7.refs_0_, f32[16,64,256]{2,1,0:T(8,128)S(1)} %shard_map.98.refs_1_), custom_call_target="tpu_custom_call" | custom-call | flops 10000000000 | bytes 3000000 | tf_op jit(solution)/shard_map/pallas_call | solution.py:520
  139.5 5.1 %shard_map.100.refs_1_ = f32[16,64,256]{2,1,0:T(8,128)S(1)} custom-call(f32[1096,128]{1,0:T(8,128)S(1)} %collective-permute-done.6.refs_0_, f32[16,64,256]{2,1,0:T(8,128)S(1)} %shard_map.99.refs_1_), custom_call_target="tpu_custom_call" | custom-call | flops 10000000000 | bytes 3000000 | tf_op jit(solution)/shard_map/pallas_call | solution.py:520
  144.5 5.1 %shard_map.101.refs_1_ = f32[16,64,256]{2,1,0:T(8,128)S(1)} custom-call(f32[1096,128]{1,0:T(8,128)S(1)} %collective-permute-done.5.refs_0_, f32[16,64,256]{2,1,0:T(8,128)S(1)} %shard_map.100.refs_1_), custom_call_target="tpu_custom_call" | custom-call | flops 10000000000 | bytes 3000000 | tf_op jit(solution)/shard_map/pallas_call | solution.py:520
  149.6 5.5 %shard_map.102.re_ref.im_ref.refs_13_.refs_14_ = f32[16,64,256]{2,1,0:T(8,128)S(1)} custom-call(f32[1096,128]{1,0:T(8,128)S(1)} %collective-permute-done.4.refs_0_, f32[16,64,256]{2,1,0:T(8,128)S(1)} %shard_map.101.refs_1_), custom_call_target="tpu_custom_call" | custom-call | flops 10000000000 | bytes 3000000 | tf_op jit(solution)/shard_map/pallas_call | solution.py:520
  155.2 2.9 %shard_map.103 = (f32[2,8,128,128]{3,2,1,0:T(8,128)S(1)}, f32[32,128]{1,0:T(8,128)S(1)}, f32[32,128]{1,0:T(8,128)S(1)}, f32[128,128]{1,0:T(8,128)S(1)}, f32[128,128]{1,0:T(8,128)S(1)}) custom-call(f32[8]{0:T(128)S(1)} %copy-done.8, f32[6,8,128,128]{3,2,1,0:T(8,128)S(1)} %shard_map.92.eta_ref.east_ref.north_ref.refs_2_.refs_3_, ...), custom_call_target="tpu_custom_call" | custom-call | flops 1000000 | bytes 6000000 | tf_op jit(solution)/shard_map/pallas_call | solution.py:539
  158.2 1.7 collective-permute-start.14
  159.9 3.6 %collective-permute-start.11 = (f32[32,128]{1,0:T(8,128)S(1)}, f32[32,128]{1,0:T(8,128)S(1)}, u32[]{:S(2)}, u32[]{:S(2)}) collective-permute-start(f32[32,128]{1,0:T(8,128)S(1)} %get-tuple-element.44), channel_id=1, source_target_pairs={{0,8},{8,16},{16,24},{1,9},{9,17},{17,25},{2,10},{10,18},{18,26},{... | collective-permute-start | bytes 49160 | tf_op jit(solution)/shard_map/ppermute | solution.py:451
  163.5 2.3 %collective-permute-start.12 = (f32[32,128]{1,0:T(8,128)S(1)}, f32[32,128]{1,0:T(8,128)S(1)}, u32[]{:S(2)}, u32[]{:S(2)}) collective-permute-start(f32[32,128]{1,0:T(8,128)S(1)} %get-tuple-element.45), channel_id=1, source_target_pairs={{8,0},{16,8},{24,16},{9,1},{17,9},{25,17},{10,2},{18,10},{26,18},{... | collective-permute-start | bytes 49160 | tf_op jit(solution)/shard_map/ppermute | solution.py:452
  165.8 4.2 %collective-permute-done.12.refs_10_ = f32[32,128]{1,0:T(8,128)S(1)} collective-permute-done((f32[32,128]{1,0:T(8,128)S(1)}, f32[32,128]{1,0:T(8,128)S(1)}, u32[]{:S(2)}, u32[]{:S(2)}) %collective-permute-start.12) | collective-permute-done | bytes 16416 | tf_op jit(solution)/shard_map/ppermute | solution.py:452
  170.0 7.2 %shard_map.104 = (f32[6,8,128,128]{3,2,1,0:T(8,128)S(1)}, f32[32,128]{1,0:T(8,128)S(1)}, f32[32,128]{1,0:T(8,128)S(1)}, f32[128,128]{1,0:T(8,128)S(1)}, f32[128,128]{1,0:T(8,128)S(1)}) custom-call(f32[8]{0:T(128)S(1)} %copy-done.8, f32[2,8,128,128]{3,2,1,0:T(8,128)S(1)} %get-tuple-element.43.refs_1_, ...), custom_call_target="tpu_custom_call" | custom-call | flops 16000000 | bytes 9000000 | tf_op jit(solution)/shard_map/pallas_call | solution.py:459
  177.3 1.7 collective-permute-start.18
  179.0 3.6 %collective-permute-start.15 = (f32[32,128]{1,0:T(8,128)S(1)}, f32[32,128]{1,0:T(8,128)S(1)}, u32[]{:S(2)}, u32[]{:S(2)}) collective-permute-start(f32[32,128]{1,0:T(8,128)S(1)} %get-tuple-element.49), channel_id=1, source_target_pairs={{0,8},{8,16},{16,24},{1,9},{9,17},{17,25},{2,10},{10,18},{18,26},{... | collective-permute-start | bytes 49160 | tf_op jit(solution)/shard_map/ppermute | solution.py:451
  182.6 2.3 %collective-permute-start.16 = (f32[32,128]{1,0:T(8,128)S(1)}, f32[32,128]{1,0:T(8,128)S(1)}, u32[]{:S(2)}, u32[]{:S(2)}) collective-permute-start(f32[32,128]{1,0:T(8,128)S(1)} %get-tuple-element.50), channel_id=1, source_target_pairs={{8,0},{16,8},{24,16},{9,1},{17,9},{25,17},{10,2},{18,10},{26,18},{... | collective-permute-start | bytes 49160 | tf_op jit(solution)/shard_map/ppermute | solution.py:452
  184.8 4.2 %collective-permute-done.16.refs_10_ = f32[32,128]{1,0:T(8,128)S(1)} collective-permute-done((f32[32,128]{1,0:T(8,128)S(1)}, f32[32,128]{1,0:T(8,128)S(1)}, u32[]{:S(2)}, u32[]{:S(2)}) %collective-permute-start.16) | collective-permute-done | bytes 16416 | tf_op jit(solution)/shard_map/ppermute | solution.py:452
  189.1 5.9 %shard_map.105 = f32[6,8,128,128]{3,2,1,0:T(8,128)} custom-call(f32[8]{0:T(128)S(1)} %copy-done.8, f32[6,8,128,128]{3,2,1,0:T(8,128)S(1)} %get-tuple-element.48.refs_1_.refs_2_.refs_3_, f32[6,8,128,128]{3,2,1,0:T(8,128)S(1)} %get-tuple-element.48.refs_1_.refs_2_.refs_3_, f32[6,8,128,128]{3,2,1,0:T(8,128)S(1)} %get-tuple-element.48.refs_1_.refs_2_.refs_3_, ...), custom_call_target="tpu_custom_call" | custom-call | flops 16000000 | bytes 9000000 | tf_op jit(solution)/shard_map/pallas_call | solution.py:459
  (55 shorter events, 4.7 us)
Async XLA Ops:
  0.9 0.9 copy-start.7
  4.7 31.8 %copy-start = (f32[48,128,128]{2,1,0:T(8,128)S(1)}, f32[48,128,128]{2,1,0:T(8,128)}, u32[]{:S(2)}) copy-start(f32[48,128,128]{2,1,0:T(8,128)} %param.9) | copy-start | bytes 9437188
  4.7 31.8 %copy-start.3 = (f32[128,128]{1,0:T(8,128)S(1)}, f32[128,128]{1,0:T(8,128)}, u32[]{:S(2)}) copy-start(f32[128,128]{1,0:T(8,128)} %refs_5_.5) | copy-start | bytes 196612
  33.5 13.1 %copy-start.13 = (f32[1096,128]{1,0:T(8,128)S(1)}, f32[1096,128]{1,0:T(8,128)}, u32[]{:S(2)}) copy-start(f32[1096,128]{1,0:T(8,128)} %get-tuple-element.42.refs_0_) | copy-start | bytes 1683460
  33.5 74.1 %collective-permute-start.10 = (f32[1096,128]{1,0:T(8,128)}, f32[1096,128]{1,0:T(8,128)}, u32[]{:S(2)}, u32[]{:S(2)}) collective-permute-start(f32[1096,128]{1,0:T(8,128)} %get-tuple-element.41), channel_id=1, source_target_pairs={{0,4},{1,5},{2,6},{3,7},{4,0},{5,1},{6,2},{7,3},{8,12},{9,13},{10,... | collective-permute-start | bytes 1683464 | tf_op jit(solution)/shard_map/ppermute | solution.py:531
  39.0 13.6 %collective-permute-start.2 = (f32[128,128]{1,0:T(8,128)}, f32[128,128]{1,0:T(8,128)S(1)}, u32[]{:S(2)}, u32[]{:S(2)}) collective-permute-start(f32[128,128]{1,0:T(8,128)} %get-tuple-element.31), channel_id=1, source_target_pairs={{0,1},{1,2},{2,3},{3,4},{4,5},{5,6},{6,7},{7,0},{8,9},{9,10},{10,1... | collective-permute-start | bytes 196616 | tf_op jit(solution)/shard_map/ppermute | solution.py:453
  39.0 14.8 %collective-permute-start.3 = (f32[128,128]{1,0:T(8,128)}, f32[128,128]{1,0:T(8,128)S(1)}, u32[]{:S(2)}, u32[]{:S(2)}) collective-permute-start(f32[128,128]{1,0:T(8,128)} %get-tuple-element.32), channel_id=1, source_target_pairs={{1,0},{2,1},{3,2},{4,3},{5,4},{6,5},{7,6},{0,7},{9,8},{10,9},{11,1... | collective-permute-start | bytes 196616 | tf_op jit(solution)/shard_map/ppermute | solution.py:454
  40.7 11.6 %collective-permute-start = (f32[32,128]{1,0:T(8,128)S(1)}, f32[32,128]{1,0:T(8,128)S(1)}, u32[]{:S(2)}, u32[]{:S(2)}) collective-permute-start(f32[32,128]{1,0:T(8,128)S(1)} %get-tuple-element.29), channel_id=1, source_target_pairs={{0,8},{8,16},{16,24},{1,9},{9,17},{17,25},{2,10},{10,18},{18,26},{... | collective-permute-start | bytes 49160 | tf_op jit(solution)/shard_map/ppermute | solution.py:451
  44.1 8.3 %collective-permute-start.1 = (f32[32,128]{1,0:T(8,128)S(1)}, f32[32,128]{1,0:T(8,128)S(1)}, u32[]{:S(2)}, u32[]{:S(2)}) collective-permute-start(f32[32,128]{1,0:T(8,128)S(1)} %get-tuple-element.30), channel_id=1, source_target_pairs={{8,0},{16,8},{24,16},{9,1},{17,9},{25,17},{10,2},{18,10},{26,18},{... | collective-permute-start | bytes 49160 | tf_op jit(solution)/shard_map/ppermute | solution.py:452
  46.6 54.6 %copy-start.4 = (s32[128,128]{1,0:T(8,128)S(1)}, s32[128,128]{1,0:T(8,128)}, u32[]{:S(2)}) copy-start(s32[128,128]{1,0:T(8,128)} %refs_7_.5) | copy-start | bytes 196612
  46.6 54.6 %copy-start.5 = (f32[128,128]{1,0:T(8,128)S(1)}, f32[128,128]{1,0:T(8,128)}, u32[]{:S(2)}) copy-start(f32[128,128]{1,0:T(8,128)} %refs_6_.5) | copy-start | bytes 196612
  46.6 54.6 %copy-start.8 = (f32[8]{0:T(128)S(1)}, f32[8]{0:T(128)}, u32[]{:S(2)}) copy-start(f32[8]{0:T(128)} %constant.18.clone.refs_0_.omega_ref) | copy-start | bytes 100
  51.4 1.0 copy-start.11
  52.4 62.1 %collective-permute-start.9 = (f32[1096,128]{1,0:T(8,128)}, f32[1096,128]{1,0:T(8,128)S(1)}, u32[]{:S(2)}, u32[]{:S(2)}) collective-permute-start(f32[1096,128]{1,0:T(8,128)} %get-tuple-element.40), channel_id=1, source_target_pairs={{0,5},{1,4},{2,7},{3,6},{4,1},{5,0},{6,3},{7,2},{8,13},{9,12},{10,... | collective-permute-start | bytes 1683464 | tf_op jit(solution)/shard_map/ppermute | solution.py:531
  52.5 71.3 %collective-permute-start.8 = (f32[1096,128]{1,0:T(8,128)}, f32[1096,128]{1,0:T(8,128)S(1)}, u32[]{:S(2)}, u32[]{:S(2)}) collective-permute-start(f32[1096,128]{1,0:T(8,128)} %get-tuple-element.39), channel_id=1, source_target_pairs={{0,6},{1,7},{2,4},{3,5},{4,2},{5,3},{6,0},{7,1},{8,14},{9,15},{10,... | collective-permute-start | bytes 1683464 | tf_op jit(solution)/shard_map/ppermute | solution.py:531
  52.6 81.3 %collective-permute-start.7 = (f32[1096,128]{1,0:T(8,128)}, f32[1096,128]{1,0:T(8,128)S(1)}, u32[]{:S(2)}, u32[]{:S(2)}) collective-permute-start(f32[1096,128]{1,0:T(8,128)} %get-tuple-element.38), channel_id=1, source_target_pairs={{0,7},{1,6},{2,5},{3,4},{4,3},{5,2},{6,1},{7,0},{8,15},{9,14},{10,... | collective-permute-start | bytes 1683464 | tf_op jit(solution)/shard_map/ppermute | solution.py:531
  53.8 85.6 %collective-permute-start.6 = (f32[1096,128]{1,0:T(8,128)}, f32[1096,128]{1,0:T(8,128)S(1)}, u32[]{:S(2)}, u32[]{:S(2)}) collective-permute-start(f32[1096,128]{1,0:T(8,128)} %get-tuple-element.37), channel_id=1, source_target_pairs={{0,1},{1,0},{2,3},{3,2},{4,5},{5,4},{6,7},{7,6},{8,9},{9,8},{10,11... | collective-permute-start | bytes 1683464 | tf_op jit(solution)/shard_map/ppermute | solution.py:531
  101.3 1.9 copy-start.1
  103.2 4.5 %copy-start.15 = (f32[1096,128]{1,0:T(8,128)S(1)}, f32[1096,128]{1,0:T(8,128)}, u32[]{:S(2)}) copy-start(f32[1096,128]{1,0:T(8,128)} %get-tuple-element.36) | copy-start | bytes 1683460
  103.2 4.6 %copy-start.12 = (f32[16,64,256]{2,1,0:T(8,128)S(1)}, f32[16,64,256]{2,1,0:T(8,128)}, u32[]{:S(2)}) copy-start(f32[16,64,256]{2,1,0:T(8,128)} %copy-done.11) | copy-start | bytes 3145732
  107.7 6.8 %copy-start.14 = (f32[1096,128]{1,0:T(8,128)S(1)}, f32[1096,128]{1,0:T(8,128)}, u32[]{:S(2)}) copy-start(f32[1096,128]{1,0:T(8,128)} %get-tuple-element.35) | copy-start | bytes 1683460
  107.7 36.9 %collective-permute-start.5 = (f32[1096,128]{1,0:T(8,128)S(1)}, f32[1096,128]{1,0:T(8,128)S(1)}, u32[]{:S(2)}, u32[]{:S(2)}) collective-permute-start(f32[1096,128]{1,0:T(8,128)S(1)} %copy-done.15), channel_id=1, source_target_pairs={{0,2},{1,3},{2,0},{3,1},{4,6},{5,7},{6,4},{7,5},{8,10},{9,11},{10,... | collective-permute-start | bytes 1683464 | tf_op jit(solution)/shard_map/ppermute | solution.py:531
  114.5 35.1 %collective-permute-start.4 = (f32[1096,128]{1,0:T(8,128)S(1)}, f32[1096,128]{1,0:T(8,128)S(1)}, u32[]{:S(2)}, u32[]{:S(2)}) collective-permute-start(f32[1096,128]{1,0:T(8,128)S(1)} %copy-done.14), channel_id=1, source_target_pairs={{0,3},{1,2},{2,1},{3,0},{4,7},{5,6},{6,5},{7,4},{8,11},{9,10},{10,... | collective-permute-start | bytes 1683464 | tf_op jit(solution)/shard_map/ppermute | solution.py:531
  155.2 14.9 %copy-start.2 = (f32[48,128,128]{2,1,0:T(8,128)S(1)}, f32[48,128,128]{2,1,0:T(8,128)}, u32[]{:S(2)}) copy-start(f32[48,128,128]{2,1,0:T(8,128)} %param.10) | copy-start | bytes 9437188
  158.1 11.9 %collective-permute-start.13 = (f32[128,128]{1,0:T(8,128)S(1)}, f32[128,128]{1,0:T(8,128)S(1)}, u32[]{:S(2)}, u32[]{:S(2)}) collective-permute-start(f32[128,128]{1,0:T(8,128)S(1)} %get-tuple-element.46), channel_id=1, source_target_pairs={{0,1},{1,2},{2,3},{3,4},{4,5},{5,6},{6,7},{7,0},{8,9},{9,10},{10,1... | collective-permute-start | bytes 196616 | tf_op jit(solution)/shard_map/ppermute | solution.py:453
  158.2 11.8 %collective-permute-start.14 = (f32[128,128]{1,0:T(8,128)S(1)}, f32[128,128]{1,0:T(8,128)S(1)}, u32[]{:S(2)}, u32[]{:S(2)}) collective-permute-start(f32[128,128]{1,0:T(8,128)S(1)} %get-tuple-element.47), channel_id=1, source_target_pairs={{1,0},{2,1},{3,2},{4,3},{5,4},{6,5},{7,6},{0,7},{9,8},{10,9},{11,1... | collective-permute-start | bytes 196616 | tf_op jit(solution)/shard_map/ppermute | solution.py:454
  159.9 5.8 %collective-permute-start.11 = (f32[32,128]{1,0:T(8,128)S(1)}, f32[32,128]{1,0:T(8,128)S(1)}, u32[]{:S(2)}, u32[]{:S(2)}) collective-permute-start(f32[32,128]{1,0:T(8,128)S(1)} %get-tuple-element.44), channel_id=1, source_target_pairs={{0,8},{8,16},{16,24},{1,9},{9,17},{17,25},{2,10},{10,18},{18,26},{... | collective-permute-start | bytes 49160 | tf_op jit(solution)/shard_map/ppermute | solution.py:451
  163.5 6.5 %collective-permute-start.12 = (f32[32,128]{1,0:T(8,128)S(1)}, f32[32,128]{1,0:T(8,128)S(1)}, u32[]{:S(2)}, u32[]{:S(2)}) collective-permute-start(f32[32,128]{1,0:T(8,128)S(1)} %get-tuple-element.45), channel_id=1, source_target_pairs={{8,0},{16,8},{24,16},{9,1},{17,9},{25,17},{10,2},{18,10},{26,18},{... | collective-permute-start | bytes 49160 | tf_op jit(solution)/shard_map/ppermute | solution.py:452
  177.2 11.9 %collective-permute-start.17 = (f32[128,128]{1,0:T(8,128)S(1)}, f32[128,128]{1,0:T(8,128)S(1)}, u32[]{:S(2)}, u32[]{:S(2)}) collective-permute-start(f32[128,128]{1,0:T(8,128)S(1)} %get-tuple-element.51), channel_id=1, source_target_pairs={{0,1},{1,2},{2,3},{3,4},{4,5},{5,6},{6,7},{7,0},{8,9},{9,10},{10,1... | collective-permute-start | bytes 196616 | tf_op jit(solution)/shard_map/ppermute | solution.py:453
  177.3 11.8 %collective-permute-start.18 = (f32[128,128]{1,0:T(8,128)S(1)}, f32[128,128]{1,0:T(8,128)S(1)}, u32[]{:S(2)}, u32[]{:S(2)}) collective-permute-start(f32[128,128]{1,0:T(8,128)S(1)} %get-tuple-element.52), channel_id=1, source_target_pairs={{1,0},{2,1},{3,2},{4,3},{5,4},{6,5},{7,6},{0,7},{9,8},{10,9},{11,1... | collective-permute-start | bytes 196616 | tf_op jit(solution)/shard_map/ppermute | solution.py:454
  179.0 5.8 %collective-permute-start.15 = (f32[32,128]{1,0:T(8,128)S(1)}, f32[32,128]{1,0:T(8,128)S(1)}, u32[]{:S(2)}, u32[]{:S(2)}) collective-permute-start(f32[32,128]{1,0:T(8,128)S(1)} %get-tuple-element.49), channel_id=1, source_target_pairs={{0,8},{8,16},{16,24},{1,9},{9,17},{17,25},{2,10},{10,18},{18,26},{... | collective-permute-start | bytes 49160 | tf_op jit(solution)/shard_map/ppermute | solution.py:451
  182.6 6.5 %collective-permute-start.16 = (f32[32,128]{1,0:T(8,128)S(1)}, f32[32,128]{1,0:T(8,128)S(1)}, u32[]{:S(2)}, u32[]{:S(2)}) collective-permute-start(f32[32,128]{1,0:T(8,128)S(1)} %get-tuple-element.50), channel_id=1, source_target_pairs={{8,0},{16,8},{24,16},{9,1},{17,9},{25,17},{10,2},{18,10},{26,18},{... | collective-permute-start | bytes 49160 | tf_op jit(solution)/shard_map/ppermute | solution.py:452
  (3 other events, 2.3 us)

commit v4 on v3

--- a/solution.py
+++ b/solution.py
@@ -35,7 +35,7 @@
     return pl.CostEstimate(flops=flops, bytes_accessed=nbytes, transcendentals=0)
 
 
-def rank_kernel(tiles, cuts, dest_ref, cell_ref, *outs):
+def rank_kernel(tiles, cuts, group, dest_ref, cell_ref, *outs):
     slot_ref, table_ref = outs
     blocks, block = dest_ref.shape[0] // 2, BLOCK
 
@@ -77,6 +77,10 @@
     table_ref[:blocks, :] = jnp.where(lane == LANES - 1, most, counts).astype(jnp.int32)
     table_ref[blocks : 2 * blocks, :] = bases.astype(jnp.int32)
     table_ref[2 * blocks : 3 * blocks, :] = (places + first[0:1]).astype(jnp.int32)
+    line, column = iota((8, LANES), 0), iota((8, LANES), 1)
+    for part in range(blocks // group):
+        largest = jnp.max(most[part * group : (part + 1) * group, :], axis=0, keepdims=True)
+        total = jnp.where((line == 1) & (column == part), largest, total)
     table_ref[3 * blocks :, :] = total.astype(jnp.int32)
 
 
@@ -158,7 +162,10 @@
         reads[part].wait()
         lax.fori_loop(0, group, permute, part * group, unroll=16)
         lax.fori_loop(0, group, spread, part * group, unroll=4)
-        lax.fori_loop(0, group, spread_rest, part * group)
+
+        @pl.when(table_ref[3 * blocks + 1, part] > chunk)
+        def _long(part=part):
+            lax.fori_loop(0, group, spread_rest, part * group)
 
     row, lane = iota((32, LANES), 0), iota((32, LANES), 1)
     joined = jnp.where((row < width) & ((lane == row) | (lane == row + width)), 1.0, 0.0)
@@ -282,13 +289,17 @@
             south[pl.ds(at, 1), :] = field[rows - 1 : rows]
 
 
-def edges_kernel(rows, state_ref, depth_ref, *strips):
-    k = pl.program_id(0)
+def edges_kernel(per, rows, state_ref, depth_ref, *strips):
+    for kk in range(per):
+        edges_at(pl.program_id(0) * per + kk, kk, rows, state_ref, depth_ref, *strips)
+
+
+def edges_at(k, kk, rows, state_ref, depth_ref, *strips):
     height = depth_ref.shape[0]
     for r0 in range(0, height, rows):
         part = slice(r0, r0 + rows)
         depth = depth_ref[part, :]
-        fields = [state_ref[g, 0, part, :] for g in range(6)]
+        fields = [state_ref[g, kk, part, :] for g in range(6)]
         fields = fields[:2] + [depth * field for field in fields[2:]]
         put_edges(strips, k, rows, r0, height, fields)
 
@@ -299,8 +310,12 @@
     return force_ref[channel, at : at + rows, side * LANES : (side + 1) * LANES]
 
 
-def join_kernel(rows, omega_ref, eta_ref, east_ref, north_ref, depth_ref, ocean_ref, re_ref, im_ref, out_ref, *strips):
-    k = pl.program_id(0)
+def join_kernel(per, rows, omega_ref, eta_ref, east_ref, north_ref, depth_ref, ocean_ref, re_ref, im_ref, out_ref, *strips):
+    for kk in range(per):
+        join_at(pl.program_id(0) * per + kk, kk, rows, omega_ref, eta_ref, east_ref, north_ref, depth_ref, ocean_ref, re_ref, im_ref, out_ref, *strips)
+
+
+def join_at(k, kk, rows, omega_ref, eta_ref, east_ref, north_ref, depth_ref, ocean_ref, re_ref, im_ref, out_ref, *strips):
     omega = omega_ref[k]
     weight = RELAX / (1.0 + omega * omega)
     height = depth_ref.shape[0]
@@ -308,19 +323,24 @@
         part = slice(r0, r0 + rows)
         depth = depth_ref[part, :]
         ocean = ocean_ref[part, :].astype(jnp.float32) * weight
-        f_re = force(re_ref, 0, r0, rows, height // 2)
-        f_im = force(im_ref, 0, r0, rows, height // 2)
-        eta_re = eta_ref[0, 0, part, :] + ocean * (f_re + f_im * omega)
-        eta_im = eta_ref[1, 0, part, :] + ocean * (f_im - f_re * omega)
-        out_ref[0, 0, part, :] = eta_re
-        out_ref[1, 0, part, :] = eta_im
+        f_re = force(re_ref, kk, r0, rows, height // 2)
+        f_im = force(im_ref, kk, r0, rows, height // 2)
+        eta_re = eta_ref[0, kk, part, :] + ocean * (f_re + f_im * omega)
+        eta_im = eta_ref[1, kk, part, :] + ocean * (f_im - f_re * omega)
+        out_ref[0, kk, part, :] = eta_re
+        out_ref[1, kk, part, :] = eta_im
         fields = [eta_re, eta_im] + [
-            depth * ref[g, 0, part, :] for ref in (east_ref, north_ref) for g in range(2)
+            depth * ref[g, kk, part, :] for ref in (east_ref, north_ref) for g in range(2)
         ]
         put_edges(strips, k, rows, r0, height, fields)
 
 
-def sweep_kernel(rows, forced, edges, *refs):
+def sweep_kernel(per, rows, forced, edges, *refs):
+    for kk in range(per):
+        sweep_at(pl.program_id(0) * per + kk, kk, rows, forced, edges, *refs)
+
+
+def sweep_at(k, kk, rows, forced, edges, *refs):
     refs = list(refs)
     omega_ref, eta_ref, vel_e_ref, vel_n_ref, pot_ref = refs[:5]
     depth_ref, drag_ref, ocean_ref, turn_ref = refs[5:9]
@@ -331,7 +351,6 @@
         refs = refs[2:]
     out_ref = refs[0]
     strips = refs[1:]
-    k = pl.program_id(0)
     omega = omega_ref[k]
     inv_eta = 1.0 / (1.0 + omega * omega)
     height = depth_ref.shape[0]
@@ -364,28 +383,28 @@
         ocean = ocean_ref[part, :].astype(jnp.float32)
         turn = turn_ref[part, :]
         inv = 1.0 / (diag * diag + omega * omega)
-        eta = [eta_ref[g, 0, part, :] for g in range(2)]
-        east = [vel_e_ref[g, 0, part, :] for g in range(2)]
-        north = [vel_n_ref[g, 0, part, :] for g in range(2)]
-        pot = [pot_ref[g, 0, part, :] for g in range(6)]
+        eta = [eta_ref[g, kk, part, :] for g in range(2)]
+        east = [vel_e_ref[g, kk, part, :] for g in range(2)]
+        north = [vel_n_ref[g, kk, part, :] for g in range(2)]
+        pot = [pot_ref[g, kk, part, :] for g in range(6)]
         flux = []
         grad_lat = []
         for g in range(2):
             hn = depth * north[g]
-            hn_first = depth_ref[before, :] * vel_n_ref[g, 0, before, :]
-            hn_last = depth_ref[after, :] * vel_n_ref[g, 0, after, :]
+            hn_first = depth_ref[before, :] * vel_n_ref[g, kk, before, :]
+            hn_last = depth_ref[after, :] * vel_n_ref[g, kk, after, :]
             flux.append(
                 dlon(depth * east[g], 2 + g, r0) + shifted(hn, hn_first, hn_last, 2 + g, r0)
             )
             grad_lat.append(
-                shifted(eta[g], eta_ref[g, 0, before, :], eta_ref[g, 0, after, :], g, r0)
+                shifted(eta[g], eta_ref[g, kk, before, :], eta_ref[g, kk, after, :], g, r0)
             )
         grad_lon = [dlon(eta[g], g, r0) for g in range(2)]
         res_re = pot[0] - (eta[0] - omega * eta[1] + flux[0])
         res_im = pot[1] - (eta[1] + omega * eta[0] + flux[1])
         if forced:
-            res_re = res_re + force(re_ref, 0, r0, rows, height // 2)
-            res_im = res_im + force(im_ref, 0, r0, rows, height // 2)
+            res_re = res_re + force(re_ref, kk, r0, rows, height // 2)
+            res_im = res_im + force(im_ref, kk, r0, rows, height // 2)
         weight = ocean * RELAX
         new = [
             ocean * eta[0] + weight * ((res_re + res_im * omega) * inv_eta),
@@ -402,7 +421,7 @@
             new.append(ocean * own[0] + scaled * (res_re * diag + res_im * omega))
             new.append(ocean * own[1] + scaled * (res_im * diag - res_re * omega))
         for g in range(6):
-            out_ref[g, 0, part, :] = new[g]
+            out_ref[g, kk, part, :] = new[g]
         if edges:
             put_edges(strips, k, rows, r0, height, new[:2] + [depth * q for q in new[2:]])
 
@@ -423,6 +442,7 @@
     cells = dest_cell.reshape(2 * blocks, LANES)
     bucket_rows = windows * (width + 1) + HEAD
 
+    group = min(32, blocks)
     omega = jnp.asarray(OMEGAS, f32)
     row_ids = lax.axis_index("lat") * height + jnp.arange(height, dtype=jnp.int32)
     lat_pos = (row_ids.astype(f32) + 0.5) / (height * lats) - 0.5
@@ -430,15 +450,15 @@
 
     state = tide_state.reshape(6, consts, height, across)
     pot = potential.reshape(6, consts, height, across)
-    chunk_rows = 32
+    chunk_rows, per = 64, 4
 
     def fields(count, first):
-        return pl.BlockSpec((count, 1, height, across), lambda k: (first // count, k, 0, 0))
+        return pl.BlockSpec((count, per, height, across), lambda k: (first // count, k, 0, 0))
 
     plane = pl.BlockSpec((height, across), lambda k: (0, 0))
     flat = pl.BlockSpec((4 * consts, across), lambda k: (0, 0))
-    half_re = pl.BlockSpec((1, height // 2, 2 * across), lambda k: (k, 0, 0))
-    half_im = pl.BlockSpec((1, height // 2, 2 * across), lambda k: (consts + k, 0, 0))
+    half_re = pl.BlockSpec((per, height // 2, 2 * across), lambda k: (k, 0, 0))
+    half_im = pl.BlockSpec((per, height // 2, 2 * across), lambda k: (consts // per + k, 0, 0))
     strip_specs = [flat, flat, plane, plane]
     strip_shapes = [jax.ShapeDtypeStruct((4 * consts, across), f32)] * 2 + [
         jax.ShapeDtypeStruct((height, across), f32)
@@ -457,8 +477,8 @@
     def sweep(eta, vel, strips, forcing, edges):
         forced = forcing is not None
         out = pl.pallas_call(
-            functools.partial(sweep_kernel, chunk_rows, forced, edges),
-            grid=(consts,),
+            functools.partial(sweep_kernel, per, chunk_rows, forced, edges),
+            grid=(consts // per,),
             in_specs=[SMEM, fields(2, 0), fields(2, 2), fields(2, 4), fields(6, 0)]
             + [plane] * 4
             + strip_specs
@@ -474,7 +494,7 @@
         return out[0], out[1:]
 
     slot, table = pl.pallas_call(
-        functools.partial(rank_kernel, tiles, cuts),
+        functools.partial(rank_kernel, tiles, cuts, group),
         in_specs=[VMEM, VMEM],
         out_specs=[VMEM] * 2,
         out_shape=[
@@ -485,8 +505,8 @@
     )(dest_tile.reshape(2 * blocks, LANES), cells)
 
     strips = pl.pallas_call(
-        functools.partial(edges_kernel, chunk_rows),
-        grid=(consts,),
+        functools.partial(edges_kernel, per, chunk_rows),
+        grid=(consts // per,),
         in_specs=[fields(6, 0), plane],
         out_specs=strip_specs,
         out_shape=strip_shapes,
@@ -495,7 +515,6 @@
     )(state, water_depth)
     strips = exchange(strips)
 
-    group = min(32, blocks)
 
     buckets = pl.pallas_call(
         functools.partial(bucket_kernel, tiles, cuts, capacity, width, group),
@@ -526,7 +545,8 @@
             cost_estimate=cost(10**10, 3 * 10**6),
         )(*parts, *(() if total is None else (total,)))
 
-    order = list(range(tiles // 2, tiles)) + list(range(1, tiles // 2))
+    half = tiles // 2
+    order = [half] + list(range(1, half)) + list(range(half + 1, tiles))
     arrived = [
         lax.ppermute(buckets[s], "lon", [(i, i ^ s) for i in range(tiles)]) for s in order
     ]
@@ -537,8 +557,8 @@
         forcing = add(arrived[first : first + each], forcing)
 
     eta, *strips = pl.pallas_call(
-        functools.partial(join_kernel, chunk_rows),
-        grid=(consts,),
+        functools.partial(join_kernel, per, chunk_rows),
+        grid=(consts // per,),
         in_specs=[
             SMEM,
             fields(2, 0),

time: 196 us -> 179 us (0.913)
  the two profiles are of different devices: /device:TPU:10 before, /device:TPU:0 now
where the time goes in v4:
time: 179 us; the launch traced here: 181 us
  Pallas kernels  66.6 us (37%)
  starting transfers between devices  62.8 us (35%)
  waiting for transfers between devices  45.6 us (25%)
  local copies, waits for them, and re-layouts  6.13 us (3%)
    ppermute x7, waiting for transfers between devices, local(): lax.ppermute(buckets[s], 'lon', [(i, i ^ s) for i in range(tiles)])  36.5 us
    pallas_call x1, Pallas kernels, local(): pl.pallas_call(functools.partial(bucket_kernel, tiles, cuts, capacity, wi...  27.5 us
    ppermute x7, starting transfers between devices, local(): lax.ppermute(buckets[s], 'lon', [(i, i ^ s) for i in range(tiles)])  24.3 us
    ppermute x3, starting transfers between devices, exchange(): lax.ppermute(west, 'lon', [((i + 1) % tiles, i) for i in range(tiles)])  21.6 us
    pallas_call x8, Pallas kernels, add(): pl.pallas_call(functools.partial(sum_kernel, width, windows, len(parts),...  19.4 us
    pallas_call x3, Pallas kernels, sweep(): pl.pallas_call(functools.partial(sweep_kernel, per, chunk_rows, forced, e...  14.1 us
    ppermute x3, starting transfers between devices, exchange(): lax.ppermute(south, 'lat', [(i, i + 1) for i in range(lats - 1)])  10.8 us
    ppermute x3, waiting for transfers between devices, exchange(): lax.ppermute(north, 'lat', [(i + 1, i) for i in range(lats - 1)])  8.81 us
  transfers between devices with their start and end apart: 19, of which 7 were waited for; matrix products, arithmetic and copies ran while one was open for 0% of the time, Pallas kernels for 13%

profile of v4, /device:TPU:0, one launch (start us, length us, event | category | flops | bytes accessed | tf_op | source)
XLA Modules:
  0.0 181.5 jit_solution(7016536617754555999)
XLA Ops:
  1.8 1.5 shard_map.93
  4.6 27.5 %shard_map.94 = (f32[1096,128]{1,0:T(8,128)}, f32[1096,128]{1,0:T(8,128)}, f32[1096,128]{1,0:T(8,128)}, f32[1096,128]{1,0:T(8,128)}, f32[1096,128]{1,0:T(8,128)}...) custom-call(s32[392,128]{1,0:T(8,128)} %copy-done.9, s32[128,256]{1,0:T(8,128)} %copy-done.10, ...), custom_call_target="tpu_custom_call" | custom-call | flops 10000000000 | bytes 7000000 | tf_op jit(solution)/shard_map/pallas_call | solution.py:519
  32.1 3.8 %collective-permute-start.10 = (f32[1096,128]{1,0:T(8,128)}, f32[1096,128]{1,0:T(8,128)}, u32[]{:S(2)}, u32[]{:S(2)}) collective-permute-start(f32[1096,128]{1,0:T(8,128)} %get-tuple-element.41), channel_id=1, source_target_pairs={{0,4},{1,5},{2,6},{3,7},{4,0},{5,1},{6,2},{7,3},{8,12},{9,13},{10,... | collective-permute-start | bytes 1683464 | tf_op jit(solution)/shard_map/ppermute | solution.py:551
  35.9 2.1 %shard_map.91 = (f32[32,128]{1,0:T(8,128)S(1)}, f32[32,128]{1,0:T(8,128)S(1)}, f32[128,128]{1,0:T(8,128)}, f32[128,128]{1,0:T(8,128)}) custom-call(f32[6,8,128,128]{3,2,1,0:T(8,128)S(1)} %bitcast.5, f32[128,128]{1,0:T(8,128)S(1)} %copy-done.3), custom_call_target="tpu_custom_call" | custom-call | flops 1000000 | bytes 3000000 | tf_op jit(solution)/shard_map/pallas_call | solution.py:507
  38.0 3.5 %collective-permute-start.3 = (f32[128,128]{1,0:T(8,128)}, f32[128,128]{1,0:T(8,128)S(1)}, u32[]{:S(2)}, u32[]{:S(2)}) collective-permute-start(f32[128,128]{1,0:T(8,128)} %get-tuple-element.32), channel_id=1, source_target_pairs={{1,0},{2,1},{3,2},{4,3},{5,4},{6,5},{7,6},{0,7},{9,8},{10,9},{11,1... | collective-permute-start | bytes 196616 | tf_op jit(solution)/shard_map/ppermute | solution.py:474
  41.6 3.7 %collective-permute-start = (f32[32,128]{1,0:T(8,128)S(1)}, f32[32,128]{1,0:T(8,128)S(1)}, u32[]{:S(2)}, u32[]{:S(2)}) collective-permute-start(f32[32,128]{1,0:T(8,128)S(1)} %get-tuple-element.29), channel_id=1, source_target_pairs={{0,8},{8,16},{16,24},{1,9},{9,17},{17,25},{2,10},{10,18},{18,26},{... | collective-permute-start | bytes 49160 | tf_op jit(solution)/shard_map/ppermute | solution.py:471
  45.3 1.3 collective-permute-start.1
  46.6 2.8 %shard_map.95.refs_1_ = f32[16,64,256]{2,1,0:T(8,128)S(1)} custom-call(f32[1096,128]{1,0:T(8,128)S(1)} %copy-done.13), custom_call_target="tpu_custom_call" | custom-call | flops 10000000000 | bytes 3000000 | tf_op jit(solution)/shard_map/pallas_call | solution.py:539
  50.9 12.0 %collective-permute-start.7 = (f32[1096,128]{1,0:T(8,128)}, f32[1096,128]{1,0:T(8,128)S(1)}, u32[]{:S(2)}, u32[]{:S(2)}) collective-permute-start(f32[1096,128]{1,0:T(8,128)} %get-tuple-element.38), channel_id=1, source_target_pairs={{0,3},{1,2},{2,1},{3,0},{4,7},{5,6},{6,5},{7,4},{8,11},{9,10},{10,... | collective-permute-start | bytes 1683464 | tf_op jit(solution)/shard_map/ppermute | solution.py:551
  63.0 1.9 %copy-done.1 = f32[48,128,128]{2,1,0:T(8,128)S(1)} copy-done((f32[48,128,128]{2,1,0:T(8,128)S(1)}, f32[48,128,128]{2,1,0:T(8,128)}, u32[]{:S(2)}) %copy-start.1) | copy-done | bytes 3145752
  64.9 3.8 %shard_map.92.eta_ref.east_ref.north_ref.refs_2_.refs_3_ = f32[6,8,128,128]{3,2,1,0:T(8,128)S(1)} custom-call(f32[8]{0:T(128)S(1)} %copy-done.8, f32[6,8,128,128]{3,2,1,0:T(8,128)S(1)} %bitcast.6, f32[6,8,128,128]{3,2,1,0:T(8,128)S(1)} %bitcast.7, f32[6,8,128,128]{3,2,1,0:T(8,128)S(1)} %bitcast.8, f32[6,8,128,128]{3,2,1,0:T(8,128)S(1)} %bitcast.9, ...), custom_call_target="tpu_custom_call" | custom-call | flops 16000000 | bytes 9000000 | tf_op jit(solution)/shard_map/pallas_call | solution.py:479
  68.8 2.4 %collective-permute-start.5 = (f32[1096,128]{1,0:T(8,128)S(1)}, f32[1096,128]{1,0:T(8,128)S(1)}, u32[]{:S(2)}, u32[]{:S(2)}) collective-permute-start(f32[1096,128]{1,0:T(8,128)S(1)} %copy-done.15), channel_id=1, source_target_pairs={{0,6},{1,7},{2,4},{3,5},{4,2},{5,3},{6,0},{7,1},{8,14},{9,15},{10,... | collective-permute-start | bytes 1683464 | tf_op jit(solution)/shard_map/ppermute | solution.py:551
  71.2 3.2 %shard_map.96.refs_1_ = f32[16,64,256]{2,1,0:T(8,128)S(1)} custom-call(f32[1096,128]{1,0:T(8,128)} %collective-permute-done.10.refs_0_, f32[16,64,256]{2,1,0:T(8,128)S(1)} %copy-done.12), custom_call_target="tpu_custom_call" | custom-call | flops 10000000000 | bytes 3000000 | tf_op jit(solution)/shard_map/pallas_call | solution.py:539
  74.4 6.0 %collective-permute-start.4 = (f32[1096,128]{1,0:T(8,128)S(1)}, f32[1096,128]{1,0:T(8,128)S(1)}, u32[]{:S(2)}, u32[]{:S(2)}) collective-permute-start(f32[1096,128]{1,0:T(8,128)S(1)} %copy-done.14), channel_id=1, source_target_pairs={{0,7},{1,6},{2,5},{3,4},{4,3},{5,2},{6,1},{7,0},{8,15},{9,14},{10,... | collective-permute-start | bytes 1683464 | tf_op jit(solution)/shard_map/ppermute | solution.py:551
  80.4 2.1 %shard_map.97.refs_1_ = f32[16,64,256]{2,1,0:T(8,128)S(1)} custom-call(f32[1096,128]{1,0:T(8,128)S(1)} %collective-permute-done.9.refs_0_, f32[16,64,256]{2,1,0:T(8,128)S(1)} %shard_map.96.refs_1_), custom_call_target="tpu_custom_call" | custom-call | flops 10000000000 | bytes 3000000 | tf_op jit(solution)/shard_map/pallas_call | solution.py:539
  82.6 3.1 %collective-permute-done.8.refs_0_ = f32[1096,128]{1,0:T(8,128)S(1)} collective-permute-done((f32[1096,128]{1,0:T(8,128)}, f32[1096,128]{1,0:T(8,128)S(1)}, u32[]{:S(2)}, u32[]{:S(2)}) %collective-permute-start.8) | collective-permute-done | bytes 561184 | tf_op jit(solution)/shard_map/ppermute | solution.py:551
  85.6 2.6 %shard_map.98.refs_1_ = f32[16,64,256]{2,1,0:T(8,128)S(1)} custom-call(f32[1096,128]{1,0:T(8,128)S(1)} %collective-permute-done.8.refs_0_, f32[16,64,256]{2,1,0:T(8,128)S(1)} %shard_map.97.refs_1_), custom_call_target="tpu_custom_call" | custom-call | flops 10000000000 | bytes 3000000 | tf_op jit(solution)/shard_map/pallas_call | solution.py:539
  88.2 33.4 %collective-permute-done.7.refs_0_ = f32[1096,128]{1,0:T(8,128)S(1)} collective-permute-done((f32[1096,128]{1,0:T(8,128)}, f32[1096,128]{1,0:T(8,128)S(1)}, u32[]{:S(2)}, u32[]{:S(2)}) %collective-permute-start.7) | collective-permute-done | bytes 561184 | tf_op jit(solution)/shard_map/ppermute | solution.py:551
  121.6 2.1 %shard_map.99.refs_1_ = f32[16,64,256]{2,1,0:T(8,128)S(1)} custom-call(f32[1096,128]{1,0:T(8,128)S(1)} %collective-permute-done.7.refs_0_, f32[16,64,256]{2,1,0:T(8,128)S(1)} %shard_map.98.refs_1_), custom_call_target="tpu_custom_call" | custom-call | flops 10000000000 | bytes 3000000 | tf_op jit(solution)/shard_map/pallas_call | solution.py:539
  123.8 2.1 %shard_map.100.refs_1_ = f32[16,64,256]{2,1,0:T(8,128)S(1)} custom-call(f32[1096,128]{1,0:T(8,128)S(1)} %collective-permute-done.6.refs_0_, f32[16,64,256]{2,1,0:T(8,128)S(1)} %shard_map.99.refs_1_), custom_call_target="tpu_custom_call" | custom-call | flops 10000000000 | bytes 3000000 | tf_op jit(solution)/shard_map/pallas_call | solution.py:539
  125.9 2.1 %shard_map.101.refs_1_ = f32[16,64,256]{2,1,0:T(8,128)S(1)} custom-call(f32[1096,128]{1,0:T(8,128)S(1)} %collective-permute-done.5.refs_0_, f32[16,64,256]{2,1,0:T(8,128)S(1)} %shard_map.100.refs_1_), custom_call_target="tpu_custom_call" | custom-call | flops 10000000000 | bytes 3000000 | tf_op jit(solution)/shard_map/pallas_call | solution.py:539
  128.0 2.3 %shard_map.102.re_ref.im_ref.refs_13_.refs_14_ = f32[16,64,256]{2,1,0:T(8,128)S(1)} custom-call(f32[1096,128]{1,0:T(8,128)S(1)} %collective-permute-done.4.refs_0_, f32[16,64,256]{2,1,0:T(8,128)S(1)} %shard_map.101.refs_1_), custom_call_target="tpu_custom_call" | custom-call | flops 10000000000 | bytes 3000000 | tf_op jit(solution)/shard_map/pallas_call | solution.py:539
  130.4 2.2 %shard_map.103 = (f32[2,8,128,128]{3,2,1,0:T(8,128)S(1)}, f32[32,128]{1,0:T(8,128)S(1)}, f32[32,128]{1,0:T(8,128)S(1)}, f32[128,128]{1,0:T(8,128)S(1)}, f32[128,128]{1,0:T(8,128)S(1)}) custom-call(f32[8]{0:T(128)S(1)} %copy-done.8, f32[6,8,128,128]{3,2,1,0:T(8,128)S(1)} %shard_map.92.eta_ref.east_ref.north_ref.refs_2_.refs_3_, ...), custom_call_target="tpu_custom_call" | custom-call | flops 1000000 | bytes 6000000 | tf_op jit(solution)/shard_map/pallas_call | solution.py:559
  132.5 2.1 %collective-permute-start.13 = (f32[128,128]{1,0:T(8,128)S(1)}, f32[128,128]{1,0:T(8,128)S(1)}, u32[]{:S(2)}, u32[]{:S(2)}) collective-permute-start(f32[128,128]{1,0:T(8,128)S(1)} %get-tuple-element.46), channel_id=1, source_target_pairs={{0,1},{1,2},{2,3},{3,4},{4,5},{5,6},{6,7},{7,0},{8,9},{9,10},{10,1... | collective-permute-start | bytes 196616 | tf_op jit(solution)/shard_map/ppermute | solution.py:473
  134.7 14.5 %collective-permute-start.14 = (f32[128,128]{1,0:T(8,128)S(1)}, f32[128,128]{1,0:T(8,128)S(1)}, u32[]{:S(2)}, u32[]{:S(2)}) collective-permute-start(f32[128,128]{1,0:T(8,128)S(1)} %get-tuple-element.47), channel_id=1, source_target_pairs={{1,0},{2,1},{3,2},{4,3},{5,4},{6,5},{7,6},{0,7},{9,8},{10,9},{11,1... | collective-permute-start | bytes 196616 | tf_op jit(solution)/shard_map/ppermute | solution.py:474
  149.2 3.6 %collective-permute-start.11 = (f32[32,128]{1,0:T(8,128)S(1)}, f32[32,128]{1,0:T(8,128)S(1)}, u32[]{:S(2)}, u32[]{:S(2)}) collective-permute-start(f32[32,128]{1,0:T(8,128)S(1)} %get-tuple-element.44), channel_id=1, source_target_pairs={{0,8},{8,16},{16,24},{1,9},{9,17},{17,25},{2,10},{10,18},{18,26},{... | collective-permute-start | bytes 49160 | tf_op jit(solution)/shard_map/ppermute | solution.py:471
  154.2 4.2 %collective-permute-done.12.refs_10_ = f32[32,128]{1,0:T(8,128)S(1)} collective-permute-done((f32[32,128]{1,0:T(8,128)S(1)}, f32[32,128]{1,0:T(8,128)S(1)}, u32[]{:S(2)}, u32[]{:S(2)}) %collective-permute-start.12) | collective-permute-done | bytes 16416 | tf_op jit(solution)/shard_map/ppermute | solution.py:472
  158.4 5.4 %shard_map.104 = (f32[6,8,128,128]{3,2,1,0:T(8,128)S(1)}, f32[32,128]{1,0:T(8,128)S(1)}, f32[32,128]{1,0:T(8,128)S(1)}, f32[128,128]{1,0:T(8,128)S(1)}, f32[128,128]{1,0:T(8,128)S(1)}) custom-call(f32[8]{0:T(128)S(1)} %copy-done.8, f32[2,8,128,128]{3,2,1,0:T(8,128)S(1)} %get-tuple-element.43.refs_1_, ...), custom_call_target="tpu_custom_call" | custom-call | flops 16000000 | bytes 9000000 | tf_op jit(solution)/shard_map/pallas_call | solution.py:479
  163.8 3.5 %collective-permute-start.18 = (f32[128,128]{1,0:T(8,128)S(1)}, f32[128,128]{1,0:T(8,128)S(1)}, u32[]{:S(2)}, u32[]{:S(2)}) collective-permute-start(f32[128,128]{1,0:T(8,128)S(1)} %get-tuple-element.52), channel_id=1, source_target_pairs={{1,0},{2,1},{3,2},{4,3},{5,4},{6,5},{7,6},{0,7},{9,8},{10,9},{11,1... | collective-permute-start | bytes 196616 | tf_op jit(solution)/shard_map/ppermute | solution.py:474
  167.4 3.6 %collective-permute-start.15 = (f32[32,128]{1,0:T(8,128)S(1)}, f32[32,128]{1,0:T(8,128)S(1)}, u32[]{:S(2)}, u32[]{:S(2)}) collective-permute-start(f32[32,128]{1,0:T(8,128)S(1)} %get-tuple-element.49), channel_id=1, source_target_pairs={{0,8},{8,16},{16,24},{1,9},{9,17},{17,25},{2,10},{10,18},{18,26},{... | collective-permute-start | bytes 49160 | tf_op jit(solution)/shard_map/ppermute | solution.py:471
  172.4 4.2 %collective-permute-done.16.refs_10_ = f32[32,128]{1,0:T(8,128)S(1)} collective-permute-done((f32[32,128]{1,0:T(8,128)S(1)}, f32[32,128]{1,0:T(8,128)S(1)}, u32[]{:S(2)}, u32[]{:S(2)}) %collective-permute-start.16) | collective-permute-done | bytes 16416 | tf_op jit(solution)/shard_map/ppermute | solution.py:472
  176.6 4.9 %shard_map.105 = f32[6,8,128,128]{3,2,1,0:T(8,128)} custom-call(f32[8]{0:T(128)S(1)} %copy-done.8, f32[6,8,128,128]{3,2,1,0:T(8,128)S(1)} %get-tuple-element.48.refs_1_.refs_2_.refs_3_, f32[6,8,128,128]{3,2,1,0:T(8,128)S(1)} %get-tuple-element.48.refs_1_.refs_2_.refs_3_, f32[6,8,128,128]{3,2,1,0:T(8,128)S(1)} %get-tuple-element.48.refs_1_.refs_2_.refs_3_, ...), custom_call_target="tpu_custom_call" | custom-call | flops 16000000 | bytes 9000000 | tf_op jit(solution)/shard_map/pallas_call | solution.py:479
  (55 shorter events, 7.7 us)
Async XLA Ops:
  0.0 0.9 copy-start.6
  4.6 31.3 %copy-start = (f32[48,128,128]{2,1,0:T(8,128)S(1)}, f32[48,128,128]{2,1,0:T(8,128)}, u32[]{:S(2)}) copy-start(f32[48,128,128]{2,1,0:T(8,128)} %param.9) | copy-start | bytes 9437188
  4.6 31.3 %copy-start.3 = (f32[128,128]{1,0:T(8,128)S(1)}, f32[128,128]{1,0:T(8,128)}, u32[]{:S(2)}) copy-start(f32[128,128]{1,0:T(8,128)} %refs_5_.5) | copy-start | bytes 196612
  32.1 14.4 %copy-start.13 = (f32[1096,128]{1,0:T(8,128)S(1)}, f32[1096,128]{1,0:T(8,128)}, u32[]{:S(2)}) copy-start(f32[1096,128]{1,0:T(8,128)} %get-tuple-element.42.refs_0_) | copy-start | bytes 1683460
  32.1 36.6 %collective-permute-start.10 = (f32[1096,128]{1,0:T(8,128)}, f32[1096,128]{1,0:T(8,128)}, u32[]{:S(2)}, u32[]{:S(2)}) collective-permute-start(f32[1096,128]{1,0:T(8,128)} %get-tuple-element.41), channel_id=1, source_target_pairs={{0,4},{1,5},{2,6},{3,7},{4,0},{5,1},{6,2},{7,3},{8,12},{9,13},{10,... | collective-permute-start | bytes 1683464 | tf_op jit(solution)/shard_map/ppermute | solution.py:551
  38.0 12.9 %collective-permute-start.2 = (f32[128,128]{1,0:T(8,128)}, f32[128,128]{1,0:T(8,128)S(1)}, u32[]{:S(2)}, u32[]{:S(2)}) collective-permute-start(f32[128,128]{1,0:T(8,128)} %get-tuple-element.31), channel_id=1, source_target_pairs={{0,1},{1,2},{2,3},{3,4},{4,5},{5,6},{6,7},{7,0},{8,9},{9,10},{10,1... | collective-permute-start | bytes 196616 | tf_op jit(solution)/shard_map/ppermute | solution.py:473
  38.0 24.9 %collective-permute-start.3 = (f32[128,128]{1,0:T(8,128)}, f32[128,128]{1,0:T(8,128)S(1)}, u32[]{:S(2)}, u32[]{:S(2)}) collective-permute-start(f32[128,128]{1,0:T(8,128)} %get-tuple-element.32), channel_id=1, source_target_pairs={{1,0},{2,1},{3,2},{4,3},{5,4},{6,5},{7,6},{0,7},{9,8},{10,9},{11,1... | collective-permute-start | bytes 196616 | tf_op jit(solution)/shard_map/ppermute | solution.py:474
  41.6 8.8 %collective-permute-start = (f32[32,128]{1,0:T(8,128)S(1)}, f32[32,128]{1,0:T(8,128)S(1)}, u32[]{:S(2)}, u32[]{:S(2)}) collective-permute-start(f32[32,128]{1,0:T(8,128)S(1)} %get-tuple-element.29), channel_id=1, source_target_pairs={{0,8},{8,16},{16,24},{1,9},{9,17},{17,25},{2,10},{10,18},{18,26},{... | collective-permute-start | bytes 49160 | tf_op jit(solution)/shard_map/ppermute | solution.py:471
  45.3 5.6 %collective-permute-start.1 = (f32[32,128]{1,0:T(8,128)S(1)}, f32[32,128]{1,0:T(8,128)S(1)}, u32[]{:S(2)}, u32[]{:S(2)}) collective-permute-start(f32[32,128]{1,0:T(8,128)S(1)} %get-tuple-element.30), channel_id=1, source_target_pairs={{8,0},{16,8},{24,16},{9,1},{17,9},{25,17},{10,2},{18,10},{26,18},{... | collective-permute-start | bytes 49160 | tf_op jit(solution)/shard_map/ppermute | solution.py:472
  46.6 16.4 %copy-start.4 = (s32[128,128]{1,0:T(8,128)S(1)}, s32[128,128]{1,0:T(8,128)}, u32[]{:S(2)}) copy-start(s32[128,128]{1,0:T(8,128)} %refs_7_.5) | copy-start | bytes 196612
  46.6 16.4 %copy-start.5 = (f32[128,128]{1,0:T(8,128)S(1)}, f32[128,128]{1,0:T(8,128)}, u32[]{:S(2)}) copy-start(f32[128,128]{1,0:T(8,128)} %refs_6_.5) | copy-start | bytes 196612
  46.6 16.4 %copy-start.8 = (f32[8]{0:T(128)S(1)}, f32[8]{0:T(128)}, u32[]{:S(2)}) copy-start(f32[8]{0:T(128)} %constant.18.clone.refs_0_.omega_ref) | copy-start | bytes 100
  49.4 1.0 copy-start.11
  50.4 24.0 %collective-permute-start.9 = (f32[1096,128]{1,0:T(8,128)}, f32[1096,128]{1,0:T(8,128)S(1)}, u32[]{:S(2)}, u32[]{:S(2)}) collective-permute-start(f32[1096,128]{1,0:T(8,128)} %get-tuple-element.40), channel_id=1, source_target_pairs={{0,1},{1,0},{2,3},{3,2},{4,5},{5,4},{6,7},{7,6},{8,9},{9,8},{10,11... | collective-permute-start | bytes 1683464 | tf_op jit(solution)/shard_map/ppermute | solution.py:551
  50.9 34.7 %collective-permute-start.8 = (f32[1096,128]{1,0:T(8,128)}, f32[1096,128]{1,0:T(8,128)S(1)}, u32[]{:S(2)}, u32[]{:S(2)}) collective-permute-start(f32[1096,128]{1,0:T(8,128)} %get-tuple-element.39), channel_id=1, source_target_pairs={{0,2},{1,3},{2,0},{3,1},{4,6},{5,7},{6,4},{7,5},{8,10},{9,11},{10,... | collective-permute-start | bytes 1683464 | tf_op jit(solution)/shard_map/ppermute | solution.py:551
  50.9 70.7 %collective-permute-start.7 = (f32[1096,128]{1,0:T(8,128)}, f32[1096,128]{1,0:T(8,128)S(1)}, u32[]{:S(2)}, u32[]{:S(2)}) collective-permute-start(f32[1096,128]{1,0:T(8,128)} %get-tuple-element.38), channel_id=1, source_target_pairs={{0,3},{1,2},{2,1},{3,0},{4,7},{5,6},{6,5},{7,4},{8,11},{9,10},{10,... | collective-permute-start | bytes 1683464 | tf_op jit(solution)/shard_map/ppermute | solution.py:551
  62.9 60.9 %collective-permute-start.6 = (f32[1096,128]{1,0:T(8,128)}, f32[1096,128]{1,0:T(8,128)S(1)}, u32[]{:S(2)}, u32[]{:S(2)}) collective-permute-start(f32[1096,128]{1,0:T(8,128)} %get-tuple-element.37), channel_id=1, source_target_pairs={{0,5},{1,4},{2,7},{3,6},{4,1},{5,0},{6,3},{7,2},{8,13},{9,12},{10,... | collective-permute-start | bytes 1683464 | tf_op jit(solution)/shard_map/ppermute | solution.py:551
  63.0 1.9 %copy-start.1 = (f32[48,128,128]{2,1,0:T(8,128)S(1)}, f32[48,128,128]{2,1,0:T(8,128)}, u32[]{:S(2)}) copy-start(f32[48,128,128]{2,1,0:T(8,128)} %param.10) | copy-start | bytes 9437188
  64.9 3.8 %copy-start.15 = (f32[1096,128]{1,0:T(8,128)S(1)}, f32[1096,128]{1,0:T(8,128)}, u32[]{:S(2)}) copy-start(f32[1096,128]{1,0:T(8,128)} %get-tuple-element.36) | copy-start | bytes 1683460
  64.9 6.3 %copy-start.12 = (f32[16,64,256]{2,1,0:T(8,128)S(1)}, f32[16,64,256]{2,1,0:T(8,128)}, u32[]{:S(2)}) copy-start(f32[16,64,256]{2,1,0:T(8,128)} %copy-done.11) | copy-start | bytes 3145732
  68.7 5.7 %copy-start.14 = (f32[1096,128]{1,0:T(8,128)S(1)}, f32[1096,128]{1,0:T(8,128)}, u32[]{:S(2)}) copy-start(f32[1096,128]{1,0:T(8,128)} %get-tuple-element.35) | copy-start | bytes 1683460
  68.8 57.1 %collective-permute-start.5 = (f32[1096,128]{1,0:T(8,128)S(1)}, f32[1096,128]{1,0:T(8,128)S(1)}, u32[]{:S(2)}, u32[]{:S(2)}) collective-permute-start(f32[1096,128]{1,0:T(8,128)S(1)} %copy-done.15), channel_id=1, source_target_pairs={{0,6},{1,7},{2,4},{3,5},{4,2},{5,3},{6,0},{7,1},{8,14},{9,15},{10,... | collective-permute-start | bytes 1683464 | tf_op jit(solution)/shard_map/ppermute | solution.py:551
  74.4 53.6 %collective-permute-start.4 = (f32[1096,128]{1,0:T(8,128)S(1)}, f32[1096,128]{1,0:T(8,128)S(1)}, u32[]{:S(2)}, u32[]{:S(2)}) collective-permute-start(f32[1096,128]{1,0:T(8,128)S(1)} %copy-done.14), channel_id=1, source_target_pairs={{0,7},{1,6},{2,5},{3,4},{4,3},{5,2},{6,1},{7,0},{8,15},{9,14},{10,... | collective-permute-start | bytes 1683464 | tf_op jit(solution)/shard_map/ppermute | solution.py:551
  130.4 28.0 %copy-start.2 = (f32[48,128,128]{2,1,0:T(8,128)S(1)}, f32[48,128,128]{2,1,0:T(8,128)}, u32[]{:S(2)}) copy-start(f32[48,128,128]{2,1,0:T(8,128)} %param.10) | copy-start | bytes 9437188
  132.5 25.8 %collective-permute-start.13 = (f32[128,128]{1,0:T(8,128)S(1)}, f32[128,128]{1,0:T(8,128)S(1)}, u32[]{:S(2)}, u32[]{:S(2)}) collective-permute-start(f32[128,128]{1,0:T(8,128)S(1)} %get-tuple-element.46), channel_id=1, source_target_pairs={{0,1},{1,2},{2,3},{3,4},{4,5},{5,6},{6,7},{7,0},{8,9},{9,10},{10,1... | collective-permute-start | bytes 196616 | tf_op jit(solution)/shard_map/ppermute | solution.py:473
  134.7 23.7 %collective-permute-start.14 = (f32[128,128]{1,0:T(8,128)S(1)}, f32[128,128]{1,0:T(8,128)S(1)}, u32[]{:S(2)}, u32[]{:S(2)}) collective-permute-start(f32[128,128]{1,0:T(8,128)S(1)} %get-tuple-element.47), channel_id=1, source_target_pairs={{1,0},{2,1},{3,2},{4,3},{5,4},{6,5},{7,6},{0,7},{9,8},{10,9},{11,1... | collective-permute-start | bytes 196616 | tf_op jit(solution)/shard_map/ppermute | solution.py:474
  149.2 5.0 %collective-permute-start.11 = (f32[32,128]{1,0:T(8,128)S(1)}, f32[32,128]{1,0:T(8,128)S(1)}, u32[]{:S(2)}, u32[]{:S(2)}) collective-permute-start(f32[32,128]{1,0:T(8,128)S(1)} %get-tuple-element.44), channel_id=1, source_target_pairs={{0,8},{8,16},{16,24},{1,9},{9,17},{17,25},{2,10},{10,18},{18,26},{... | collective-permute-start | bytes 49160 | tf_op jit(solution)/shard_map/ppermute | solution.py:471
  152.7 5.6 %collective-permute-start.12 = (f32[32,128]{1,0:T(8,128)S(1)}, f32[32,128]{1,0:T(8,128)S(1)}, u32[]{:S(2)}, u32[]{:S(2)}) collective-permute-start(f32[32,128]{1,0:T(8,128)S(1)} %get-tuple-element.45), channel_id=1, source_target_pairs={{8,0},{16,8},{24,16},{9,1},{17,9},{25,17},{10,2},{18,10},{26,18},{... | collective-permute-start | bytes 49160 | tf_op jit(solution)/shard_map/ppermute | solution.py:472
  163.8 12.8 %collective-permute-start.17 = (f32[128,128]{1,0:T(8,128)S(1)}, f32[128,128]{1,0:T(8,128)S(1)}, u32[]{:S(2)}, u32[]{:S(2)}) collective-permute-start(f32[128,128]{1,0:T(8,128)S(1)} %get-tuple-element.51), channel_id=1, source_target_pairs={{0,1},{1,2},{2,3},{3,4},{4,5},{5,6},{6,7},{7,0},{8,9},{9,10},{10,1... | collective-permute-start | bytes 196616 | tf_op jit(solution)/shard_map/ppermute | solution.py:473
  163.8 12.8 %collective-permute-start.18 = (f32[128,128]{1,0:T(8,128)S(1)}, f32[128,128]{1,0:T(8,128)S(1)}, u32[]{:S(2)}, u32[]{:S(2)}) collective-permute-start(f32[128,128]{1,0:T(8,128)S(1)} %get-tuple-element.52), channel_id=1, source_target_pairs={{1,0},{2,1},{3,2},{4,3},{5,4},{6,5},{7,6},{0,7},{9,8},{10,9},{11,1... | collective-permute-start | bytes 196616 | tf_op jit(solution)/shard_map/ppermute | solution.py:474
  167.4 5.0 %collective-permute-start.15 = (f32[32,128]{1,0:T(8,128)S(1)}, f32[32,128]{1,0:T(8,128)S(1)}, u32[]{:S(2)}, u32[]{:S(2)}) collective-permute-start(f32[32,128]{1,0:T(8,128)S(1)} %get-tuple-element.49), channel_id=1, source_target_pairs={{0,8},{8,16},{16,24},{1,9},{9,17},{17,25},{2,10},{10,18},{18,26},{... | collective-permute-start | bytes 49160 | tf_op jit(solution)/shard_map/ppermute | solution.py:471
  171.0 5.6 %collective-permute-start.16 = (f32[32,128]{1,0:T(8,128)S(1)}, f32[32,128]{1,0:T(8,128)S(1)}, u32[]{:S(2)}, u32[]{:S(2)}) collective-permute-start(f32[32,128]{1,0:T(8,128)S(1)} %get-tuple-element.50), channel_id=1, source_target_pairs={{8,0},{16,8},{24,16},{9,1},{17,9},{25,17},{10,2},{18,10},{26,18},{... | collective-permute-start | bytes 49160 | tf_op jit(solution)/shard_map/ppermute | solution.py:472
  (3 other events, 2.3 us)

commit v5 on v4

--- a/solution.py
+++ b/solution.py
@@ -35,8 +35,7 @@
     return pl.CostEstimate(flops=flops, bytes_accessed=nbytes, transcendentals=0)
 
 
-def rank_kernel(tiles, cuts, group, dest_ref, cell_ref, *outs):
-    slot_ref, table_ref = outs
+def rank(tiles, cuts, group, dest_ref, cell_ref, slot_ref, table_ref):
     blocks, block = dest_ref.shape[0] // 2, BLOCK
 
     def lines(ref):
@@ -84,10 +83,11 @@
     table_ref[3 * blocks :, :] = total.astype(jnp.int32)
 
 
-def bucket_kernel(tiles, cuts, capacity, width, group, table_ref, *refs):
-    slot_ref, cell_ref, rows_any = refs[:3]
+def bucket_kernel(tiles, cuts, capacity, width, group, *refs):
+    dest_ref, cell_ref, rows_any = refs[:3]
     outs = refs[3 : 3 + tiles]
-    staged, held, turned, rows_ref, read_sem, write_sem = refs[3 + tiles :]
+    staged, held, turned, rows_ref, slot_ref, table_held, table_ref = refs[3 + tiles : 10 + tiles]
+    read_sem, write_sem, table_sem = refs[10 + tiles :]
     keys = tiles * cuts
     blocks = slot_ref.shape[0]
     windows = capacity // LANES
@@ -158,9 +158,13 @@
     ]
     for read in reads:
         read.start()
+    rank(tiles, cuts, group, dest_ref, cell_ref, slot_ref, table_held)
+    tabled = pltpu.make_async_copy(table_held, table_ref, table_sem)
+    tabled.start()
+    tabled.wait()
     for part in range(blocks // group):
         reads[part].wait()
-        lax.fori_loop(0, group, permute, part * group, unroll=16)
+        lax.fori_loop(0, group, permute, part * group, unroll=32)
         lax.fori_loop(0, group, spread, part * group, unroll=4)
 
         @pl.when(table_ref[3 * blocks + 1, part] > chunk)
@@ -493,17 +497,6 @@
         )
         return out[0], out[1:]
 
-    slot, table = pl.pallas_call(
-        functools.partial(rank_kernel, tiles, cuts, group),
-        in_specs=[VMEM, VMEM],
-        out_specs=[VMEM] * 2,
-        out_shape=[
-            jax.ShapeDtypeStruct((blocks, BLOCK), jnp.int32),
-            jax.ShapeDtypeStruct((3 * blocks + 8, LANES), jnp.int32),
-        ],
-        compiler_params=params(32),
-    )(dest_tile.reshape(2 * blocks, LANES), cells)
-
     strips = pl.pallas_call(
         functools.partial(edges_kernel, per, chunk_rows),
         grid=(consts // per,),
@@ -518,7 +511,7 @@
 
     buckets = pl.pallas_call(
         functools.partial(bucket_kernel, tiles, cuts, capacity, width, group),
-        in_specs=[SMEM, VMEM, VMEM, ANY],
+        in_specs=[VMEM, VMEM, ANY],
         out_specs=[ANY] * tiles,
         out_shape=[jax.ShapeDtypeStruct((bucket_rows, LANES), f32)] * tiles,
         scratch_shapes=[
@@ -526,12 +519,16 @@
             pltpu.VMEM((tiles * (capacity + BLOCK), LANES), f32),
             pltpu.VMEM((tiles, bucket_rows, LANES), f32),
             pltpu.VMEM((width, row_count), f32),
+            pltpu.VMEM((blocks, BLOCK), jnp.int32),
+            pltpu.VMEM((3 * blocks + 8, LANES), jnp.int32),
+            pltpu.SMEM((3 * blocks + 8, LANES), jnp.int32),
             pltpu.SemaphoreType.DMA((blocks // group,)),
             pltpu.SemaphoreType.DMA((tiles,)),
+            pltpu.SemaphoreType.DMA,
         ],
         compiler_params=params(60),
         cost_estimate=cost(10**10, 7 * 10**6),
-    )(table, slot, cells, residual_rows)
+    )(dest_tile.reshape(2 * blocks, LANES), cells, residual_rows)
 
     grid_shape = jax.ShapeDtypeStruct((width, height // 2, 2 * across), f32)
 

time: 179 us -> 173 us (0.966); the launches traced: 181 us -> 173 us
  starting transfers between devices: 62.8 us -> 44.8 us
  Pallas kernels: 66.6 us -> 80.4 us
  local copies, waits for them, and re-layouts: 6.13 us -> 2.97 us
    pallas_call x8, Pallas kernels: 19.4 us -> 34.1 us  [add(): pl.pallas_call(functools.partial(sum_kernel, width, windows, len(parts),...]
    ppermute x3, starting transfers between devices: 21.6 us -> 11 us  [exchange(): lax.ppermute(west, 'lon', [((i + 1) % tiles, i) for i in range(tiles)])]
    ppermute x7, starting transfers between devices: 24.3 us -> 19 us  [local(): lax.ppermute(buckets[s], 'lon', [(i, i ^ s) for i in range(tiles)])]
    unnamed x32 -> x24, local copies, waits for them, and re-layouts: 6.06 us -> 2.9 us
    ppermute x3, starting transfers between devices: 2.19 us -> 0.12 us  [exchange(): lax.ppermute(east, 'lon', [(i, (i + 1) % tiles) for i in range(tiles)])]
  transfers between devices with their start and end apart: 19 -> 19, of which waited for: 7 -> 6; matrix products, arithmetic and copies ran while one was open for 0% -> 0% of each run, Pallas kernels for 13% -> 21%
where the time goes in v5:
time: 173 us
  Pallas kernels  80.4 us (46%)
  waiting for transfers between devices  44.9 us (26%)
  starting transfers between devices  44.8 us (26%)
  local copies, waits for them, and re-layouts  2.97 us (2%)
    ppermute x7, waiting for transfers between devices, local(): lax.ppermute(buckets[s], 'lon', [(i, i ^ s) for i in range(tiles)])  36.2 us
    pallas_call x8, Pallas kernels, add(): pl.pallas_call(functools.partial(sum_kernel, width, windows, len(parts),...  34.1 us
    pallas_call x1, Pallas kernels, local(): pl.pallas_call(functools.partial(bucket_kernel, tiles, cuts, capacity, wi...  28 us
    ppermute x7, starting transfers between devices, local(): lax.ppermute(buckets[s], 'lon', [(i, i ^ s) for i in range(tiles)])  19 us
    pallas_call x3, Pallas kernels, sweep(): pl.pallas_call(functools.partial(sweep_kernel, per, chunk_rows, forced, e...  14.1 us
    ppermute x3, starting transfers between devices, exchange(): lax.ppermute(west, 'lon', [((i + 1) % tiles, i) for i in range(tiles)])  11 us
    ppermute x3, starting transfers between devices, exchange(): lax.ppermute(south, 'lat', [(i, i + 1) for i in range(lats - 1)])  10.8 us
    ppermute x3, waiting for transfers between devices, exchange(): lax.ppermute(north, 'lat', [(i + 1, i) for i in range(lats - 1)])  8.42 us
  transfers between devices with their start and end apart: 19, of which 6 were waited for; matrix products, arithmetic and copies ran while one was open for 0% of the time, Pallas kernels for 21%

profile of v5, /device:TPU:0, one launch (start us, length us, event | category | flops | bytes accessed | tf_op | source)
XLA Modules:
  0.0 173.5 jit_solution(10473999361454153838)
XLA Ops:
  0.0 28.0 %shard_map.93 = (f32[1096,128]{1,0:T(8,128)}, f32[1096,128]{1,0:T(8,128)}, f32[1096,128]{1,0:T(8,128)}, f32[1096,128]{1,0:T(8,128)}, f32[1096,128]{1,0:T(8,128)}...) custom-call(s32[256,128]{1,0:T(8,128)} %bitcast.12, s32[256,128]{1,0:T(8,128)} %bitcast.13, ...), custom_call_target="tpu_custom_call" | custom-call | flops 10000000000 | bytes 7000000 | tf_op jit(solution)/shard_map/pallas_call | solution.py:512
  28.0 4.1 %collective-permute-start.10 = (f32[1096,128]{1,0:T(8,128)}, f32[1096,128]{1,0:T(8,128)}, u32[]{:S(2)}, u32[]{:S(2)}) collective-permute-start(f32[1096,128]{1,0:T(8,128)} %get-tuple-element.37), channel_id=1, source_target_pairs={{0,4},{1,5},{2,6},{3,7},{4,0},{5,1},{6,2},{7,3},{8,12},{9,13},{10,... | collective-permute-start | bytes 1683464 | tf_op jit(solution)/shard_map/ppermute | solution.py:548
  32.1 2.1 %shard_map.91 = (f32[32,128]{1,0:T(8,128)S(1)}, f32[32,128]{1,0:T(8,128)S(1)}, f32[128,128]{1,0:T(8,128)}, f32[128,128]{1,0:T(8,128)}) custom-call(f32[6,8,128,128]{3,2,1,0:T(8,128)S(1)} %bitcast.5, f32[128,128]{1,0:T(8,128)S(1)} %copy-done.3), custom_call_target="tpu_custom_call" | custom-call | flops 1000000 | bytes 3000000 | tf_op jit(solution)/shard_map/pallas_call | solution.py:500
  34.2 3.5 %collective-permute-start.3 = (f32[128,128]{1,0:T(8,128)}, f32[128,128]{1,0:T(8,128)S(1)}, u32[]{:S(2)}, u32[]{:S(2)}) collective-permute-start(f32[128,128]{1,0:T(8,128)} %get-tuple-element.30), channel_id=1, source_target_pairs={{1,0},{2,1},{3,2},{4,3},{5,4},{6,5},{7,6},{0,7},{9,8},{10,9},{11,1... | collective-permute-start | bytes 196616 | tf_op jit(solution)/shard_map/ppermute | solution.py:478
  37.8 3.4 %collective-permute-start = (f32[32,128]{1,0:T(8,128)S(1)}, f32[32,128]{1,0:T(8,128)S(1)}, u32[]{:S(2)}, u32[]{:S(2)}) collective-permute-start(f32[32,128]{1,0:T(8,128)S(1)} %get-tuple-element.27), channel_id=1, source_target_pairs={{0,8},{8,16},{16,24},{1,9},{9,17},{17,25},{2,10},{10,18},{18,26},{... | collective-permute-start | bytes 49160 | tf_op jit(solution)/shard_map/ppermute | solution.py:475
  41.1 1.3 collective-permute-start.1
  42.5 4.3 %shard_map.94.refs_1_ = f32[16,64,256]{2,1,0:T(8,128)S(1)} custom-call(f32[1096,128]{1,0:T(8,128)S(1)} %copy-done.9), custom_call_target="tpu_custom_call" | custom-call | flops 10000000000 | bytes 3000000 | tf_op jit(solution)/shard_map/pallas_call | solution.py:536
  48.0 11.2 %collective-permute-start.7 = (f32[1096,128]{1,0:T(8,128)}, f32[1096,128]{1,0:T(8,128)S(1)}, u32[]{:S(2)}, u32[]{:S(2)}) collective-permute-start(f32[1096,128]{1,0:T(8,128)} %get-tuple-element.34), channel_id=1, source_target_pairs={{0,3},{1,2},{2,1},{3,0},{4,7},{5,6},{6,5},{7,4},{8,11},{9,10},{10,... | collective-permute-start | bytes 1683464 | tf_op jit(solution)/shard_map/ppermute | solution.py:548
  59.3 1.9 %copy-done.1 = f32[48,128,128]{2,1,0:T(8,128)S(1)} copy-done((f32[48,128,128]{2,1,0:T(8,128)S(1)}, f32[48,128,128]{2,1,0:T(8,128)}, u32[]{:S(2)}) %copy-start.1) | copy-done | bytes 3145752
  61.2 3.8 %shard_map.92.eta_ref.east_ref.north_ref.refs_2_.refs_3_ = f32[6,8,128,128]{3,2,1,0:T(8,128)S(1)} custom-call(f32[8]{0:T(128)S(1)} %copy-done.6, f32[6,8,128,128]{3,2,1,0:T(8,128)S(1)} %bitcast.6, f32[6,8,128,128]{3,2,1,0:T(8,128)S(1)} %bitcast.7, f32[6,8,128,128]{3,2,1,0:T(8,128)S(1)} %bitcast.8, f32[6,8,128,128]{3,2,1,0:T(8,128)S(1)} %bitcast.9, ...), custom_call_target="tpu_custom_call" | custom-call | flops 16000000 | bytes 9000000 | tf_op jit(solution)/shard_map/pallas_call | solution.py:483
  65.0 2.4 %collective-permute-start.5 = (f32[1096,128]{1,0:T(8,128)S(1)}, f32[1096,128]{1,0:T(8,128)S(1)}, u32[]{:S(2)}, u32[]{:S(2)}) collective-permute-start(f32[1096,128]{1,0:T(8,128)S(1)} %copy-done.11), channel_id=1, source_target_pairs={{0,6},{1,7},{2,4},{3,5},{4,2},{5,3},{6,0},{7,1},{8,14},{9,15},{10,... | collective-permute-start | bytes 1683464 | tf_op jit(solution)/shard_map/ppermute | solution.py:548
  67.5 5.2 %shard_map.95.refs_1_ = f32[16,64,256]{2,1,0:T(8,128)S(1)} custom-call(f32[1096,128]{1,0:T(8,128)} %collective-permute-done.10.refs_0_, f32[16,64,256]{2,1,0:T(8,128)S(1)} %copy-done.8), custom_call_target="tpu_custom_call" | custom-call | flops 10000000000 | bytes 3000000 | tf_op jit(solution)/shard_map/pallas_call | solution.py:536
  72.7 1.1 collective-permute-start.4
  73.8 4.1 %shard_map.96.refs_1_ = f32[16,64,256]{2,1,0:T(8,128)S(1)} custom-call(f32[1096,128]{1,0:T(8,128)S(1)} %collective-permute-done.9.refs_0_, f32[16,64,256]{2,1,0:T(8,128)S(1)} %shard_map.95.refs_1_), custom_call_target="tpu_custom_call" | custom-call | flops 10000000000 | bytes 3000000 | tf_op jit(solution)/shard_map/pallas_call | solution.py:536
  77.9 3.3 %collective-permute-done.8.refs_0_ = f32[1096,128]{1,0:T(8,128)S(1)} collective-permute-done((f32[1096,128]{1,0:T(8,128)}, f32[1096,128]{1,0:T(8,128)S(1)}, u32[]{:S(2)}, u32[]{:S(2)}) %collective-permute-start.8) | collective-permute-done | bytes 561184 | tf_op jit(solution)/shard_map/ppermute | solution.py:548
  81.2 4.1 %shard_map.97.refs_1_ = f32[16,64,256]{2,1,0:T(8,128)S(1)} custom-call(f32[1096,128]{1,0:T(8,128)S(1)} %collective-permute-done.8.refs_0_, f32[16,64,256]{2,1,0:T(8,128)S(1)} %shard_map.96.refs_1_), custom_call_target="tpu_custom_call" | custom-call | flops 10000000000 | bytes 3000000 | tf_op jit(solution)/shard_map/pallas_call | solution.py:536
  85.2 32.9 %collective-permute-done.7.refs_0_ = f32[1096,128]{1,0:T(8,128)S(1)} collective-permute-done((f32[1096,128]{1,0:T(8,128)}, f32[1096,128]{1,0:T(8,128)S(1)}, u32[]{:S(2)}, u32[]{:S(2)}) %collective-permute-start.7) | collective-permute-done | bytes 561184 | tf_op jit(solution)/shard_map/ppermute | solution.py:548
  118.1 4.1 %shard_map.98.refs_1_ = f32[16,64,256]{2,1,0:T(8,128)S(1)} custom-call(f32[1096,128]{1,0:T(8,128)S(1)} %collective-permute-done.7.refs_0_, f32[16,64,256]{2,1,0:T(8,128)S(1)} %shard_map.97.refs_1_), custom_call_target="tpu_custom_call" | custom-call | flops 10000000000 | bytes 3000000 | tf_op jit(solution)/shard_map/pallas_call | solution.py:536
  122.2 4.1 %shard_map.99.refs_1_ = f32[16,64,256]{2,1,0:T(8,128)S(1)} custom-call(f32[1096,128]{1,0:T(8,128)S(1)} %collective-permute-done.6.refs_0_, f32[16,64,256]{2,1,0:T(8,128)S(1)} %shard_map.98.refs_1_), custom_call_target="tpu_custom_call" | custom-call | flops 10000000000 | bytes 3000000 | tf_op jit(solution)/shard_map/pallas_call | solution.py:536
  126.3 4.3 %shard_map.100.refs_1_ = f32[16,64,256]{2,1,0:T(8,128)S(1)} custom-call(f32[1096,128]{1,0:T(8,128)S(1)} %collective-permute-done.5.refs_0_, f32[16,64,256]{2,1,0:T(8,128)S(1)} %shard_map.99.refs_1_), custom_call_target="tpu_custom_call" | custom-call | flops 10000000000 | bytes 3000000 | tf_op jit(solution)/shard_map/pallas_call | solution.py:536
  130.6 4.1 %shard_map.101.re_ref.im_ref.refs_13_.refs_14_ = f32[16,64,256]{2,1,0:T(8,128)S(1)} custom-call(f32[1096,128]{1,0:T(8,128)S(1)} %collective-permute-done.4.refs_0_, f32[16,64,256]{2,1,0:T(8,128)S(1)} %shard_map.100.refs_1_), custom_call_target="tpu_custom_call" | custom-call | flops 10000000000 | bytes 3000000 | tf_op jit(solution)/shard_map/pallas_call | solution.py:536
  134.7 2.2 %shard_map.102 = (f32[2,8,128,128]{3,2,1,0:T(8,128)S(1)}, f32[32,128]{1,0:T(8,128)S(1)}, f32[32,128]{1,0:T(8,128)S(1)}, f32[128,128]{1,0:T(8,128)S(1)}, f32[128,128]{1,0:T(8,128)S(1)}) custom-call(f32[8]{0:T(128)S(1)} %copy-done.6, f32[6,8,128,128]{3,2,1,0:T(8,128)S(1)} %shard_map.92.eta_ref.east_ref.north_ref.refs_2_.refs_3_, ...), custom_call_target="tpu_custom_call" | custom-call | flops 1000000 | bytes 6000000 | tf_op jit(solution)/shard_map/pallas_call | solution.py:556
  136.9 3.5 %collective-permute-start.14 = (f32[128,128]{1,0:T(8,128)S(1)}, f32[128,128]{1,0:T(8,128)S(1)}, u32[]{:S(2)}, u32[]{:S(2)}) collective-permute-start(f32[128,128]{1,0:T(8,128)S(1)} %get-tuple-element.43), channel_id=1, source_target_pairs={{1,0},{2,1},{3,2},{4,3},{5,4},{6,5},{7,6},{0,7},{9,8},{10,9},{11,1... | collective-permute-start | bytes 196616 | tf_op jit(solution)/shard_map/ppermute | solution.py:478
  140.5 2.9 %collective-permute-start.11 = (f32[32,128]{1,0:T(8,128)S(1)}, f32[32,128]{1,0:T(8,128)S(1)}, u32[]{:S(2)}, u32[]{:S(2)}) collective-permute-start(f32[32,128]{1,0:T(8,128)S(1)} %get-tuple-element.40), channel_id=1, source_target_pairs={{0,8},{8,16},{16,24},{1,9},{9,17},{17,25},{2,10},{10,18},{18,26},{... | collective-permute-start | bytes 49160 | tf_op jit(solution)/shard_map/ppermute | solution.py:475
  143.4 1.3 collective-permute-start.12
  144.8 4.2 %collective-permute-done.12.refs_10_ = f32[32,128]{1,0:T(8,128)S(1)} collective-permute-done((f32[32,128]{1,0:T(8,128)S(1)}, f32[32,128]{1,0:T(8,128)S(1)}, u32[]{:S(2)}, u32[]{:S(2)}) %collective-permute-start.12) | collective-permute-done | bytes 16416 | tf_op jit(solution)/shard_map/ppermute | solution.py:476
  149.0 5.4 %shard_map.103 = (f32[6,8,128,128]{3,2,1,0:T(8,128)S(1)}, f32[32,128]{1,0:T(8,128)S(1)}, f32[32,128]{1,0:T(8,128)S(1)}, f32[128,128]{1,0:T(8,128)S(1)}, f32[128,128]{1,0:T(8,128)S(1)}) custom-call(f32[8]{0:T(128)S(1)} %copy-done.6, f32[2,8,128,128]{3,2,1,0:T(8,128)S(1)} %get-tuple-element.39.refs_1_, ...), custom_call_target="tpu_custom_call" | custom-call | flops 16000000 | bytes 9000000 | tf_op jit(solution)/shard_map/pallas_call | solution.py:483
  154.5 4.0 %collective-permute-start.18 = (f32[128,128]{1,0:T(8,128)S(1)}, f32[128,128]{1,0:T(8,128)S(1)}, u32[]{:S(2)}, u32[]{:S(2)}) collective-permute-start(f32[128,128]{1,0:T(8,128)S(1)} %get-tuple-element.48), channel_id=1, source_target_pairs={{1,0},{2,1},{3,2},{4,3},{5,4},{6,5},{7,6},{0,7},{9,8},{10,9},{11,1... | collective-permute-start | bytes 196616 | tf_op jit(solution)/shard_map/ppermute | solution.py:478
  158.4 4.5 %collective-permute-start.15 = (f32[32,128]{1,0:T(8,128)S(1)}, f32[32,128]{1,0:T(8,128)S(1)}, u32[]{:S(2)}, u32[]{:S(2)}) collective-permute-start(f32[32,128]{1,0:T(8,128)S(1)} %get-tuple-element.45), channel_id=1, source_target_pairs={{0,8},{8,16},{16,24},{1,9},{9,17},{17,25},{2,10},{10,18},{18,26},{... | collective-permute-start | bytes 49160 | tf_op jit(solution)/shard_map/ppermute | solution.py:475
  163.0 1.3 collective-permute-start.16
  164.4 4.2 %collective-permute-done.16.refs_10_ = f32[32,128]{1,0:T(8,128)S(1)} collective-permute-done((f32[32,128]{1,0:T(8,128)S(1)}, f32[32,128]{1,0:T(8,128)S(1)}, u32[]{:S(2)}, u32[]{:S(2)}) %collective-permute-start.16) | collective-permute-done | bytes 16416 | tf_op jit(solution)/shard_map/ppermute | solution.py:476
  168.6 4.9 %shard_map.104 = f32[6,8,128,128]{3,2,1,0:T(8,128)} custom-call(f32[8]{0:T(128)S(1)} %copy-done.6, f32[6,8,128,128]{3,2,1,0:T(8,128)S(1)} %get-tuple-element.44.refs_1_.refs_2_.refs_3_, f32[6,8,128,128]{3,2,1,0:T(8,128)S(1)} %get-tuple-element.44.refs_1_.refs_2_.refs_3_, f32[6,8,128,128]{3,2,1,0:T(8,128)S(1)} %get-tuple-element.44.refs_1_.refs_2_.refs_3_, ...), custom_call_target="tpu_custom_call" | custom-call | flops 16000000 | bytes 9000000 | tf_op jit(solution)/shard_map/pallas_call | solution.py:483
  (46 shorter events, 1.7 us)
Async XLA Ops:
  0.0 32.1 %copy-start = (f32[48,128,128]{2,1,0:T(8,128)S(1)}, f32[48,128,128]{2,1,0:T(8,128)}, u32[]{:S(2)}) copy-start(f32[48,128,128]{2,1,0:T(8,128)} %param.9) | copy-start | bytes 9437188
  0.0 32.1 %copy-start.3 = (f32[128,128]{1,0:T(8,128)S(1)}, f32[128,128]{1,0:T(8,128)}, u32[]{:S(2)}) copy-start(f32[128,128]{1,0:T(8,128)} %refs_5_.5) | copy-start | bytes 196612
  28.0 14.5 %copy-start.9 = (f32[1096,128]{1,0:T(8,128)S(1)}, f32[1096,128]{1,0:T(8,128)}, u32[]{:S(2)}) copy-start(f32[1096,128]{1,0:T(8,128)} %get-tuple-element.38.refs_0_) | copy-start | bytes 1683460
  28.0 37.0 %collective-permute-start.10 = (f32[1096,128]{1,0:T(8,128)}, f32[1096,128]{1,0:T(8,128)}, u32[]{:S(2)}, u32[]{:S(2)}) collective-permute-start(f32[1096,128]{1,0:T(8,128)} %get-tuple-element.37), channel_id=1, source_target_pairs={{0,4},{1,5},{2,6},{3,7},{4,0},{5,1},{6,2},{7,3},{8,12},{9,13},{10,... | collective-permute-start | bytes 1683464 | tf_op jit(solution)/shard_map/ppermute | solution.py:548
  34.2 13.8 %collective-permute-start.2 = (f32[128,128]{1,0:T(8,128)}, f32[128,128]{1,0:T(8,128)S(1)}, u32[]{:S(2)}, u32[]{:S(2)}) collective-permute-start(f32[128,128]{1,0:T(8,128)} %get-tuple-element.29), channel_id=1, source_target_pairs={{0,1},{1,2},{2,3},{3,4},{4,5},{5,6},{6,7},{7,0},{8,9},{9,10},{10,1... | collective-permute-start | bytes 196616 | tf_op jit(solution)/shard_map/ppermute | solution.py:477
  34.2 25.0 %collective-permute-start.3 = (f32[128,128]{1,0:T(8,128)}, f32[128,128]{1,0:T(8,128)S(1)}, u32[]{:S(2)}, u32[]{:S(2)}) collective-permute-start(f32[128,128]{1,0:T(8,128)} %get-tuple-element.30), channel_id=1, source_target_pairs={{1,0},{2,1},{3,2},{4,3},{5,4},{6,5},{7,6},{0,7},{9,8},{10,9},{11,1... | collective-permute-start | bytes 196616 | tf_op jit(solution)/shard_map/ppermute | solution.py:478
  37.8 10.0 %collective-permute-start = (f32[32,128]{1,0:T(8,128)S(1)}, f32[32,128]{1,0:T(8,128)S(1)}, u32[]{:S(2)}, u32[]{:S(2)}) collective-permute-start(f32[32,128]{1,0:T(8,128)S(1)} %get-tuple-element.27), channel_id=1, source_target_pairs={{0,8},{8,16},{16,24},{1,9},{9,17},{17,25},{2,10},{10,18},{18,26},{... | collective-permute-start | bytes 49160 | tf_op jit(solution)/shard_map/ppermute | solution.py:475
  41.1 6.7 %collective-permute-start.1 = (f32[32,128]{1,0:T(8,128)S(1)}, f32[32,128]{1,0:T(8,128)S(1)}, u32[]{:S(2)}, u32[]{:S(2)}) collective-permute-start(f32[32,128]{1,0:T(8,128)S(1)} %get-tuple-element.28), channel_id=1, source_target_pairs={{8,0},{16,8},{24,16},{9,1},{17,9},{25,17},{10,2},{18,10},{26,18},{... | collective-permute-start | bytes 49160 | tf_op jit(solution)/shard_map/ppermute | solution.py:476
  42.5 16.8 %copy-start.4 = (s32[128,128]{1,0:T(8,128)S(1)}, s32[128,128]{1,0:T(8,128)}, u32[]{:S(2)}) copy-start(s32[128,128]{1,0:T(8,128)} %refs_7_.5) | copy-start | bytes 196612
  42.5 16.8 %copy-start.5 = (f32[128,128]{1,0:T(8,128)S(1)}, f32[128,128]{1,0:T(8,128)}, u32[]{:S(2)}) copy-start(f32[128,128]{1,0:T(8,128)} %refs_6_.5) | copy-start | bytes 196612
  42.5 16.8 %copy-start.6 = (f32[8]{0:T(128)S(1)}, f32[8]{0:T(128)}, u32[]{:S(2)}) copy-start(f32[8]{0:T(128)} %constant.18.clone.refs_0_.omega_ref) | copy-start | bytes 100
  46.8 1.0 copy-start.7
  47.8 24.9 %collective-permute-start.9 = (f32[1096,128]{1,0:T(8,128)}, f32[1096,128]{1,0:T(8,128)S(1)}, u32[]{:S(2)}, u32[]{:S(2)}) collective-permute-start(f32[1096,128]{1,0:T(8,128)} %get-tuple-element.36), channel_id=1, source_target_pairs={{0,1},{1,0},{2,3},{3,2},{4,5},{5,4},{6,7},{7,6},{8,9},{9,8},{10,11... | collective-permute-start | bytes 1683464 | tf_op jit(solution)/shard_map/ppermute | solution.py:548
  47.9 33.3 %collective-permute-start.8 = (f32[1096,128]{1,0:T(8,128)}, f32[1096,128]{1,0:T(8,128)S(1)}, u32[]{:S(2)}, u32[]{:S(2)}) collective-permute-start(f32[1096,128]{1,0:T(8,128)} %get-tuple-element.35), channel_id=1, source_target_pairs={{0,2},{1,3},{2,0},{3,1},{4,6},{5,7},{6,4},{7,5},{8,10},{9,11},{10,... | collective-permute-start | bytes 1683464 | tf_op jit(solution)/shard_map/ppermute | solution.py:548
  48.0 70.2 %collective-permute-start.7 = (f32[1096,128]{1,0:T(8,128)}, f32[1096,128]{1,0:T(8,128)S(1)}, u32[]{:S(2)}, u32[]{:S(2)}) collective-permute-start(f32[1096,128]{1,0:T(8,128)} %get-tuple-element.34), channel_id=1, source_target_pairs={{0,3},{1,2},{2,1},{3,0},{4,7},{5,6},{6,5},{7,4},{8,11},{9,10},{10,... | collective-permute-start | bytes 1683464 | tf_op jit(solution)/shard_map/ppermute | solution.py:548
  59.2 63.0 %collective-permute-start.6 = (f32[1096,128]{1,0:T(8,128)}, f32[1096,128]{1,0:T(8,128)S(1)}, u32[]{:S(2)}, u32[]{:S(2)}) collective-permute-start(f32[1096,128]{1,0:T(8,128)} %get-tuple-element.33), channel_id=1, source_target_pairs={{0,5},{1,4},{2,7},{3,6},{4,1},{5,0},{6,3},{7,2},{8,13},{9,12},{10,... | collective-permute-start | bytes 1683464 | tf_op jit(solution)/shard_map/ppermute | solution.py:548
  59.3 1.9 %copy-start.1 = (f32[48,128,128]{2,1,0:T(8,128)S(1)}, f32[48,128,128]{2,1,0:T(8,128)}, u32[]{:S(2)}) copy-start(f32[48,128,128]{2,1,0:T(8,128)} %param.10) | copy-start | bytes 9437188
  61.2 3.8 %copy-start.11 = (f32[1096,128]{1,0:T(8,128)S(1)}, f32[1096,128]{1,0:T(8,128)}, u32[]{:S(2)}) copy-start(f32[1096,128]{1,0:T(8,128)} %get-tuple-element.32) | copy-start | bytes 1683460
  61.2 6.3 %copy-start.8 = (f32[16,64,256]{2,1,0:T(8,128)S(1)}, f32[16,64,256]{2,1,0:T(8,128)}, u32[]{:S(2)}) copy-start(f32[16,64,256]{2,1,0:T(8,128)} %copy-done.7) | copy-start | bytes 3145732
  65.0 7.6 %copy-start.10 = (f32[1096,128]{1,0:T(8,128)S(1)}, f32[1096,128]{1,0:T(8,128)}, u32[]{:S(2)}) copy-start(f32[1096,128]{1,0:T(8,128)} %get-tuple-element.31) | copy-start | bytes 1683460
  65.0 61.3 %collective-permute-start.5 = (f32[1096,128]{1,0:T(8,128)S(1)}, f32[1096,128]{1,0:T(8,128)S(1)}, u32[]{:S(2)}, u32[]{:S(2)}) collective-permute-start(f32[1096,128]{1,0:T(8,128)S(1)} %copy-done.11), channel_id=1, source_target_pairs={{0,6},{1,7},{2,4},{3,5},{4,2},{5,3},{6,0},{7,1},{8,14},{9,15},{10,... | collective-permute-start | bytes 1683464 | tf_op jit(solution)/shard_map/ppermute | solution.py:548
  72.7 57.9 %collective-permute-start.4 = (f32[1096,128]{1,0:T(8,128)S(1)}, f32[1096,128]{1,0:T(8,128)S(1)}, u32[]{:S(2)}, u32[]{:S(2)}) collective-permute-start(f32[1096,128]{1,0:T(8,128)S(1)} %copy-done.10), channel_id=1, source_target_pairs={{0,7},{1,6},{2,5},{3,4},{4,3},{5,2},{6,1},{7,0},{8,15},{9,14},{10,... | collective-permute-start | bytes 1683464 | tf_op jit(solution)/shard_map/ppermute | solution.py:548
  134.7 14.3 %copy-start.2 = (f32[48,128,128]{2,1,0:T(8,128)S(1)}, f32[48,128,128]{2,1,0:T(8,128)}, u32[]{:S(2)}) copy-start(f32[48,128,128]{2,1,0:T(8,128)} %param.10) | copy-start | bytes 9437188
  136.9 12.1 %collective-permute-start.13 = (f32[128,128]{1,0:T(8,128)S(1)}, f32[128,128]{1,0:T(8,128)S(1)}, u32[]{:S(2)}, u32[]{:S(2)}) collective-permute-start(f32[128,128]{1,0:T(8,128)S(1)} %get-tuple-element.42), channel_id=1, source_target_pairs={{0,1},{1,2},{2,3},{3,4},{4,5},{5,6},{6,7},{7,0},{8,9},{9,10},{10,1... | collective-permute-start | bytes 196616 | tf_op jit(solution)/shard_map/ppermute | solution.py:477
  136.9 12.1 %collective-permute-start.14 = (f32[128,128]{1,0:T(8,128)S(1)}, f32[128,128]{1,0:T(8,128)S(1)}, u32[]{:S(2)}, u32[]{:S(2)}) collective-permute-start(f32[128,128]{1,0:T(8,128)S(1)} %get-tuple-element.43), channel_id=1, source_target_pairs={{1,0},{2,1},{3,2},{4,3},{5,4},{6,5},{7,6},{0,7},{9,8},{10,9},{11,1... | collective-permute-start | bytes 196616 | tf_op jit(solution)/shard_map/ppermute | solution.py:478
  140.5 4.3 %collective-permute-start.11 = (f32[32,128]{1,0:T(8,128)S(1)}, f32[32,128]{1,0:T(8,128)S(1)}, u32[]{:S(2)}, u32[]{:S(2)}) collective-permute-start(f32[32,128]{1,0:T(8,128)S(1)} %get-tuple-element.40), channel_id=1, source_target_pairs={{0,8},{8,16},{16,24},{1,9},{9,17},{17,25},{2,10},{10,18},{18,26},{... | collective-permute-start | bytes 49160 | tf_op jit(solution)/shard_map/ppermute | solution.py:475
  143.4 5.6 %collective-permute-start.12 = (f32[32,128]{1,0:T(8,128)S(1)}, f32[32,128]{1,0:T(8,128)S(1)}, u32[]{:S(2)}, u32[]{:S(2)}) collective-permute-start(f32[32,128]{1,0:T(8,128)S(1)} %get-tuple-element.41), channel_id=1, source_target_pairs={{8,0},{16,8},{24,16},{9,1},{17,9},{25,17},{10,2},{18,10},{26,18},{... | collective-permute-start | bytes 49160 | tf_op jit(solution)/shard_map/ppermute | solution.py:476
  154.4 14.2 %collective-permute-start.17 = (f32[128,128]{1,0:T(8,128)S(1)}, f32[128,128]{1,0:T(8,128)S(1)}, u32[]{:S(2)}, u32[]{:S(2)}) collective-permute-start(f32[128,128]{1,0:T(8,128)S(1)} %get-tuple-element.47), channel_id=1, source_target_pairs={{0,1},{1,2},{2,3},{3,4},{4,5},{5,6},{6,7},{7,0},{8,9},{9,10},{10,1... | collective-permute-start | bytes 196616 | tf_op jit(solution)/shard_map/ppermute | solution.py:477
  154.5 14.1 %collective-permute-start.18 = (f32[128,128]{1,0:T(8,128)S(1)}, f32[128,128]{1,0:T(8,128)S(1)}, u32[]{:S(2)}, u32[]{:S(2)}) collective-permute-start(f32[128,128]{1,0:T(8,128)S(1)} %get-tuple-element.48), channel_id=1, source_target_pairs={{1,0},{2,1},{3,2},{4,3},{5,4},{6,5},{7,6},{0,7},{9,8},{10,9},{11,1... | collective-permute-start | bytes 196616 | tf_op jit(solution)/shard_map/ppermute | solution.py:478
  158.4 6.0 %collective-permute-start.15 = (f32[32,128]{1,0:T(8,128)S(1)}, f32[32,128]{1,0:T(8,128)S(1)}, u32[]{:S(2)}, u32[]{:S(2)}) collective-permute-start(f32[32,128]{1,0:T(8,128)S(1)} %get-tuple-element.45), channel_id=1, source_target_pairs={{0,8},{8,16},{16,24},{1,9},{9,17},{17,25},{2,10},{10,18},{18,26},{... | collective-permute-start | bytes 49160 | tf_op jit(solution)/shard_map/ppermute | solution.py:475
  163.0 5.6 %collective-permute-start.16 = (f32[32,128]{1,0:T(8,128)S(1)}, f32[32,128]{1,0:T(8,128)S(1)}, u32[]{:S(2)}, u32[]{:S(2)}) collective-permute-start(f32[32,128]{1,0:T(8,128)S(1)} %get-tuple-element.46), channel_id=1, source_target_pairs={{8,0},{16,8},{24,16},{9,1},{17,9},{25,17},{10,2},{18,10},{26,18},{... | collective-permute-start | bytes 49160 | tf_op jit(solution)/shard_map/ppermute | solution.py:476

commit v6 on v5

--- a/solution.py
+++ b/solution.py
@@ -550,8 +550,9 @@
     state, _ = sweep(state, state, strips, None, False)
     forcing = add([buckets[0]], None)
     each = tiles // 8
-    for first in range(0, len(arrived), each):
-        forcing = add(arrived[first : first + each], forcing)
+    ends = [0, each, 2 * each, 3 * each, 5 * each, 6 * each, len(arrived)]
+    for first, last in zip(ends, ends[1:]):
+        forcing = add(arrived[first:last], forcing)
 
     eta, *strips = pl.pallas_call(
         functools.partial(join_kernel, per, chunk_rows),

time: 173 us -> 173 us (level); the launches traced: 173 us -> 171 us
  Pallas kernels: 80.4 us -> 69.6 us
  waiting for transfers between devices: 44.9 us -> 49.4 us
  starting transfers between devices: 44.8 us -> 49.1 us
    pallas_call x8 -> x7, Pallas kernels: 34.1 us -> 23.4 us  [add(): pl.pallas_call(functools.partial(sum_kernel, width, windows, len(parts),...]
    ppermute x3, starting transfers between devices: 0.12 us -> 7.35 us  [exchange(): lax.ppermute(east, 'lon', [(i, (i + 1) % tiles) for i in range(tiles)])]
    ppermute x3, starting transfers between devices: 11 us -> 7.07 us  [exchange(): lax.ppermute(west, 'lon', [((i + 1) % tiles, i) for i in range(tiles)])]
    ppermute x7, waiting for transfers between devices: 36.2 us -> 39.7 us  [local(): lax.ppermute(buckets[s], 'lon', [(i, i ^ s) for i in range(tiles)])]
    ppermute x7, starting transfers between devices: 19 us -> 21.6 us  [local(): lax.ppermute(buckets[s], 'lon', [(i, i ^ s) for i in range(tiles)])]
  transfers between devices with their start and end apart: 19 -> 19, of which waited for: 6 -> 8; matrix products, arithmetic and copies ran while one was open for 0% -> 0% of each run, Pallas kernels for 21% -> 15%
where the time goes in v6:
time: 173 us; the launch traced here: 171 us
  Pallas kernels  69.6 us (40%)
  waiting for transfers between devices  49.4 us (29%)
  starting transfers between devices  49.1 us (28%)
  local copies, waits for them, and re-layouts  2.97 us (2%)
    ppermute x7, waiting for transfers between devices, local(): lax.ppermute(buckets[s], 'lon', [(i, i ^ s) for i in range(tiles)])  39.7 us
    pallas_call x1, Pallas kernels, local(): pl.pallas_call(functools.partial(bucket_kernel, tiles, cuts, capacity, wi...  28 us
    pallas_call x7, Pallas kernels, add(): pl.pallas_call(functools.partial(sum_kernel, width, windows, len(parts),...  23.4 us
    ppermute x7, starting transfers between devices, local(): lax.ppermute(buckets[s], 'lon', [(i, i ^ s) for i in range(tiles)])  21.6 us
    pallas_call x3, Pallas kernels, sweep(): pl.pallas_call(functools.partial(sweep_kernel, per, chunk_rows, forced, e...  14 us
    ppermute x3, waiting for transfers between devices, exchange(): lax.ppermute(north, 'lat', [(i + 1, i) for i in range(lats - 1)])  9.29 us
    ppermute x3, starting transfers between devices, exchange(): lax.ppermute(south, 'lat', [(i, i + 1) for i in range(lats - 1)])  9.19 us
    ppermute x3, starting transfers between devices, exchange(): lax.ppermute(east, 'lon', [(i, (i + 1) % tiles) for i in range(tiles)])  7.35 us
  transfers between devices with their start and end apart: 19, of which 8 were waited for; matrix products, arithmetic and copies ran while one was open for 0% of the time, Pallas kernels for 15%

profile of v6, /device:TPU:0, one launch (start us, length us, event | category | flops | bytes accessed | tf_op | source)
XLA Modules:
  0.0 171.4 jit_solution(9850213105823831124)
XLA Ops:
  0.0 28.0 %shard_map.93 = (f32[1096,128]{1,0:T(8,128)}, f32[1096,128]{1,0:T(8,128)}, f32[1096,128]{1,0:T(8,128)}, f32[1096,128]{1,0:T(8,128)}, f32[1096,128]{1,0:T(8,128)}...) custom-call(s32[256,128]{1,0:T(8,128)} %bitcast.12, s32[256,128]{1,0:T(8,128)} %bitcast.13, ...), custom_call_target="tpu_custom_call" | custom-call | flops 10000000000 | bytes 7000000 | tf_op jit(solution)/shard_map/pallas_call | solution.py:512
  28.0 4.1 %collective-permute-start.10 = (f32[1096,128]{1,0:T(8,128)}, f32[1096,128]{1,0:T(8,128)}, u32[]{:S(2)}, u32[]{:S(2)}) collective-permute-start(f32[1096,128]{1,0:T(8,128)} %get-tuple-element.37), channel_id=1, source_target_pairs={{0,4},{1,5},{2,6},{3,7},{4,0},{5,1},{6,2},{7,3},{8,12},{9,13},{10,... | collective-permute-start | bytes 1683464 | tf_op jit(solution)/shard_map/ppermute | solution.py:548
  32.1 2.1 %shard_map.91 = (f32[32,128]{1,0:T(8,128)S(1)}, f32[32,128]{1,0:T(8,128)S(1)}, f32[128,128]{1,0:T(8,128)}, f32[128,128]{1,0:T(8,128)}) custom-call(f32[6,8,128,128]{3,2,1,0:T(8,128)S(1)} %bitcast.5, f32[128,128]{1,0:T(8,128)S(1)} %copy-done.3), custom_call_target="tpu_custom_call" | custom-call | flops 1000000 | bytes 3000000 | tf_op jit(solution)/shard_map/pallas_call | solution.py:500
  34.2 3.5 %collective-permute-start.3 = (f32[128,128]{1,0:T(8,128)}, f32[128,128]{1,0:T(8,128)S(1)}, u32[]{:S(2)}, u32[]{:S(2)}) collective-permute-start(f32[128,128]{1,0:T(8,128)} %get-tuple-element.30), channel_id=1, source_target_pairs={{1,0},{2,1},{3,2},{4,3},{5,4},{6,5},{7,6},{0,7},{9,8},{10,9},{11,1... | collective-permute-start | bytes 196616 | tf_op jit(solution)/shard_map/ppermute | solution.py:478
  37.8 3.1 %collective-permute-start = (f32[32,128]{1,0:T(8,128)S(1)}, f32[32,128]{1,0:T(8,128)S(1)}, u32[]{:S(2)}, u32[]{:S(2)}) collective-permute-start(f32[32,128]{1,0:T(8,128)S(1)} %get-tuple-element.27), channel_id=1, source_target_pairs={{0,8},{8,16},{16,24},{1,9},{9,17},{17,25},{2,10},{10,18},{18,26},{... | collective-permute-start | bytes 49160 | tf_op jit(solution)/shard_map/ppermute | solution.py:475
  40.9 1.3 collective-permute-start.1
  42.2 2.3 %shard_map.94.refs_1_ = f32[16,64,256]{2,1,0:T(8,128)S(1)} custom-call(f32[1096,128]{1,0:T(8,128)S(1)} %copy-done.9), custom_call_target="tpu_custom_call" | custom-call | flops 10000000000 | bytes 3000000 | tf_op jit(solution)/shard_map/pallas_call | solution.py:536
  46.5 2.4 %collective-permute-start.8 = (f32[1096,128]{1,0:T(8,128)}, f32[1096,128]{1,0:T(8,128)S(1)}, u32[]{:S(2)}, u32[]{:S(2)}) collective-permute-start(f32[1096,128]{1,0:T(8,128)} %get-tuple-element.35), channel_id=1, source_target_pairs={{0,2},{1,3},{2,0},{3,1},{4,6},{5,7},{6,4},{7,5},{8,10},{9,11},{10,... | collective-permute-start | bytes 1683464 | tf_op jit(solution)/shard_map/ppermute | solution.py:548
  48.9 9.6 %collective-permute-start.6 = (f32[1096,128]{1,0:T(8,128)}, f32[1096,128]{1,0:T(8,128)S(1)}, u32[]{:S(2)}, u32[]{:S(2)}) collective-permute-start(f32[1096,128]{1,0:T(8,128)} %get-tuple-element.33), channel_id=1, source_target_pairs={{0,3},{1,2},{2,1},{3,0},{4,7},{5,6},{6,5},{7,4},{8,11},{9,10},{10,... | collective-permute-start | bytes 1683464 | tf_op jit(solution)/shard_map/ppermute | solution.py:548
  58.6 1.9 %copy-done.1 = f32[48,128,128]{2,1,0:T(8,128)S(1)} copy-done((f32[48,128,128]{2,1,0:T(8,128)S(1)}, f32[48,128,128]{2,1,0:T(8,128)}, u32[]{:S(2)}) %copy-start.1) | copy-done | bytes 3145752
  60.5 3.8 %shard_map.92.eta_ref.east_ref.north_ref.refs_2_.refs_3_ = f32[6,8,128,128]{3,2,1,0:T(8,128)S(1)} custom-call(f32[8]{0:T(128)S(1)} %copy-done.6, f32[6,8,128,128]{3,2,1,0:T(8,128)S(1)} %bitcast.6, f32[6,8,128,128]{3,2,1,0:T(8,128)S(1)} %bitcast.7, f32[6,8,128,128]{3,2,1,0:T(8,128)S(1)} %bitcast.8, f32[6,8,128,128]{3,2,1,0:T(8,128)S(1)} %bitcast.9, ...), custom_call_target="tpu_custom_call" | custom-call | flops 16000000 | bytes 9000000 | tf_op jit(solution)/shard_map/pallas_call | solution.py:483
  64.3 2.8 %collective-permute-start.5 = (f32[1096,128]{1,0:T(8,128)S(1)}, f32[1096,128]{1,0:T(8,128)S(1)}, u32[]{:S(2)}, u32[]{:S(2)}) collective-permute-start(f32[1096,128]{1,0:T(8,128)S(1)} %copy-done.11), channel_id=1, source_target_pairs={{0,6},{1,7},{2,4},{3,5},{4,2},{5,3},{6,0},{7,1},{8,14},{9,15},{10,... | collective-permute-start | bytes 1683464 | tf_op jit(solution)/shard_map/ppermute | solution.py:548
  67.1 3.2 %shard_map.95.refs_1_ = f32[16,64,256]{2,1,0:T(8,128)S(1)} custom-call(f32[1096,128]{1,0:T(8,128)} %collective-permute-done.10.refs_0_, f32[16,64,256]{2,1,0:T(8,128)S(1)} %copy-done.8), custom_call_target="tpu_custom_call" | custom-call | flops 10000000000 | bytes 3000000 | tf_op jit(solution)/shard_map/pallas_call | solution.py:536
  70.4 2.7 %collective-permute-start.4 = (f32[1096,128]{1,0:T(8,128)S(1)}, f32[1096,128]{1,0:T(8,128)S(1)}, u32[]{:S(2)}, u32[]{:S(2)}) collective-permute-start(f32[1096,128]{1,0:T(8,128)S(1)} %copy-done.10), channel_id=1, source_target_pairs={{0,7},{1,6},{2,5},{3,4},{4,3},{5,2},{6,1},{7,0},{8,15},{9,14},{10,... | collective-permute-start | bytes 1683464 | tf_op jit(solution)/shard_map/ppermute | solution.py:548
  73.1 2.1 %shard_map.96.refs_1_ = f32[16,64,256]{2,1,0:T(8,128)S(1)} custom-call(f32[1096,128]{1,0:T(8,128)S(1)} %collective-permute-done.9.refs_0_, f32[16,64,256]{2,1,0:T(8,128)S(1)} %shard_map.95.refs_1_), custom_call_target="tpu_custom_call" | custom-call | flops 10000000000 | bytes 3000000 | tf_op jit(solution)/shard_map/pallas_call | solution.py:536
  75.2 5.1 %collective-permute-done.8.refs_0_ = f32[1096,128]{1,0:T(8,128)S(1)} collective-permute-done((f32[1096,128]{1,0:T(8,128)}, f32[1096,128]{1,0:T(8,128)S(1)}, u32[]{:S(2)}, u32[]{:S(2)}) %collective-permute-start.8) | collective-permute-done | bytes 561184 | tf_op jit(solution)/shard_map/ppermute | solution.py:548
  80.3 3.1 %shard_map.97.refs_2_ = f32[16,64,256]{2,1,0:T(8,128)S(1)} custom-call(f32[1096,128]{1,0:T(8,128)S(1)} %collective-permute-done.8.refs_0_, f32[16,64,256]{2,1,0:T(8,128)S(1)} %shard_map.96.refs_1_), custom_call_target="tpu_custom_call" | custom-call | flops 10000000000 | bytes 3000000 | tf_op jit(solution)/shard_map/pallas_call | solution.py:536
  83.4 34.5 %collective-permute-done.6.refs_0_ = f32[1096,128]{1,0:T(8,128)S(1)} collective-permute-done((f32[1096,128]{1,0:T(8,128)}, f32[1096,128]{1,0:T(8,128)S(1)}, u32[]{:S(2)}, u32[]{:S(2)}) %collective-permute-start.6) | collective-permute-done | bytes 561184 | tf_op jit(solution)/shard_map/ppermute | solution.py:548
  118.0 5.2 %shard_map.98.refs_1_ = f32[16,64,256]{2,1,0:T(8,128)S(1)} custom-call(f32[1096,128]{1,0:T(8,128)S(1)} %collective-permute-done.6.refs_0_, f32[1096,128]{1,0:T(8,128)S(1)} %collective-permute-done.7.refs_1_, f32[16,64,256]{2,1,0:T(8,128)S(1)} %shard_map.97.refs_2_), custom_call_target="tpu_custom_call" | custom-call | flops 10000000000 | bytes 3000000 | tf_op jit(solution)/shard_map/pallas_call | solution.py:536
  123.2 4.3 %shard_map.99.refs_1_ = f32[16,64,256]{2,1,0:T(8,128)S(1)} custom-call(f32[1096,128]{1,0:T(8,128)S(1)} %collective-permute-done.5.refs_0_, f32[16,64,256]{2,1,0:T(8,128)S(1)} %shard_map.98.refs_1_), custom_call_target="tpu_custom_call" | custom-call | flops 10000000000 | bytes 3000000 | tf_op jit(solution)/shard_map/pallas_call | solution.py:536
  127.5 3.1 %shard_map.100.re_ref.im_ref.refs_13_.refs_14_ = f32[16,64,256]{2,1,0:T(8,128)S(1)} custom-call(f32[1096,128]{1,0:T(8,128)S(1)} %collective-permute-done.4.refs_0_, f32[16,64,256]{2,1,0:T(8,128)S(1)} %shard_map.99.refs_1_), custom_call_target="tpu_custom_call" | custom-call | flops 10000000000 | bytes 3000000 | tf_op jit(solution)/shard_map/pallas_call | solution.py:536
  130.6 2.2 %shard_map.101 = (f32[2,8,128,128]{3,2,1,0:T(8,128)S(1)}, f32[32,128]{1,0:T(8,128)S(1)}, f32[32,128]{1,0:T(8,128)S(1)}, f32[128,128]{1,0:T(8,128)S(1)}, f32[128,128]{1,0:T(8,128)S(1)}) custom-call(f32[8]{0:T(128)S(1)} %copy-done.6, f32[6,8,128,128]{3,2,1,0:T(8,128)S(1)} %shard_map.92.eta_ref.east_ref.north_ref.refs_2_.refs_3_, ...), custom_call_target="tpu_custom_call" | custom-call | flops 1000000 | bytes 6000000 | tf_op jit(solution)/shard_map/pallas_call | solution.py:557
  132.9 3.5 %collective-permute-start.14 = (f32[128,128]{1,0:T(8,128)S(1)}, f32[128,128]{1,0:T(8,128)S(1)}, u32[]{:S(2)}, u32[]{:S(2)}) collective-permute-start(f32[128,128]{1,0:T(8,128)S(1)} %get-tuple-element.43), channel_id=1, source_target_pairs={{1,0},{2,1},{3,2},{4,3},{5,4},{6,5},{7,6},{0,7},{9,8},{10,9},{11,1... | collective-permute-start | bytes 196616 | tf_op jit(solution)/shard_map/ppermute | solution.py:478
  136.4 1.6 collective-permute-start.11
  138.0 1.3 collective-permute-start.12
  139.4 4.2 %collective-permute-done.12.refs_10_ = f32[32,128]{1,0:T(8,128)S(1)} collective-permute-done((f32[32,128]{1,0:T(8,128)S(1)}, f32[32,128]{1,0:T(8,128)S(1)}, u32[]{:S(2)}, u32[]{:S(2)}) %collective-permute-start.12) | collective-permute-done | bytes 16416 | tf_op jit(solution)/shard_map/ppermute | solution.py:476
  143.8 5.3 %shard_map.102 = (f32[6,8,128,128]{3,2,1,0:T(8,128)S(1)}, f32[32,128]{1,0:T(8,128)S(1)}, f32[32,128]{1,0:T(8,128)S(1)}, f32[128,128]{1,0:T(8,128)S(1)}, f32[128,128]{1,0:T(8,128)S(1)}) custom-call(f32[8]{0:T(128)S(1)} %copy-done.6, f32[2,8,128,128]{3,2,1,0:T(8,128)S(1)} %get-tuple-element.39.refs_1_, ...), custom_call_target="tpu_custom_call" | custom-call | flops 16000000 | bytes 9000000 | tf_op jit(solution)/shard_map/pallas_call | solution.py:483
  149.1 7.3 %collective-permute-start.17 = (f32[128,128]{1,0:T(8,128)S(1)}, f32[128,128]{1,0:T(8,128)S(1)}, u32[]{:S(2)}, u32[]{:S(2)}) collective-permute-start(f32[128,128]{1,0:T(8,128)S(1)} %get-tuple-element.47), channel_id=1, source_target_pairs={{0,1},{1,2},{2,3},{3,4},{4,5},{5,6},{6,7},{7,0},{8,9},{9,10},{10,1... | collective-permute-start | bytes 196616 | tf_op jit(solution)/shard_map/ppermute | solution.py:477
  156.4 4.5 %collective-permute-start.15 = (f32[32,128]{1,0:T(8,128)S(1)}, f32[32,128]{1,0:T(8,128)S(1)}, u32[]{:S(2)}, u32[]{:S(2)}) collective-permute-start(f32[32,128]{1,0:T(8,128)S(1)} %get-tuple-element.45), channel_id=1, source_target_pairs={{0,8},{8,16},{16,24},{1,9},{9,17},{17,25},{2,10},{10,18},{18,26},{... | collective-permute-start | bytes 49160 | tf_op jit(solution)/shard_map/ppermute | solution.py:475
  160.9 1.3 collective-permute-start.16
  162.4 4.2 %collective-permute-done.16.refs_10_ = f32[32,128]{1,0:T(8,128)S(1)} collective-permute-done((f32[32,128]{1,0:T(8,128)S(1)}, f32[32,128]{1,0:T(8,128)S(1)}, u32[]{:S(2)}, u32[]{:S(2)}) %collective-permute-start.16) | collective-permute-done | bytes 16416 | tf_op jit(solution)/shard_map/ppermute | solution.py:476
  166.6 4.8 %shard_map.103 = f32[6,8,128,128]{3,2,1,0:T(8,128)} custom-call(f32[8]{0:T(128)S(1)} %copy-done.6, f32[6,8,128,128]{3,2,1,0:T(8,128)S(1)} %get-tuple-element.44.refs_1_.refs_2_.refs_3_, f32[6,8,128,128]{3,2,1,0:T(8,128)S(1)} %get-tuple-element.44.refs_1_.refs_2_.refs_3_, f32[6,8,128,128]{3,2,1,0:T(8,128)S(1)} %get-tuple-element.44.refs_1_.refs_2_.refs_3_, ...), custom_call_target="tpu_custom_call" | custom-call | flops 16000000 | bytes 9000000 | tf_op jit(solution)/shard_map/pallas_call | solution.py:483
  (45 shorter events, 2.6 us)
Async XLA Ops:
  0.0 32.1 %copy-start = (f32[48,128,128]{2,1,0:T(8,128)S(1)}, f32[48,128,128]{2,1,0:T(8,128)}, u32[]{:S(2)}) copy-start(f32[48,128,128]{2,1,0:T(8,128)} %param.9) | copy-start | bytes 9437188
  0.0 32.1 %copy-start.3 = (f32[128,128]{1,0:T(8,128)S(1)}, f32[128,128]{1,0:T(8,128)}, u32[]{:S(2)}) copy-start(f32[128,128]{1,0:T(8,128)} %refs_5_.5) | copy-start | bytes 196612
  28.0 14.2 %copy-start.9 = (f32[1096,128]{1,0:T(8,128)S(1)}, f32[1096,128]{1,0:T(8,128)}, u32[]{:S(2)}) copy-start(f32[1096,128]{1,0:T(8,128)} %get-tuple-element.38.refs_0_) | copy-start | bytes 1683460
  28.0 36.3 %collective-permute-start.10 = (f32[1096,128]{1,0:T(8,128)}, f32[1096,128]{1,0:T(8,128)}, u32[]{:S(2)}, u32[]{:S(2)}) collective-permute-start(f32[1096,128]{1,0:T(8,128)} %get-tuple-element.37), channel_id=1, source_target_pairs={{0,4},{1,5},{2,6},{3,7},{4,0},{5,1},{6,2},{7,3},{8,12},{9,13},{10,... | collective-permute-start | bytes 1683464 | tf_op jit(solution)/shard_map/ppermute | solution.py:548
  34.2 14.7 %collective-permute-start.2 = (f32[128,128]{1,0:T(8,128)}, f32[128,128]{1,0:T(8,128)S(1)}, u32[]{:S(2)}, u32[]{:S(2)}) collective-permute-start(f32[128,128]{1,0:T(8,128)} %get-tuple-element.29), channel_id=1, source_target_pairs={{0,1},{1,2},{2,3},{3,4},{4,5},{5,6},{6,7},{7,0},{8,9},{9,10},{10,1... | collective-permute-start | bytes 196616 | tf_op jit(solution)/shard_map/ppermute | solution.py:477
  34.2 24.3 %collective-permute-start.3 = (f32[128,128]{1,0:T(8,128)}, f32[128,128]{1,0:T(8,128)S(1)}, u32[]{:S(2)}, u32[]{:S(2)}) collective-permute-start(f32[128,128]{1,0:T(8,128)} %get-tuple-element.30), channel_id=1, source_target_pairs={{1,0},{2,1},{3,2},{4,3},{5,4},{6,5},{7,6},{0,7},{9,8},{10,9},{11,1... | collective-permute-start | bytes 196616 | tf_op jit(solution)/shard_map/ppermute | solution.py:478
  37.8 7.8 %collective-permute-start = (f32[32,128]{1,0:T(8,128)S(1)}, f32[32,128]{1,0:T(8,128)S(1)}, u32[]{:S(2)}, u32[]{:S(2)}) collective-permute-start(f32[32,128]{1,0:T(8,128)S(1)} %get-tuple-element.27), channel_id=1, source_target_pairs={{0,8},{8,16},{16,24},{1,9},{9,17},{17,25},{2,10},{10,18},{18,26},{... | collective-permute-start | bytes 49160 | tf_op jit(solution)/shard_map/ppermute | solution.py:475
  40.9 5.6 %collective-permute-start.1 = (f32[32,128]{1,0:T(8,128)S(1)}, f32[32,128]{1,0:T(8,128)S(1)}, u32[]{:S(2)}, u32[]{:S(2)}) collective-permute-start(f32[32,128]{1,0:T(8,128)S(1)} %get-tuple-element.28), channel_id=1, source_target_pairs={{8,0},{16,8},{24,16},{9,1},{17,9},{25,17},{10,2},{18,10},{26,18},{... | collective-permute-start | bytes 49160 | tf_op jit(solution)/shard_map/ppermute | solution.py:476
  42.2 16.4 %copy-start.4 = (s32[128,128]{1,0:T(8,128)S(1)}, s32[128,128]{1,0:T(8,128)}, u32[]{:S(2)}) copy-start(s32[128,128]{1,0:T(8,128)} %refs_7_.5) | copy-start | bytes 196612
  42.2 16.4 %copy-start.5 = (f32[128,128]{1,0:T(8,128)S(1)}, f32[128,128]{1,0:T(8,128)}, u32[]{:S(2)}) copy-start(f32[128,128]{1,0:T(8,128)} %refs_6_.5) | copy-start | bytes 196612
  42.2 16.4 %copy-start.6 = (f32[8]{0:T(128)S(1)}, f32[8]{0:T(128)}, u32[]{:S(2)}) copy-start(f32[8]{0:T(128)} %constant.18.clone.refs_0_.omega_ref) | copy-start | bytes 100
  44.5 1.0 copy-start.7
  45.5 24.9 %collective-permute-start.9 = (f32[1096,128]{1,0:T(8,128)}, f32[1096,128]{1,0:T(8,128)S(1)}, u32[]{:S(2)}, u32[]{:S(2)}) collective-permute-start(f32[1096,128]{1,0:T(8,128)} %get-tuple-element.36), channel_id=1, source_target_pairs={{0,1},{1,0},{2,3},{3,2},{4,5},{5,4},{6,7},{7,6},{8,9},{9,8},{10,11... | collective-permute-start | bytes 1683464 | tf_op jit(solution)/shard_map/ppermute | solution.py:548
  46.5 33.8 %collective-permute-start.8 = (f32[1096,128]{1,0:T(8,128)}, f32[1096,128]{1,0:T(8,128)S(1)}, u32[]{:S(2)}, u32[]{:S(2)}) collective-permute-start(f32[1096,128]{1,0:T(8,128)} %get-tuple-element.35), channel_id=1, source_target_pairs={{0,2},{1,3},{2,0},{3,1},{4,6},{5,7},{6,4},{7,5},{8,10},{9,11},{10,... | collective-permute-start | bytes 1683464 | tf_op jit(solution)/shard_map/ppermute | solution.py:548
  48.9 69.1 %collective-permute-start.6 = (f32[1096,128]{1,0:T(8,128)}, f32[1096,128]{1,0:T(8,128)S(1)}, u32[]{:S(2)}, u32[]{:S(2)}) collective-permute-start(f32[1096,128]{1,0:T(8,128)} %get-tuple-element.33), channel_id=1, source_target_pairs={{0,3},{1,2},{2,1},{3,0},{4,7},{5,6},{6,5},{7,4},{8,11},{9,10},{10,... | collective-permute-start | bytes 1683464 | tf_op jit(solution)/shard_map/ppermute | solution.py:548
  58.5 59.5 %collective-permute-start.7 = (f32[1096,128]{1,0:T(8,128)}, f32[1096,128]{1,0:T(8,128)S(1)}, u32[]{:S(2)}, u32[]{:S(2)}) collective-permute-start(f32[1096,128]{1,0:T(8,128)} %get-tuple-element.34), channel_id=1, source_target_pairs={{0,5},{1,4},{2,7},{3,6},{4,1},{5,0},{6,3},{7,2},{8,13},{9,12},{10,... | collective-permute-start | bytes 1683464 | tf_op jit(solution)/shard_map/ppermute | solution.py:548
  58.6 1.9 %copy-start.1 = (f32[48,128,128]{2,1,0:T(8,128)S(1)}, f32[48,128,128]{2,1,0:T(8,128)}, u32[]{:S(2)}) copy-start(f32[48,128,128]{2,1,0:T(8,128)} %param.10) | copy-start | bytes 9437188
  60.5 3.8 %copy-start.11 = (f32[1096,128]{1,0:T(8,128)S(1)}, f32[1096,128]{1,0:T(8,128)}, u32[]{:S(2)}) copy-start(f32[1096,128]{1,0:T(8,128)} %get-tuple-element.32) | copy-start | bytes 1683460
  60.5 6.7 %copy-start.8 = (f32[16,64,256]{2,1,0:T(8,128)S(1)}, f32[16,64,256]{2,1,0:T(8,128)}, u32[]{:S(2)}) copy-start(f32[16,64,256]{2,1,0:T(8,128)} %copy-done.7) | copy-start | bytes 3145732
  64.3 6.1 %copy-start.10 = (f32[1096,128]{1,0:T(8,128)S(1)}, f32[1096,128]{1,0:T(8,128)}, u32[]{:S(2)}) copy-start(f32[1096,128]{1,0:T(8,128)} %get-tuple-element.31) | copy-start | bytes 1683460
  64.3 58.9 %collective-permute-start.5 = (f32[1096,128]{1,0:T(8,128)S(1)}, f32[1096,128]{1,0:T(8,128)S(1)}, u32[]{:S(2)}, u32[]{:S(2)}) collective-permute-start(f32[1096,128]{1,0:T(8,128)S(1)} %copy-done.11), channel_id=1, source_target_pairs={{0,6},{1,7},{2,4},{3,5},{4,2},{5,3},{6,0},{7,1},{8,14},{9,15},{10,... | collective-permute-start | bytes 1683464 | tf_op jit(solution)/shard_map/ppermute | solution.py:548
  70.4 57.1 %collective-permute-start.4 = (f32[1096,128]{1,0:T(8,128)S(1)}, f32[1096,128]{1,0:T(8,128)S(1)}, u32[]{:S(2)}, u32[]{:S(2)}) collective-permute-start(f32[1096,128]{1,0:T(8,128)S(1)} %copy-done.10), channel_id=1, source_target_pairs={{0,7},{1,6},{2,5},{3,4},{4,3},{5,2},{6,1},{7,0},{8,15},{9,14},{10,... | collective-permute-start | bytes 1683464 | tf_op jit(solution)/shard_map/ppermute | solution.py:548
  130.6 13.1 %copy-start.2 = (f32[48,128,128]{2,1,0:T(8,128)S(1)}, f32[48,128,128]{2,1,0:T(8,128)}, u32[]{:S(2)}) copy-start(f32[48,128,128]{2,1,0:T(8,128)} %param.10) | copy-start | bytes 9437188
  132.8 10.8 %collective-permute-start.13 = (f32[128,128]{1,0:T(8,128)S(1)}, f32[128,128]{1,0:T(8,128)S(1)}, u32[]{:S(2)}, u32[]{:S(2)}) collective-permute-start(f32[128,128]{1,0:T(8,128)S(1)} %get-tuple-element.42), channel_id=1, source_target_pairs={{0,1},{1,2},{2,3},{3,4},{4,5},{5,6},{6,7},{7,0},{8,9},{9,10},{10,1... | collective-permute-start | bytes 196616 | tf_op jit(solution)/shard_map/ppermute | solution.py:477
  132.9 10.9 %collective-permute-start.14 = (f32[128,128]{1,0:T(8,128)S(1)}, f32[128,128]{1,0:T(8,128)S(1)}, u32[]{:S(2)}, u32[]{:S(2)}) collective-permute-start(f32[128,128]{1,0:T(8,128)S(1)} %get-tuple-element.43), channel_id=1, source_target_pairs={{1,0},{2,1},{3,2},{4,3},{5,4},{6,5},{7,6},{0,7},{9,8},{10,9},{11,1... | collective-permute-start | bytes 196616 | tf_op jit(solution)/shard_map/ppermute | solution.py:478
  136.4 3.0 %collective-permute-start.11 = (f32[32,128]{1,0:T(8,128)S(1)}, f32[32,128]{1,0:T(8,128)S(1)}, u32[]{:S(2)}, u32[]{:S(2)}) collective-permute-start(f32[32,128]{1,0:T(8,128)S(1)} %get-tuple-element.40), channel_id=1, source_target_pairs={{0,8},{8,16},{16,24},{1,9},{9,17},{17,25},{2,10},{10,18},{18,26},{... | collective-permute-start | bytes 49160 | tf_op jit(solution)/shard_map/ppermute | solution.py:475
  138.0 5.6 %collective-permute-start.12 = (f32[32,128]{1,0:T(8,128)S(1)}, f32[32,128]{1,0:T(8,128)S(1)}, u32[]{:S(2)}, u32[]{:S(2)}) collective-permute-start(f32[32,128]{1,0:T(8,128)S(1)} %get-tuple-element.41), channel_id=1, source_target_pairs={{8,0},{16,8},{24,16},{9,1},{17,9},{25,17},{10,2},{18,10},{26,18},{... | collective-permute-start | bytes 49160 | tf_op jit(solution)/shard_map/ppermute | solution.py:476
  149.1 17.5 %collective-permute-start.17 = (f32[128,128]{1,0:T(8,128)S(1)}, f32[128,128]{1,0:T(8,128)S(1)}, u32[]{:S(2)}, u32[]{:S(2)}) collective-permute-start(f32[128,128]{1,0:T(8,128)S(1)} %get-tuple-element.47), channel_id=1, source_target_pairs={{0,1},{1,2},{2,3},{3,4},{4,5},{5,6},{6,7},{7,0},{8,9},{9,10},{10,1... | collective-permute-start | bytes 196616 | tf_op jit(solution)/shard_map/ppermute | solution.py:477
  156.4 10.2 %collective-permute-start.18 = (f32[128,128]{1,0:T(8,128)S(1)}, f32[128,128]{1,0:T(8,128)S(1)}, u32[]{:S(2)}, u32[]{:S(2)}) collective-permute-start(f32[128,128]{1,0:T(8,128)S(1)} %get-tuple-element.48), channel_id=1, source_target_pairs={{1,0},{2,1},{3,2},{4,3},{5,4},{6,5},{7,6},{0,7},{9,8},{10,9},{11,1... | collective-permute-start | bytes 196616 | tf_op jit(solution)/shard_map/ppermute | solution.py:478
  156.4 6.0 %collective-permute-start.15 = (f32[32,128]{1,0:T(8,128)S(1)}, f32[32,128]{1,0:T(8,128)S(1)}, u32[]{:S(2)}, u32[]{:S(2)}) collective-permute-start(f32[32,128]{1,0:T(8,128)S(1)} %get-tuple-element.45), channel_id=1, source_target_pairs={{0,8},{8,16},{16,24},{1,9},{9,17},{17,25},{2,10},{10,18},{18,26},{... | collective-permute-start | bytes 49160 | tf_op jit(solution)/shard_map/ppermute | solution.py:475
  160.9 5.6 %collective-permute-start.16 = (f32[32,128]{1,0:T(8,128)S(1)}, f32[32,128]{1,0:T(8,128)S(1)}, u32[]{:S(2)}, u32[]{:S(2)}) collective-permute-start(f32[32,128]{1,0:T(8,128)S(1)} %get-tuple-element.46), channel_id=1, source_target_pairs={{8,0},{16,8},{24,16},{9,1},{17,9},{25,17},{10,2},{18,10},{26,18},{... | collective-permute-start | bytes 49160 | tf_op jit(solution)/shard_map/ppermute | solution.py:476
